TPU v7x, 256 devices: a whole 4x4x8 slice. The times are simulated.
256 devices in a mesh: member: 16 (over z_lo, x, core), grid: 16 (over y, z_hi).
Axes of the slice: x: 4, y: 4, z: 8 (z_hi: 4, z_lo: 2; z = z_hi * 2 + z_lo), core: 2. Of those that a mesh axis runs over, the one named last changes fastest.
Arguments:
- latent: float32 [16, 32768, 512], P('member', 'grid'), may hold values from -6 to 6
- dec_weight: float32 [512, 32], replicated, may hold values from -0.25 to 0.25
- dec_bias: float32 [32], replicated, may hold values from -3 to 3
- target: float32 [32, 32768], P(None, 'grid'), may hold values from -9 to 9
- area: float32 [32768], P('grid'), may hold values from 0.05 to 1.6, as said below
- var_weight: float32 [32], replicated, may hold values from 0.5 to 4
Outputs:
- loss: float32 [], replicated
- grad_latent: float32 [16, 32768, 512], P('member', 'grid')
- grad_weight: float32 [512, 32], replicated
- grad_bias: float32 [32], replicated
Inputs may be any that keep to these rules, and one draw needn't show every extreme that they name: Positive area weights of the window's nodes.
All inputs are finite; a program needn't handle non-finite values.
Results may differ from a plain program's by a relative error of at most 0.00017.
Values sent between devices are 32-bit elements; how exact they have to be, the bound alone decides.
No kernel may reach another device: no remote copies, remote signals or barrier semaphores. Data moves between devices by JAX's collectives and lax.ppermute only.
A program may use at most 64 MiB of HBM per device.

v0:
```python
import jax
import jax.numpy as jnp
from jax import lax
from jax.sharding import PartitionSpec as P

MEMBERS = 16


SMOOTHING = 0.1


def smooth_abs(spread):
    return jnp.sqrt(spread * spread + SMOOTHING * SMOOTHING)


def smooth_slope(spread):
    return spread / smooth_abs(spread)


def body(latent, dec_weight, dec_bias, target, area, var_weight):
    highest = lax.Precision.HIGHEST
    slab_nodes = area.shape[0]
    all_nodes = slab_nodes * lax.axis_size("grid")
    area_sum = lax.psum(jnp.sum(area), "grid")
    area_mean = area_sum / all_nodes
    node_scale = var_weight[:, None] * (area / area_mean)[None, :]
    fields = (
        jnp.einsum("mnk,kv->mvn", latent, dec_weight, precision=highest) + dec_bias[None, :, None]
    )
    own_count = fields.shape[0]
    norm_pairs = float(MEMBERS * (MEMBERS - 1))
    to_target = fields - target[None]
    target_term = jnp.sum(smooth_abs(to_target), 0) / MEMBERS
    target_slope = smooth_slope(to_target) / MEMBERS
    spread = fields[:, None] - lax.all_gather(fields, "member", axis=0, tiled=True)[None]
    pair_sum = jnp.sum(smooth_abs(spread), (0, 1))
    pair_slope = jnp.sum(smooth_slope(spread), 1)
    pair_sum = 0.5 * (pair_sum - own_count * SMOOTHING)
    crps_part = target_term - pair_sum / norm_pairs
    loss_part = jnp.sum(node_scale * crps_part)
    field_grad = node_scale[None] * (target_slope - pair_slope / norm_pairs)
    grad_latent = jnp.einsum("mvn,kv->mnk", field_grad, dec_weight, precision=highest)
    weight_part = jnp.einsum("mnk,mvn->kv", latent, field_grad, precision=highest)
    bias_part = jnp.sum(field_grad, (0, 2))
    weight_sum, bias_sum, loss_sum = lax.psum(
        (weight_part, bias_part, loss_part), ("member", "grid")
    )
    return (loss_sum / all_nodes, grad_latent, weight_sum / all_nodes, bias_sum / all_nodes)


def solution(mesh):
    placed = (P("member", "grid", None), P(), P(), P(None, "grid"), P("grid"), P())
    return jax.shard_map(
        body,
        mesh=mesh,
        in_specs=placed,
        out_specs=(P(), P("member", "grid", None), P(), P()),
        check_vma=False,
    )
```

profile of v0, /device:TPU:1, one launch (start us, length us, event | category | flops | bytes accessed | tf_op | source)
XLA Modules:
  0.0 392.5 jit_solution(4428409452434725733)
XLA Ops:
  7.2 0.0 copy-start
  7.2 0.0 copy-start.3
  7.2 0.0 copy-start.4
  7.2 0.0 copy-start.2
  7.2 0.0 all-gather.3.cloned.1.call-start
  7.3 0.8 copy-done
  8.0 6.7 %fusion.7 = f32[32,2048]{1,0:T(8,128)} fusion(f32[512,32]{0,1:T(8,128)S(1)} %copy-done, f32[1,2048,512]{2,1,0:T(8,128)} %param.6, f32[32]{0:T(128)} %param.8), kind=kOutput, calls=%fused_computation.9 | convolution fusion | flops 402718720 | bytes 4522112 | tf_op jit(solution)/shard_map/mnk,kv->mvn/dot_general | solution.py:28
  14.7 0.0 copy-start.1
  14.7 0.0 all-gather.3.cloned.1.call-update
  14.8 0.0 all-reduce.3.cloned.1.call-start
  14.8 0.0 copy-done.3
  14.8 0.6 reduce_sum.49
  15.4 42.4 %psum.28 = f32[]{:T(128)} all-reduce(f32[]{:T(128)} %reduce_sum.49), channel_id=1, replica_groups=mesh['member'=16,'grid'=16] {'grid'}, use_global_device_ids=true, to_apply=%region_1.0 | all-reduce | flops 1 | bytes 8 | tf_op jit(solution)/shard_map/psum | solution.py:24
  58.5 0.6 all-gather.3.cloned.1.call-done
  59.1 4.4 %fusion.6 = (f32[32,2048]{1,0:T(8,128)S(1)}, f32[32,2048]{1,0:T(8,128)S(1)}) fusion(f32[16,32,2048]{2,1,0:T(8,128)} %bitcast.18, f32[32,2048]{1,0:T(8,128)} %fusion.7), kind=kLoop, calls=%fused_computation.7 | loop fusion | flops 6160384 | bytes 4980736 | tf_op jit(solution)/shard_map/reduce_sum | solution.py:37
  63.5 0.0 copy-done.4
  63.6 0.0 copy-done.2
  63.6 0.0 copy-done.1
  63.6 0.9 fusion.14
  64.4 80.1 %all-reduce = (f32[]{:T(128)}, f32[32]{0:T(128)S(1)}) all-reduce(f32[]{:T(128)} %get-tuple-element.10, f32[32]{0:T(128)S(1)} %get-tuple-element.8), channel_id=1, replica_groups=mesh['member'=16,'grid'=16] {'member','grid'}, use_global_device_ids=true, to_apply=%region_4.0 | all-reduce | flops 33 | bytes 264 | tf_op jit(solution)/shard_map/psum | solution.py:45
  144.5 0.5 broadcast_multiply_fusion.1
  145.0 5.3 %fusion.10 = f32[512,32]{0,1:T(8,128)} fusion(f32[32,2048]{1,0:T(8,128)S(1)} %get-tuple-element.9, f32[1,2048,512]{2,1,0:T(8,128)} %param.6), kind=kOutput, calls=%fused_computation.10 | convolution fusion | flops 402653184 | bytes 4521984 | tf_op jit(solution)/shard_map/mnk,mvn->kv/dot_general | solution.py:43
  150.3 0.0 all-reduce.3.cloned.1.call-update
  150.3 5.0 %convolution_bitcast_fusion = f32[1,2048,512]{2,1,0:T(8,128)} fusion(f32[32,2048]{1,0:T(8,128)S(1)} %get-tuple-element.9, f32[512,32]{0,1:T(8,128)S(1)} %copy-done), kind=kOutput, calls=%fused_computation.8 | convolution fusion | flops 402653184 | bytes 4521984 | tf_op jit(solution)/shard_map/mvn,kv->mnk/dot_general | solution.py:42
  156.0 227.1 %all-reduce.3.cloned.1.call-done = f32[512,32]{0,1:T(8,128)} async-done(((f32[512,32]{0,1:T(8,128)}), f32[512,32]{0,1:T(8,128)}) %all-reduce.3.cloned.1.call-update) | async-done | bytes 65552 | tf_op jit(solution)/shard_map/psum | solution.py:45
  383.1 1.5 broadcast_multiply_fusion
  (1 shorter events, 0.0 us)
Async XLA Ops:
  7.2 0.8 copy-start
  7.2 7.6 %copy-start.3 = (f32[2048]{0:T(1024)S(1)}, f32[2048]{0:T(1024)}, u32[]{:S(2)}) copy-start(f32[2048]{0:T(1024)} %param.10) | copy-start | bytes 24580
  7.2 56.4 %copy-start.4 = (f32[32]{0:T(128)S(1)}, f32[32]{0:T(128)}, u32[]{:S(2)}) copy-start(f32[32]{0:T(128)} %param.11) | copy-start | bytes 388
  7.2 56.4 %copy-start.2 = (f32[32,2048]{1,0:T(8,128)S(1)}, f32[32,2048]{1,0:T(8,128)}, u32[]{:S(2)}) copy-start(f32[32,2048]{1,0:T(8,128)} %param.9) | copy-start | bytes 786436
  7.2 51.9 %all-gather.3.cloned.1.call-start = ((), (), s32[]{:S(2)}) async-start(), calls=%async_computation.1 | async-start | bytes 4456448 | tf_op jit(solution)/shard_map/all_gather | solution.py:35
  14.7 48.8 %copy-start.1 = (f32[32,2048]{1,0:T(8,128)S(1)}, f32[32,2048]{1,0:T(8,128)}, u32[]{:S(2)}) copy-start(f32[32,2048]{1,0:T(8,128)} %fusion.7) | copy-start | bytes 786436
  14.8 368.3 %all-reduce.3.cloned.1.call-start = ((), (), s32[]{:S(2)}) async-start(), calls=%async_computation | async-start | bytes 131072 | tf_op jit(solution)/shard_map/psum | solution.py:45
Sparse Core Ops, SparseCore 0:
  14.9 44.1 all-gather.2
  150.4 232.6 all-reduce.2
where the time goes:
time: 393 us
  waiting for transfers between devices  228 us (58%)
  blocking collectives  122 us (31%)
  matrix products  17.1 us (4%)
  between operations  16.5 us (4%)
  other arithmetic  7.9 us (2%)
    psum x1, waiting for transfers between devices, body(): lax.psum((weight_part, bias_part, loss_part), ('member', 'grid'))  227 us
    psum x1, blocking collectives, body(): lax.psum((weight_part, bias_part, loss_part), ('member', 'grid'))  80.1 us
    psum x1, blocking collectives, body(): area_sum = lax.psum(jnp.sum(area), 'grid')  42.4 us
  transfers between devices with their start and end apart: 2, of which 2 were waited for; matrix products, arithmetic and copies ran while one was open for 1% of the time, Pallas kernels for 0%

commit v1 on v0

v1 whole, which is shorter than its diff:
```python
import jax
import jax.numpy as jnp
from jax import lax
from jax.experimental import pallas as pl
from jax.experimental.pallas import tpu as pltpu
from jax.sharding import Mesh, PartitionSpec as P

MEMBERS = 16
LATENT = 512
VARS = 32
SMOOTHING = 0.1
LANES = 128
BLOCK = 512
CHUNKS = BLOCK // LANES
HALF = LATENT // 2
ROWS = VARS * HALF // LANES
EXTRA = 8
MEMBER = ("zl", "x", "c")
GRID = ("y", "zh")
F32 = jnp.float32
BF16 = jnp.bfloat16


def params(mib):
    return pltpu.CompilerParams(vmem_limit_bytes=mib * 1024 * 1024)


def split(a):
    hi = a.astype(BF16)
    return hi, (a - hi.astype(F32)).astype(BF16)


def dot(a, b, over):
    return lax.dot_general(a, b, (((over[0],), (over[1],)), ((), ())), preferred_element_type=F32)


def columns(row):
    return jnp.transpose(jnp.broadcast_to(row, (LANES, VARS)))


def decode_kernel(x_ref, w_ref, b_ref, out_ref):
    xh, xl = split(x_ref[...])
    wh, wl = split(w_ref[...])
    both = dot(jnp.concatenate([wh, wl], 0), xh, (1, 1))
    f = both[:VARS] + both[VARS:] + dot(wh, xl, (1, 1))
    bias = columns(b_ref[...])
    for i in range(CHUNKS):
        out_ref[i] = f[:, i * LANES : (i + 1) * LANES] + bias


def crps_kernel(at_ref, f_ref, t_ref, a_ref, v_ref, grad_ref, extra_ref):
    area = a_ref[pl.ds(at_ref[0], 1), :]
    scale = columns(v_ref[...]) * area
    sums = []
    loss = jnp.zeros((8, LANES), F32)
    for r in range(0, VARS, 8):
        rows = slice(r, r + 8)
        t = t_ref[rows, :]
        f = [f_ref[m, rows, :] for m in range(MEMBERS)]
        slope = [None] * MEMBERS
        near = jnp.zeros((8, LANES), F32)
        pairs = jnp.zeros((8, LANES), F32)
        total = [jnp.zeros((8, LANES), F32) for _ in range(MEMBERS)]
        for i in range(MEMBERS):
            d = f[i] - t
            q = d * d + SMOOTHING * SMOOTHING
            inv = lax.rsqrt(q)
            near = near + q * inv
            slope[i] = d * inv
            for j in range(i + 1, MEMBERS):
                d = f[i] - f[j]
                q = d * d + SMOOTHING * SMOOTHING
                inv = lax.rsqrt(q)
                pairs = pairs + q * inv
                s = d * inv
                total[i] = total[i] + s
                total[j] = total[j] - s
        norm = 1.0 / (MEMBERS * (MEMBERS - 1))
        here = scale[rows]
        loss = loss + here * (near * (1.0 / MEMBERS) - pairs * norm)
        fsum = jnp.zeros((8, LANES), F32)
        for m in range(MEMBERS):
            g = here * (slope[m] * (1.0 / MEMBERS) - total[m] * norm)
            grad_ref[m, rows, :] = g
            fsum = fsum + g
        sums.append(fsum)
    extra_ref[...] = jnp.zeros((EXTRA, LANES), F32)
    bias = jnp.sum(jnp.transpose(jnp.concatenate(sums, 0)), 0, keepdims=True)
    extra_ref[0:1, 0:VARS] = bias
    extra_ref[1:2, :] = jnp.sum(loss, 0, keepdims=True)
    extra_ref[2:3, :] = area


def weight_kernel(c_ref, g_ref, x_ref, e_ref, own_ref, other_ref, acc_ref):
    step = pl.program_id(0)
    g = jnp.concatenate([g_ref[i] for i in range(CHUNKS)], 1)
    gh, gl = split(g)
    xh, xl = split(x_ref[...])
    both = dot(jnp.concatenate([gh, gl], 0), xh, (1, 0))
    part = both[:VARS] + both[VARS:] + dot(gh, xl, (1, 0))

    @pl.when(step == 0)
    def _():
        acc_ref[...] = part

    @pl.when(step > 0)
    def _():
        acc_ref[...] += part

    @pl.when(step == pl.num_programs(0) - 1)
    def _():
        first = c_ref[0] == 0
        for i in range(HALF // LANES):
            rows = slice(i * VARS, (i + 1) * VARS)
            low = acc_ref[:, i * LANES : (i + 1) * LANES]
            high = acc_ref[:, HALF + i * LANES : HALF + (i + 1) * LANES]
            own_ref[rows, :] = jnp.where(first, low, high)
            other_ref[rows, :] = jnp.where(first, high, low)
        own_ref[ROWS:, :] = e_ref[...]
        other_ref[ROWS:, :] = e_ref[...]


def pair_kernel(a_ref, b_ref, out_ref):
    s = a_ref[...] + b_ref[...]
    for i in range(out_ref.shape[0]):
        out_ref[i] = s


def fold_kernel(in_ref, out_ref):
    s = in_ref[0]
    for i in range(1, in_ref.shape[0]):
        s = s + in_ref[i]
    for i in range(out_ref.shape[0]):
        out_ref[i] = s


def last_kernel(in_ref, w_ref, e_ref):
    s = in_ref[0]
    for i in range(1, in_ref.shape[0]):
        s = s + in_ref[i]
    e = s[ROWS:]
    area = jnp.sum(e[2:3], 1, keepdims=True)
    w_ref[...] = s[:ROWS] / area
    e_ref[0:1, :] = e[0:1] / area
    e_ref[1:2, :] = jnp.broadcast_to(jnp.sum(e[1:2], 1, keepdims=True) / area, (1, LANES))
    e_ref[2:3, :] = jnp.broadcast_to(1.0 / area, (1, LANES))
    e_ref[3:, :] = jnp.zeros((EXTRA - 3, LANES), F32)


def latent_kernel(nodes, g_ref, w_ref, e_ref, out_ref):
    inv = e_ref[2:3, :] * float(nodes)
    g = jnp.concatenate([g_ref[i] * inv for i in range(CHUNKS)], 1)
    gh, gl = split(g)
    wh, wl = split(w_ref[...])
    out_ref[...] = dot(jnp.concatenate([gh, gl, gh], 0), jnp.concatenate([wh, wh, wl], 0), (0, 0))


def whole(shape):
    return pl.BlockSpec(shape, lambda *_: (0,) * len(shape))


def shape(*s):
    return jax.ShapeDtypeStruct(s, F32)


def body(latent, dec_weight, dec_bias, target, area, var_weight):
    slab = area.shape[0]
    nodes = slab * lax.axis_size("y") * lax.axis_size("zh")
    steps = slab // BLOCK
    x = latent.reshape(slab, LATENT)
    wt = dec_weight.T
    me = lax.axis_index(MEMBER).astype(jnp.int32).reshape(1)
    core = lax.axis_index("c").astype(jnp.int32).reshape(1)

    fields = pl.pallas_call(
        decode_kernel,
        out_shape=shape(MEMBERS, VARS, LANES),
        grid=(steps,),
        in_specs=[
            pl.BlockSpec((BLOCK, LATENT), lambda i: (i, 0)),
            whole((VARS, LATENT)),
            whole((1, VARS)),
        ],
        out_specs=pl.BlockSpec((CHUNKS, VARS, LANES), lambda i: (i, 0, 0)),
        compiler_params=params(24),
    )(x, wt, dec_bias.reshape(1, VARS))

    fields = lax.all_to_all(fields, MEMBER, 0, 0)

    grads, extra = pl.pallas_call(
        crps_kernel,
        out_shape=(shape(MEMBERS, VARS, LANES), shape(EXTRA, LANES)),
        grid_spec=pltpu.PrefetchScalarGridSpec(
            num_scalar_prefetch=1,
            grid=(1,),
            in_specs=[
                whole((MEMBERS, VARS, LANES)),
                pl.BlockSpec((VARS, LANES), lambda i, at: (0, at[0])),
                whole((slab // LANES, LANES)),
                whole((1, VARS)),
            ],
            out_specs=(whole((MEMBERS, VARS, LANES)), whole((EXTRA, LANES))),
        ),
        compiler_params=params(16),
    )(me, fields, target, area.reshape(slab // LANES, LANES), var_weight.reshape(1, VARS))

    grads = lax.all_to_all(grads, MEMBER, 0, 0)

    own, other = pl.pallas_call(
        weight_kernel,
        out_shape=(shape(ROWS + EXTRA, LANES),) * 2,
        grid_spec=pltpu.PrefetchScalarGridSpec(
            num_scalar_prefetch=1,
            grid=(steps,),
            in_specs=[
                pl.BlockSpec((CHUNKS, VARS, LANES), lambda i, c: (i, 0, 0)),
                pl.BlockSpec((BLOCK, LATENT), lambda i, c: (i, 0)),
                whole((EXTRA, LANES)),
            ],
            out_specs=(whole((ROWS + EXTRA, LANES)),) * 2,
            scratch_shapes=[pltpu.VMEM((VARS, LATENT), F32)],
        ),
        compiler_params=params(24),
    )(core, grads, x, extra)

    swap = [(0, 1), (1, 0)]
    came = lax.ppermute(other, "c", swap)
    plane = lax.axis_size("x") * lax.axis_size("y")
    depth = lax.axis_size("zl") * lax.axis_size("zh")
    parts = pl.pallas_call(
        pair_kernel, out_shape=shape(plane, ROWS + EXTRA, LANES), compiler_params=params(16)
    )(own, came)
    parts = lax.all_to_all(parts, ("x", "y"), 0, 0)
    parts = pl.pallas_call(
        fold_kernel, out_shape=shape(depth, ROWS + EXTRA, LANES), compiler_params=params(16)
    )(parts)
    parts = lax.all_to_all(parts, ("zl", "zh"), 0, 0)
    mine, extra = pl.pallas_call(
        last_kernel, out_shape=(shape(ROWS, LANES), shape(EXTRA, LANES)), compiler_params=params(16)
    )(parts)
    theirs = lax.ppermute(mine, "c", swap)

    grad_latent = pl.pallas_call(
        lambda *refs: latent_kernel(nodes, *refs),
        out_shape=shape(slab, LATENT),
        grid=(steps,),
        in_specs=[
            pl.BlockSpec((CHUNKS, VARS, LANES), lambda i: (i, 0, 0)),
            whole((VARS, LATENT)),
            whole((EXTRA, LANES)),
        ],
        out_specs=pl.BlockSpec((BLOCK, LATENT), lambda i: (i, 0)),
        compiler_params=params(24),
        cost_estimate=pl.CostEstimate(flops=6 * slab * VARS * LATENT, bytes_accessed=4 * slab * LATENT, transcendentals=0),
    )(grads, wt, extra)

    first = core[0] == 0
    low = jnp.where(first, mine, theirs)
    high = jnp.where(first, theirs, mine)
    weight = jnp.concatenate([low[:VARS], low[VARS:], high[:VARS], high[VARS:]], 1).T
    return extra[1, 0], grad_latent[None], weight, extra[0, :VARS]


def solution(mesh):
    shaped = Mesh(mesh.devices.reshape(2, 4, 2, 4, 4), MEMBER + GRID)
    return jax.shard_map(
        body,
        mesh=shaped,
        in_specs=(P(MEMBER, GRID, None), P(), P(), P(None, GRID), P(GRID), P()),
        out_specs=(P(), P(MEMBER, GRID, None), P(), P()),
        check_vma=False,
    )
```

time: 393 us -> 79.4 us (0.20)
  waiting for transfers between devices: 228 us -> 15.9 us
  blocking collectives: 122 us -> 27 us
  starting transfers between devices: 0.08 us -> 19.3 us
  matrix products: 17.1 us -> 0 us
  between operations: 16.5 us -> 0.7 us
  Pallas kernels: 0 us -> 8.47 us
  other arithmetic: 7.9 us -> 0.64 us
  local copies, waits for them, and re-layouts: 0.78 us -> 6.92 us
    psum x1 -> x0, waiting for transfers between devices: 227 us -> none  [body(): lax.psum((weight_part, bias_part, loss_part), ('member', 'grid'))]
    psum x2 -> x0, blocking collectives: 122 us -> none  [the longest x1 80.1 us: body(): lax.psum((weight_part, bias_part, loss_part), ('member', 'grid'))]
    all_to_all x0 -> x2, blocking collectives: none -> 27 us  [the longest x1 16.3 us: body(): parts = lax.all_to_all(parts, ('x', 'y'), 0, 0)]
    dot_general x3 -> x0, matrix products: 17.1 us -> none  [the longest x1 6.73 us: body(): jnp.einsum('mnk,kv->mvn', latent, dec_weight, precision=highest)]
    all_to_all x0 -> x2, waiting for transfers between devices: none -> 15 us  [the longest x1 7.81 us: body(): parts = lax.all_to_all(parts, ('zl', 'zh'), 0, 0)]
    all_to_all x0 -> x2, starting transfers between devices: none -> 14.5 us  [the longest x1 7.28 us: body(): parts = lax.all_to_all(parts, ('zl', 'zh'), 0, 0)]
    pallas_call x0 -> x7, Pallas kernels: none -> 8.47 us  [the longest x1 2.93 us: body(): pl.pallas_call(lambda *refs: latent_kernel(nodes, *refs), out_shape=shape...]
    reduce_sum x3 -> x0, other arithmetic: 5.91 us -> none  [the longest x1 4.45 us: body(): pair_slope = jnp.sum(smooth_slope(spread), 1)]
  transfers between devices with their start and end apart: 2 -> 4, of which waited for: 2 -> 3; matrix products, arithmetic and copies ran while one was open for 1% -> 1% of each run, Pallas kernels for 0% -> 4%
where the time goes in v1:
time: 79.4 us; the launch traced here: 78.9 us
  blocking collectives  27 us (34%)
  starting transfers between devices  19.3 us (24%)
  waiting for transfers between devices  15.9 us (20%)
  Pallas kernels  8.47 us (11%)
  local copies, waits for them, and re-layouts  6.92 us (9%)
    all_to_all x1, blocking collectives, body(): parts = lax.all_to_all(parts, ('x', 'y'), 0, 0)  16.3 us
    all_to_all x1, blocking collectives, body(): grads = lax.all_to_all(grads, MEMBER, 0, 0)  10.8 us
    all_to_all x1, waiting for transfers between devices, body(): parts = lax.all_to_all(parts, ('zl', 'zh'), 0, 0)  7.81 us
    all_to_all x1, starting transfers between devices, body(): parts = lax.all_to_all(parts, ('zl', 'zh'), 0, 0)  7.28 us
    all_to_all x1, waiting for transfers between devices, body(): fields = lax.all_to_all(fields, MEMBER, 0, 0)  7.17 us
    all_to_all x1, starting transfers between devices, body(): fields = lax.all_to_all(fields, MEMBER, 0, 0)  7.17 us
    unnamed x16, local copies, waits for them, and re-layouts  5.89 us
    ppermute x1, starting transfers between devices, body(): theirs = lax.ppermute(mine, 'c', swap)  3.74 us
  transfers between devices with their start and end apart: 4, of which 3 were waited for; matrix products, arithmetic and copies ran while one was open for 1% of the time, Pallas kernels for 4%

profile of v1, /device:TPU:1, one launch (start us, length us, event | category | flops | bytes accessed | tf_op | source)
XLA Modules:
  0.0 78.9 jit_solution(14112016646363444058)
XLA Ops:
  0.6 0.0 copy-start.7
  0.6 0.0 copy-start
  0.7 2.2 %copy-done = f32[1,2048,512]{2,1,0:T(8,128)S(1)} copy-done((f32[1,2048,512]{2,1,0:T(8,128)S(1)}, f32[1,2048,512]{2,1,0:T(8,128)}, u32[]{:S(2)}) %copy-start) | copy-done | bytes 4194328
  2.8 0.0 copy-start.2
  2.8 0.8 %copy-done.2 = f32[512,32]{0,1:T(8,128)S(1)} copy-done((f32[512,32]{0,1:T(8,128)S(1)}, f32[512,32]{0,1:T(8,128)}, u32[]{:S(2)}) %copy-start.2) | copy-done | bytes 65560
  3.7 0.0 copy-start.6
  3.7 0.7 copy-done.6
  4.3 2.6 %shard_map.93 = f32[16,32,128]{2,1,0:T(8,128)} custom-call(f32[2048,512]{1,0:T(8,128)S(1)} %bitcast.13, f32[32,512]{1,0:T(8,128)S(1)} %bitcast.15, f32[1,32]{1,0:T(1,128)S(1)} %bitcast.18), custom_call_target="tpu_custom_call" | custom-call | tf_op jit(solution)/shard_map/pallas_call | solution.py:175
  6.9 7.2 %all-to-all-start = ((f32[16,32,128]{2,1,0:T(8,128)}), f32[16,32,128]{2,1,0:T(8,128)S(1)}, u32[]{:S(2)}, u32[]{:S(2)}) async-start(f32[16,32,128]{2,1,0:T(8,128)} %shard_map.93), calls=%async_computation | async-start | bytes 524288 | tf_op jit(solution)/shard_map/all_to_all | solution.py:188
  14.1 7.2 %all-to-all-done.f_ref = f32[16,32,128]{2,1,0:T(8,128)S(1)} async-done(((f32[16,32,128]{2,1,0:T(8,128)}), f32[16,32,128]{2,1,0:T(8,128)S(1)}, u32[]{:S(2)}, u32[]{:S(2)}) %all-to-all-start) | async-done | bytes 262176 | tf_op jit(solution)/shard_map/all_to_all | solution.py:188
  21.2 0.0 copy-done.7
  21.2 0.0 copy-done.4
  21.2 0.0 copy-done.5
  21.2 0.8 %shard_map.94 = (f32[16,32,128]{2,1,0:T(8,128)S(1)}, f32[8,128]{1,0:T(8,128)S(1)}) custom-call(s32[1]{0:T(128)} %bitcast.1.at_ref, f32[16,32,128]{2,1,0:T(8,128)S(1)} %all-to-all-done.f_ref, f32[32,2048]{1,0:T(8,128)S(1)} %copy-done.4, f32[16,128]{1,0:T(8,128)S(1)} %bitcast.17, f32[1,32]{1,0:T(1,128)S(1)} %bitcast.19), custom_call_target="tpu_custom_call" | custom-call | tf_op jit(solution)/shard_map/pallas_call | solution.py:190
  22.1 0.0 copy-start.3
  22.1 10.8 %all_to_all.20.g_ref.refs_0_ = f32[16,32,128]{2,1,0:T(8,128)S(1)} all-to-all(f32[16,32,128]{2,1,0:T(8,128)S(1)} %get-tuple-element.10), channel_id=1, replica_groups=mesh['zl'=2,'x'=4,'c'=2,'y'=4,'zh'=4] {'zl','x','c'}, dimensions={0} | all-to-all | bytes 524288 | tf_op jit(solution)/shard_map/all_to_all | solution.py:207
  32.8 2.2 %copy-done.1 = f32[1,2048,512]{2,1,0:T(8,128)S(1)} copy-done((f32[1,2048,512]{2,1,0:T(8,128)S(1)}, f32[1,2048,512]{2,1,0:T(8,128)}, u32[]{:S(2)}) %copy-start.1) | copy-done | bytes 4194328
  35.0 1.2 %shard_map.95 = (f32[72,128]{1,0:T(8,128)S(1)}, f32[72,128]{1,0:T(8,128)S(1)}) custom-call(s32[1]{0:T(128)} %bitcast.c_ref, f32[16,32,128]{2,1,0:T(8,128)S(1)} %all_to_all.20.g_ref.refs_0_, f32[2048,512]{1,0:T(8,128)S(1)} %bitcast.14, f32[8,128]{1,0:T(8,128)S(1)} %get-tuple-element.11.e_ref), custom_call_target="tpu_custom_call" | custom-call | tf_op jit(solution)/shard_map/pallas_call | solution.py:209
  36.3 1.1 %collective-permute-start = (f32[72,128]{1,0:T(8,128)S(1)}, f32[72,128]{1,0:T(8,128)S(1)}, u32[]{:S(2)}, u32[]{:S(2)}) collective-permute-start(f32[72,128]{1,0:T(8,128)S(1)} %get-tuple-element.13), channel_id=1, source_target_pairs={{0,16},{16,0},{1,17},{17,1},{2,18},{18,2},{3,19},{19,3},{4,20},{20... | collective-permute-start | bytes 110600 | tf_op jit(solution)/shard_map/ppermute | solution.py:227
  37.3 0.9 %collective-permute-done.b_ref = f32[72,128]{1,0:T(8,128)S(1)} collective-permute-done((f32[72,128]{1,0:T(8,128)S(1)}, f32[72,128]{1,0:T(8,128)S(1)}, u32[]{:S(2)}, u32[]{:S(2)}) %collective-permute-start) | collective-permute-done | bytes 36896 | tf_op jit(solution)/shard_map/ppermute | solution.py:227
  38.2 16.3 %all_to_all.21.in_ref = f32[16,72,128]{2,1,0:T(8,128)S(1)} all-to-all(f32[16,72,128]{2,1,0:T(8,128)S(1)} %shard_map.96), channel_id=1, replica_groups=mesh['zl'=2,'x'=4,'c'=2,'y'=4,'zh'=4] {'x','y'}, dimensions={0} | all-to-all | bytes 1179648 | tf_op jit(solution)/shard_map/all_to_all | solution.py:233
  54.5 0.8 shard_map.97
  55.3 7.3 %all-to-all-start.3 = ((f32[8,72,128]{2,1,0:T(8,128)}), f32[8,72,128]{2,1,0:T(8,128)S(1)}, u32[]{:S(2)}, u32[]{:S(2)}) async-start(f32[8,72,128]{2,1,0:T(8,128)} %shard_map.97), calls=%async_computation.3 | async-start | bytes 589824 | tf_op jit(solution)/shard_map/all_to_all | solution.py:237
  62.5 7.8 %all-to-all-done.3.in_ref = f32[8,72,128]{2,1,0:T(8,128)S(1)} async-done(((f32[8,72,128]{2,1,0:T(8,128)}), f32[8,72,128]{2,1,0:T(8,128)S(1)}, u32[]{:S(2)}, u32[]{:S(2)}) %all-to-all-start.3) | async-done | bytes 294944 | tf_op jit(solution)/shard_map/all_to_all | solution.py:237
  70.4 0.2 shard_map.98
  70.5 3.7 %collective-permute-start.1 = (f32[64,128]{1,0:T(8,128)S(1)}, f32[64,128]{1,0:T(8,128)S(1)}, u32[]{:S(2)}, u32[]{:S(2)}) collective-permute-start(f32[64,128]{1,0:T(8,128)S(1)} %get-tuple-element.15), channel_id=1, source_target_pairs={{0,16},{16,0},{1,17},{17,1},{2,18},{18,2},{3,19},{19,3},{4,20},{20... | collective-permute-start | bytes 98312 | tf_op jit(solution)/shard_map/ppermute | solution.py:241
  74.3 0.5 slice_bitcast_fusion
  74.8 0.5 slice.18
  75.3 0.0 copy-done.3
  75.3 2.9 %shard_map.99 = f32[2048,512]{1,0:T(8,128)} custom-call(f32[16,32,128]{2,1,0:T(8,128)S(1)} %all_to_all.20.g_ref.refs_0_, f32[32,512]{1,0:T(8,128)S(1)} %bitcast.16, f32[8,128]{1,0:T(8,128)S(1)} %get-tuple-element.14.refs_2_), custom_call_target="tpu_custom_call" | custom-call | flops 201326592 | bytes 4194304 | tf_op jit(solution)/shard_map/pallas_call | solution.py:243
  78.2 0.0 collective-permute-done.1
  78.2 0.6 maximum_bitcast_fusion
  (6 shorter events, 0.1 us)
Async XLA Ops:
  0.6 20.6 %copy-start.7 = (f32[32]{0:T(128)S(1)}, f32[32]{0:T(128)}, u32[]{:S(2)}) copy-start(f32[32]{0:T(128)} %param.11) | copy-start | bytes 388
  0.6 2.2 %copy-start = (f32[1,2048,512]{2,1,0:T(8,128)S(1)}, f32[1,2048,512]{2,1,0:T(8,128)}, u32[]{:S(2)}) copy-start(f32[1,2048,512]{2,1,0:T(8,128)} %param.6) | copy-start | bytes 12582916
  2.8 0.8 %copy-start.2 = (f32[512,32]{0,1:T(8,128)S(1)}, f32[512,32]{0,1:T(8,128)}, u32[]{:S(2)}) copy-start(f32[512,32]{0,1:T(8,128)} %param.7) | copy-start | bytes 196612
  3.7 0.7 copy-start.6
  4.3 16.9 %copy-start.4 = (f32[32,2048]{1,0:T(8,128)S(1)}, f32[32,2048]{1,0:T(8,128)}, u32[]{:S(2)}) copy-start(f32[32,2048]{1,0:T(8,128)} %t_ref.1) | copy-start | bytes 786436
  4.3 16.9 %copy-start.5 = (f32[2048]{0:T(1024)S(1)}, f32[2048]{0:T(1024)}, u32[]{:S(2)}) copy-start(f32[2048]{0:T(1024)} %param.10) | copy-start | bytes 24580
  6.9 14.3 %all-to-all-start = ((f32[16,32,128]{2,1,0:T(8,128)}), f32[16,32,128]{2,1,0:T(8,128)S(1)}, u32[]{:S(2)}, u32[]{:S(2)}) async-start(f32[16,32,128]{2,1,0:T(8,128)} %shard_map.93), calls=%async_computation | async-start | bytes 524288 | tf_op jit(solution)/shard_map/all_to_all | solution.py:188
  22.1 53.2 %copy-start.3 = (f32[512,32]{0,1:T(8,128)S(1)}, f32[512,32]{0,1:T(8,128)}, u32[]{:S(2)}) copy-start(f32[512,32]{0,1:T(8,128)} %param.7) | copy-start | bytes 196612
  32.8 2.2 %copy-start.1 = (f32[1,2048,512]{2,1,0:T(8,128)S(1)}, f32[1,2048,512]{2,1,0:T(8,128)}, u32[]{:S(2)}) copy-start(f32[1,2048,512]{2,1,0:T(8,128)} %param.6) | copy-start | bytes 12582916
  36.3 1.9 %collective-permute-start = (f32[72,128]{1,0:T(8,128)S(1)}, f32[72,128]{1,0:T(8,128)S(1)}, u32[]{:S(2)}, u32[]{:S(2)}) collective-permute-start(f32[72,128]{1,0:T(8,128)S(1)} %get-tuple-element.13), channel_id=1, source_target_pairs={{0,16},{16,0},{1,17},{17,1},{2,18},{18,2},{3,19},{19,3},{4,20},{20... | collective-permute-start | bytes 110600 | tf_op jit(solution)/shard_map/ppermute | solution.py:227
  55.3 15.1 %all-to-all-start.3 = ((f32[8,72,128]{2,1,0:T(8,128)}), f32[8,72,128]{2,1,0:T(8,128)S(1)}, u32[]{:S(2)}, u32[]{:S(2)}) async-start(f32[8,72,128]{2,1,0:T(8,128)} %shard_map.97), calls=%async_computation.3 | async-start | bytes 589824 | tf_op jit(solution)/shard_map/all_to_all | solution.py:237
  70.5 7.7 %collective-permute-start.1 = (f32[64,128]{1,0:T(8,128)S(1)}, f32[64,128]{1,0:T(8,128)S(1)}, u32[]{:S(2)}, u32[]{:S(2)}) collective-permute-start(f32[64,128]{1,0:T(8,128)S(1)} %get-tuple-element.15), channel_id=1, source_target_pairs={{0,16},{16,0},{1,17},{17,1},{2,18},{18,2},{3,19},{19,3},{4,20},{20... | collective-permute-start | bytes 98312 | tf_op jit(solution)/shard_map/ppermute | solution.py:241

commit v2 on v1

--- a/solution.py
+++ b/solution.py
@@ -19,6 +19,13 @@
 GRID = ("y", "zh")
 F32 = jnp.float32
 BF16 = jnp.bfloat16
+VMEM = pl.BlockSpec(memory_space=pltpu.VMEM)
+SMEM = pl.BlockSpec(memory_space=pltpu.SMEM)
+HBM = pl.BlockSpec(memory_space=pltpu.HBM)
+
+
+def in_hbm(a):
+    return pltpu.with_memory_space_constraint(a, pltpu.HBM)
 
 
 def params(mib):
@@ -38,14 +45,31 @@
     return jnp.transpose(jnp.broadcast_to(row, (LANES, VARS)))
 
 
-def decode_kernel(x_ref, w_ref, b_ref, out_ref):
-    xh, xl = split(x_ref[...])
+def decode_kernel(me_ref, core_ref, x_hbm, w_hbm, b_hbm, out_ref, x_ref, w_ref, b_ref, sems, more):
+    first = [
+        pltpu.make_async_copy(w_hbm, w_ref, more.at[0]),
+        pltpu.make_async_copy(b_hbm, b_ref, more.at[1]),
+    ]
+    for copy in first:
+        copy.start()
+    copies = []
+    for i in range(x_ref.shape[0] // BLOCK):
+        rows = pl.ds(i * BLOCK, BLOCK)
+        copies.append(pltpu.make_async_copy(x_hbm.at[rows], x_ref.at[rows], sems.at[i]))
+        copies[-1].start()
+    for copy in first:
+        copy.wait()
     wh, wl = split(w_ref[...])
-    both = dot(jnp.concatenate([wh, wl], 0), xh, (1, 1))
-    f = both[:VARS] + both[VARS:] + dot(wh, xl, (1, 1))
+    both = jnp.concatenate([wh, wl], 0)
     bias = columns(b_ref[...])
-    for i in range(CHUNKS):
-        out_ref[i] = f[:, i * LANES : (i + 1) * LANES] + bias
+    for i, copy in enumerate(copies):
+        copy.wait()
+        rows = slice(i * BLOCK, (i + 1) * BLOCK)
+        xh, xl = split(x_ref[rows, :])
+        f = dot(both, xh, (1, 1))
+        f = f[:VARS] + f[VARS:] + dot(wh, xl, (1, 1))
+        for j in range(CHUNKS):
+            out_ref[i * CHUNKS + j] = f[:, j * LANES : (j + 1) * LANES] + bias
 
 
 def crps_kernel(at_ref, f_ref, t_ref, a_ref, v_ref, grad_ref, extra_ref):
@@ -91,33 +115,24 @@
     extra_ref[2:3, :] = area
 
 
-def weight_kernel(c_ref, g_ref, x_ref, e_ref, own_ref, other_ref, acc_ref):
-    step = pl.program_id(0)
-    g = jnp.concatenate([g_ref[i] for i in range(CHUNKS)], 1)
-    gh, gl = split(g)
-    xh, xl = split(x_ref[...])
-    both = dot(jnp.concatenate([gh, gl], 0), xh, (1, 0))
-    part = both[:VARS] + both[VARS:] + dot(gh, xl, (1, 0))
-
-    @pl.when(step == 0)
-    def _():
-        acc_ref[...] = part
-
-    @pl.when(step > 0)
-    def _():
-        acc_ref[...] += part
-
-    @pl.when(step == pl.num_programs(0) - 1)
-    def _():
-        first = c_ref[0] == 0
-        for i in range(HALF // LANES):
-            rows = slice(i * VARS, (i + 1) * VARS)
-            low = acc_ref[:, i * LANES : (i + 1) * LANES]
-            high = acc_ref[:, HALF + i * LANES : HALF + (i + 1) * LANES]
-            own_ref[rows, :] = jnp.where(first, low, high)
-            other_ref[rows, :] = jnp.where(first, high, low)
-        own_ref[ROWS:, :] = e_ref[...]
-        other_ref[ROWS:, :] = e_ref[...]
+def weight_kernel(c_ref, g_ref, x_ref, e_ref, own_ref, other_ref):
+    acc = jnp.zeros((VARS, LATENT), F32)
+    for i in range(x_ref.shape[0] // BLOCK):
+        rows = slice(i * BLOCK, (i + 1) * BLOCK)
+        g = jnp.concatenate([g_ref[i * CHUNKS + j] for j in range(CHUNKS)], 1)
+        gh, gl = split(g)
+        xh, xl = split(x_ref[rows, :])
+        both = dot(jnp.concatenate([gh, gl], 0), xh, (1, 0))
+        acc = acc + (both[:VARS] + both[VARS:] + dot(gh, xl, (1, 0)))
+    first = c_ref[0] == 0
+    for i in range(HALF // LANES):
+        rows = slice(i * VARS, (i + 1) * VARS)
+        low = acc[:, i * LANES : (i + 1) * LANES]
+        high = acc[:, HALF + i * LANES : HALF + (i + 1) * LANES]
+        own_ref[rows, :] = jnp.where(first, low, high)
+        other_ref[rows, :] = jnp.where(first, high, low)
+    own_ref[ROWS:, :] = e_ref[...]
+    other_ref[ROWS:, :] = e_ref[...]
 
 
 def pair_kernel(a_ref, b_ref, out_ref):
@@ -134,25 +149,41 @@
         out_ref[i] = s
 
 
-def last_kernel(in_ref, w_ref, e_ref):
+def last_kernel(in_ref, w_ref, loss_ref, bias_ref, inv_ref):
     s = in_ref[0]
     for i in range(1, in_ref.shape[0]):
         s = s + in_ref[i]
     e = s[ROWS:]
     area = jnp.sum(e[2:3], 1, keepdims=True)
     w_ref[...] = s[:ROWS] / area
-    e_ref[0:1, :] = e[0:1] / area
-    e_ref[1:2, :] = jnp.broadcast_to(jnp.sum(e[1:2], 1, keepdims=True) / area, (1, LANES))
-    e_ref[2:3, :] = jnp.broadcast_to(1.0 / area, (1, LANES))
-    e_ref[3:, :] = jnp.zeros((EXTRA - 3, LANES), F32)
-
-
-def latent_kernel(nodes, g_ref, w_ref, e_ref, out_ref):
-    inv = e_ref[2:3, :] * float(nodes)
-    g = jnp.concatenate([g_ref[i] * inv for i in range(CHUNKS)], 1)
-    gh, gl = split(g)
+    loss_ref[...] = jnp.sum(e[1:2], 1, keepdims=True) / area
+    bias_ref[...] = (e[0:1] / area)[:, :VARS]
+    inv_ref[...] = jnp.broadcast_to(1.0 / area, (1, LANES))
+
+
+def latent_kernel(nodes, g_ref, w_ref, inv_ref, out_hbm, out_ref, sems):
+    inv = inv_ref[...] * float(nodes)
     wh, wl = split(w_ref[...])
-    out_ref[...] = dot(jnp.concatenate([gh, gl, gh], 0), jnp.concatenate([wh, wh, wl], 0), (0, 0))
+    w = jnp.concatenate([wh, wh, wl], 0)
+    copies = []
+    for i in range(out_ref.shape[0] // BLOCK):
+        rows = pl.ds(i * BLOCK, BLOCK)
+        g = jnp.concatenate([g_ref[i * CHUNKS + j] * inv for j in range(CHUNKS)], 1)
+        gh, gl = split(g)
+        out_ref[rows, :] = dot(jnp.concatenate([gh, gl, gh], 0), w, (0, 0))
+        copies.append(pltpu.make_async_copy(out_ref.at[rows], out_hbm.at[rows], sems.at[i]))
+        copies[-1].start()
+    for copy in copies:
+        copy.wait()
+
+
+def join_kernel(c_ref, mine_ref, theirs_ref, out_ref):
+    first = c_ref[0] == 0
+    for i in range(HALF // LANES):
+        rows = slice(i * VARS, (i + 1) * VARS)
+        mine, theirs = mine_ref[rows, :], theirs_ref[rows, :]
+        out_ref[:, i * LANES : (i + 1) * LANES] = jnp.where(first, mine, theirs)
+        out_ref[:, HALF + i * LANES : HALF + (i + 1) * LANES] = jnp.where(first, theirs, mine)
 
 
 def whole(shape):
@@ -172,18 +203,19 @@
     me = lax.axis_index(MEMBER).astype(jnp.int32).reshape(1)
     core = lax.axis_index("c").astype(jnp.int32).reshape(1)
 
-    fields = pl.pallas_call(
+    fields, kept = pl.pallas_call(
         decode_kernel,
-        out_shape=shape(MEMBERS, VARS, LANES),
-        grid=(steps,),
-        in_specs=[
-            pl.BlockSpec((BLOCK, LATENT), lambda i: (i, 0)),
-            whole((VARS, LATENT)),
-            whole((1, VARS)),
+        out_shape=(shape(MEMBERS, VARS, LANES), shape(slab, LATENT)),
+        in_specs=[SMEM, SMEM, HBM, HBM, HBM],
+        out_specs=(VMEM, VMEM),
+        scratch_shapes=[
+            pltpu.VMEM((VARS, LATENT), F32),
+            pltpu.VMEM((1, VARS), F32),
+            pltpu.SemaphoreType.DMA((steps,)),
+            pltpu.SemaphoreType.DMA((2,)),
         ],
-        out_specs=pl.BlockSpec((CHUNKS, VARS, LANES), lambda i: (i, 0, 0)),
         compiler_params=params(24),
-    )(x, wt, dec_bias.reshape(1, VARS))
+    )(me, core, in_hbm(x), in_hbm(wt), in_hbm(dec_bias.reshape(1, VARS)))
 
     fields = lax.all_to_all(fields, MEMBER, 0, 0)
 
@@ -209,19 +241,10 @@
     own, other = pl.pallas_call(
         weight_kernel,
         out_shape=(shape(ROWS + EXTRA, LANES),) * 2,
-        grid_spec=pltpu.PrefetchScalarGridSpec(
-            num_scalar_prefetch=1,
-            grid=(steps,),
-            in_specs=[
-                pl.BlockSpec((CHUNKS, VARS, LANES), lambda i, c: (i, 0, 0)),
-                pl.BlockSpec((BLOCK, LATENT), lambda i, c: (i, 0)),
-                whole((EXTRA, LANES)),
-            ],
-            out_specs=(whole((ROWS + EXTRA, LANES)),) * 2,
-            scratch_shapes=[pltpu.VMEM((VARS, LATENT), F32)],
-        ),
+        in_specs=[SMEM, VMEM, VMEM, VMEM],
+        out_specs=(VMEM, VMEM),
         compiler_params=params(24),
-    )(core, grads, x, extra)
+    )(core, grads, kept, extra)
 
     swap = [(0, 1), (1, 0)]
     came = lax.ppermute(other, "c", swap)
@@ -235,30 +258,31 @@
         fold_kernel, out_shape=shape(depth, ROWS + EXTRA, LANES), compiler_params=params(16)
     )(parts)
     parts = lax.all_to_all(parts, ("zl", "zh"), 0, 0)
-    mine, extra = pl.pallas_call(
-        last_kernel, out_shape=(shape(ROWS, LANES), shape(EXTRA, LANES)), compiler_params=params(16)
+    mine, loss, bias, inv = pl.pallas_call(
+        last_kernel,
+        out_shape=(shape(ROWS, LANES), shape(1, 1), shape(1, VARS), shape(1, LANES)),
+        compiler_params=params(16),
     )(parts)
     theirs = lax.ppermute(mine, "c", swap)
 
     grad_latent = pl.pallas_call(
         lambda *refs: latent_kernel(nodes, *refs),
         out_shape=shape(slab, LATENT),
-        grid=(steps,),
-        in_specs=[
-            pl.BlockSpec((CHUNKS, VARS, LANES), lambda i: (i, 0, 0)),
-            whole((VARS, LATENT)),
-            whole((EXTRA, LANES)),
-        ],
-        out_specs=pl.BlockSpec((BLOCK, LATENT), lambda i: (i, 0)),
+        in_specs=[VMEM, VMEM, VMEM],
+        out_specs=HBM,
+        scratch_shapes=[pltpu.VMEM((slab, LATENT), F32), pltpu.SemaphoreType.DMA((steps,))],
         compiler_params=params(24),
         cost_estimate=pl.CostEstimate(flops=6 * slab * VARS * LATENT, bytes_accessed=4 * slab * LATENT, transcendentals=0),
-    )(grads, wt, extra)
-
-    first = core[0] == 0
-    low = jnp.where(first, mine, theirs)
-    high = jnp.where(first, theirs, mine)
-    weight = jnp.concatenate([low[:VARS], low[VARS:], high[:VARS], high[VARS:]], 1).T
-    return extra[1, 0], grad_latent[None], weight, extra[0, :VARS]
+    )(grads, wt, inv)
+
+    weight = pl.pallas_call(
+        join_kernel,
+        out_shape=shape(VARS, LATENT),
+        in_specs=[SMEM, VMEM, VMEM],
+        out_specs=VMEM,
+        compiler_params=params(16),
+    )(core, mine, theirs)
+    return loss.reshape(()), grad_latent[None], weight.T, bias.reshape(VARS)
 
 
 def solution(mesh):

time: 79.4 us -> 73.4 us (0.924)
  blocking collectives: 27 us -> 58.3 us
  waiting for transfers between devices: 15.9 us -> 0.87 us
  starting transfers between devices: 19.3 us -> 4.36 us
  local copies, waits for them, and re-layouts: 6.92 us -> 0.02 us
    all_to_all x0 -> x2, blocking collectives: none -> 31.3 us  [the longest x1 17.1 us: body(): parts = lax.all_to_all(parts, ('zl', 'zh'), 0, 0)]
    all_to_all x2 -> x0, waiting for transfers between devices: 15 us -> none  [the longest x1 7.81 us: body(): parts = lax.all_to_all(parts, ('zl', 'zh'), 0, 0)]
    all_to_all x2 -> x0, starting transfers between devices: 14.5 us -> none  [the longest x1 7.28 us: body(): parts = lax.all_to_all(parts, ('zl', 'zh'), 0, 0)]
    unnamed x16 -> x8, local copies, waits for them, and re-layouts: 5.89 us -> 0.02 us
    pallas_call x2 -> x3, Pallas kernels: 2.71 us -> 4.76 us  [the longest x1 3.51 us: body(): pl.pallas_call(decode_kernel, out_shape=(shape(MEMBERS, VARS, LANES), sha...]
  transfers between devices with their start and end apart: 4 -> 2, of which waited for: 3 -> 1; matrix products, arithmetic and copies ran while one was open for 1% -> 0% of each run, Pallas kernels for 4% -> 3%
where the time goes in v2:
time: 73.4 us; the launch traced here: 73.1 us
  blocking collectives  58.3 us (79%)
  Pallas kernels  8.88 us (12%)
  starting transfers between devices  4.36 us (6%)
  waiting for transfers between devices  0.87 us (1%)
    all_to_all x1, blocking collectives, body(): parts = lax.all_to_all(parts, ('zl', 'zh'), 0, 0)  17.1 us
    all_to_all x1, blocking collectives, body(): parts = lax.all_to_all(parts, ('x', 'y'), 0, 0)  16.3 us
    all_to_all x1, blocking collectives, body(): fields = lax.all_to_all(fields, MEMBER, 0, 0)  14.1 us
    all_to_all x1, blocking collectives, body(): grads = lax.all_to_all(grads, MEMBER, 0, 0)  10.8 us
    pallas_call x1, Pallas kernels, body(): pl.pallas_call(decode_kernel, out_shape=(shape(MEMBERS, VARS, LANES), sha...  3.51 us
    ppermute x1, starting transfers between devices, body(): theirs = lax.ppermute(mine, 'c', swap)  3.36 us
    pallas_call x1, Pallas kernels, body(): pl.pallas_call(lambda *refs: latent_kernel(nodes, *refs), out_shape=shape...  2.36 us
  transfers between devices with their start and end apart: 2, of which 1 were waited for; matrix products, arithmetic and copies ran while one was open for 0% of the time, Pallas kernels for 3%

profile of v2, /device:TPU:1, one launch (start us, length us, event | category | flops | bytes accessed | tf_op | source)
XLA Modules:
  0.0 73.1 jit_solution(13906350250616567026)
XLA Ops:
  0.6 0.0 copy-start.3
  0.6 0.0 copy-start.2
  0.7 0.0 copy-start.1
  0.7 3.5 %shard_map.93 = (f32[16,32,128]{2,1,0:T(8,128)S(1)}, f32[2048,512]{1,0:T(8,128)S(1)}) custom-call(s32[1]{0:T(128)} %bitcast.1.me_ref.at_ref, s32[1]{0:T(128)} %bitcast.core_ref.c_ref, f32[2048,512]{1,0:T(8,128)} %bitcast.15, f32[32,512]{1,0:T(8,128)} %bitcast.11, f32[1,32]{1,0:T(1,128)} %bitcast.18), custom_call_target="tpu_custom_call" | custom-call | tf_op jit(solution)/shard_map/pallas_call | solution.py:206
  4.2 14.1 %all_to_all.20.f_ref = f32[16,32,128]{2,1,0:T(8,128)S(1)} all-to-all(f32[16,32,128]{2,1,0:T(8,128)S(1)} %get-tuple-element.14), channel_id=1, replica_groups=mesh['zl'=2,'x'=4,'c'=2,'y'=4,'zh'=4] {'zl','x','c'}, dimensions={0} | all-to-all | bytes 524288 | tf_op jit(solution)/shard_map/all_to_all | solution.py:220
  18.3 0.0 copy-done.3
  18.3 0.0 copy-done.2
  18.3 0.0 copy-done.1
  18.3 0.8 %shard_map.94 = (f32[16,32,128]{2,1,0:T(8,128)S(1)}, f32[8,128]{1,0:T(8,128)S(1)}) custom-call(s32[1]{0:T(128)} %bitcast.1.me_ref.at_ref, f32[16,32,128]{2,1,0:T(8,128)S(1)} %all_to_all.20.f_ref, f32[32,2048]{1,0:T(8,128)S(1)} %copy-done.1, f32[16,128]{1,0:T(8,128)S(1)} %bitcast.13, f32[1,32]{1,0:T(1,128)S(1)} %bitcast.14), custom_call_target="tpu_custom_call" | custom-call | tf_op jit(solution)/shard_map/pallas_call | solution.py:222
  19.1 0.0 copy-start
  19.2 10.8 %all_to_all.21.g_ref.refs_0_ = f32[16,32,128]{2,1,0:T(8,128)S(1)} all-to-all(f32[16,32,128]{2,1,0:T(8,128)S(1)} %get-tuple-element.15), channel_id=1, replica_groups=mesh['zl'=2,'x'=4,'c'=2,'y'=4,'zh'=4] {'zl','x','c'}, dimensions={0} | all-to-all | bytes 524288 | tf_op jit(solution)/shard_map/all_to_all | solution.py:239
  29.9 0.9 %shard_map.95 = (f32[72,128]{1,0:T(8,128)S(1)}, f32[72,128]{1,0:T(8,128)S(1)}) custom-call(s32[1]{0:T(128)} %bitcast.core_ref.c_ref, f32[16,32,128]{2,1,0:T(8,128)S(1)} %all_to_all.21.g_ref.refs_0_, f32[2048,512]{1,0:T(8,128)S(1)} %get-tuple-element.16.x_ref, f32[8,128]{1,0:T(8,128)S(1)} %get-tuple-element.17.e_ref), custom_call_target="tpu_custom_call" | custom-call | tf_op jit(solution)/shard_map/pallas_call | solution.py:241
  30.8 1.0 %collective-permute-start = (f32[72,128]{1,0:T(8,128)S(1)}, f32[72,128]{1,0:T(8,128)S(1)}, u32[]{:S(2)}, u32[]{:S(2)}) collective-permute-start(f32[72,128]{1,0:T(8,128)S(1)} %get-tuple-element.19), channel_id=1, source_target_pairs={{0,16},{16,0},{1,17},{17,1},{2,18},{18,2},{3,19},{19,3},{4,20},{20... | collective-permute-start | bytes 110600 | tf_op jit(solution)/shard_map/ppermute | solution.py:250
  31.8 0.9 %collective-permute-done.b_ref = f32[72,128]{1,0:T(8,128)S(1)} collective-permute-done((f32[72,128]{1,0:T(8,128)S(1)}, f32[72,128]{1,0:T(8,128)S(1)}, u32[]{:S(2)}, u32[]{:S(2)}) %collective-permute-start) | collective-permute-done | bytes 36896 | tf_op jit(solution)/shard_map/ppermute | solution.py:250
  32.7 16.3 %all_to_all.22.in_ref = f32[16,72,128]{2,1,0:T(8,128)S(1)} all-to-all(f32[16,72,128]{2,1,0:T(8,128)S(1)} %shard_map.96), channel_id=1, replica_groups=mesh['zl'=2,'x'=4,'c'=2,'y'=4,'zh'=4] {'x','y'}, dimensions={0} | all-to-all | bytes 1179648 | tf_op jit(solution)/shard_map/all_to_all | solution.py:256
  49.0 17.1 %all_to_all.23.in_ref = f32[8,72,128]{2,1,0:T(8,128)S(1)} all-to-all(f32[8,72,128]{2,1,0:T(8,128)S(1)} %shard_map.97), channel_id=1, replica_groups=mesh['zl'=2,'x'=4,'c'=2,'y'=4,'zh'=4] {'zl','zh'}, dimensions={0} | all-to-all | bytes 589824 | tf_op jit(solution)/shard_map/all_to_all | solution.py:260
  66.1 0.6 shard_map.98
  66.7 3.4 %collective-permute-start.1 = (f32[64,128]{1,0:T(8,128)S(1)}, f32[64,128]{1,0:T(8,128)S(1)}, u32[]{:S(2)}, u32[]{:S(2)}) collective-permute-start(f32[64,128]{1,0:T(8,128)S(1)} %get-tuple-element.22.mine_ref), channel_id=1, source_target_pairs={{0,16},{16,0},{1,17},{17,1},{2,18},{18,2},{3,19},{19,3},{4,20},{20... | collective-permute-start | bytes 98312 | tf_op jit(solution)/shard_map/ppermute | solution.py:266
  70.1 0.0 copy-done
  70.1 2.4 %shard_map.99 = f32[2048,512]{1,0:T(8,128)} custom-call(f32[16,32,128]{2,1,0:T(8,128)S(1)} %all_to_all.21.g_ref.refs_0_, f32[32,512]{1,0:T(8,128)S(1)} %bitcast.12, f32[1,128]{1,0:T(1,128)S(1)} %get-tuple-element.21.refs_2_), custom_call_target="tpu_custom_call" | custom-call | flops 201326592 | bytes 4194304 | tf_op jit(solution)/shard_map/pallas_call | solution.py:268
  72.5 0.0 collective-permute-done.1.theirs_ref
  72.5 0.6 shard_map.100
  (2 shorter events, 0.1 us)
Async XLA Ops:
  0.6 17.7 %copy-start.3 = (f32[32]{0:T(128)S(1)}, f32[32]{0:T(128)}, u32[]{:S(2)}) copy-start(f32[32]{0:T(128)} %param.11) | copy-start | bytes 388
  0.6 17.7 %copy-start.2 = (f32[2048]{0:T(1024)S(1)}, f32[2048]{0:T(1024)}, u32[]{:S(2)}) copy-start(f32[2048]{0:T(1024)} %param.10) | copy-start | bytes 24580
  0.7 17.7 %copy-start.1 = (f32[32,2048]{1,0:T(8,128)S(1)}, f32[32,2048]{1,0:T(8,128)}, u32[]{:S(2)}) copy-start(f32[32,2048]{1,0:T(8,128)} %t_ref.1) | copy-start | bytes 786436
  19.1 51.0 %copy-start = (f32[512,32]{0,1:T(8,128)S(1)}, f32[512,32]{0,1:T(8,128)}, u32[]{:S(2)}) copy-start(f32[512,32]{0,1:T(8,128)} %param.7) | copy-start | bytes 196612
  30.8 1.9 %collective-permute-start = (f32[72,128]{1,0:T(8,128)S(1)}, f32[72,128]{1,0:T(8,128)S(1)}, u32[]{:S(2)}, u32[]{:S(2)}) collective-permute-start(f32[72,128]{1,0:T(8,128)S(1)} %get-tuple-element.19), channel_id=1, source_target_pairs={{0,16},{16,0},{1,17},{17,1},{2,18},{18,2},{3,19},{19,3},{4,20},{20... | collective-permute-start | bytes 110600 | tf_op jit(solution)/shard_map/ppermute | solution.py:250
  66.7 5.7 %collective-permute-start.1 = (f32[64,128]{1,0:T(8,128)S(1)}, f32[64,128]{1,0:T(8,128)S(1)}, u32[]{:S(2)}, u32[]{:S(2)}) collective-permute-start(f32[64,128]{1,0:T(8,128)S(1)} %get-tuple-element.22.mine_ref), channel_id=1, source_target_pairs={{0,16},{16,0},{1,17},{17,1},{2,18},{18,2},{3,19},{19,3},{4,20},{20... | collective-permute-start | bytes 98312 | tf_op jit(solution)/shard_map/ppermute | solution.py:266

commit v3 on v2

v3 whole, which is shorter than its diff:
```python
import functools
import itertools

import jax
import jax.numpy as jnp
from jax import lax
from jax.experimental import pallas as pl
from jax.experimental.pallas import tpu as pltpu
from jax.sharding import Mesh, PartitionSpec as P

MEMBERS = 16
LATENT = 512
VARS = 32
SMOOTHING = 0.1
LANES = 128
BLOCK = 512
CHUNKS = BLOCK // LANES
HALF = LATENT // 2
ROWS = VARS * HALF // LANES
EXTRA = 8
SUMS = ROWS + EXTRA
MEMBER = ("zl", "x", "c")
GRID = ("y", "zh")
F32 = jnp.float32
BF16 = jnp.bfloat16
VMEM = pl.BlockSpec(memory_space=pltpu.VMEM)
SMEM = pl.BlockSpec(memory_space=pltpu.SMEM)
HBM = pl.BlockSpec(memory_space=pltpu.HBM)


def in_hbm(a):
    return pltpu.with_memory_space_constraint(a, pltpu.HBM)


def params(mib):
    return pltpu.CompilerParams(vmem_limit_bytes=mib * 1024 * 1024)


def split(a):
    hi = a.astype(BF16)
    return hi, (a - hi.astype(F32)).astype(BF16)


def dot(a, b, over):
    return lax.dot_general(a, b, (((over[0],), (over[1],)), ((), ())), preferred_element_type=F32)


def columns(row):
    return jnp.transpose(jnp.broadcast_to(row, (LANES, VARS)))


def decode_kernel(me_ref, core_ref, x_hbm, w_hbm, b_hbm, out_ref, keep_ref, send_ref, w_ref, b_ref, sems, more):
    first = [
        pltpu.make_async_copy(w_hbm, w_ref, more.at[0]),
        pltpu.make_async_copy(b_hbm, b_ref, more.at[1]),
    ]
    for copy in first:
        copy.start()
    core = core_ref[0]
    half = keep_ref.shape[0]
    jobs = []
    for part, (to_ref, side) in enumerate(((send_ref, 1 - core), (keep_ref, core))):
        for i in range(half // BLOCK):
            rows = pl.ds(i * BLOCK, BLOCK)
            source = pl.ds(pl.multiple_of(side * half, BLOCK) + i * BLOCK, BLOCK)
            copy = pltpu.make_async_copy(x_hbm.at[source], to_ref.at[rows], sems.at[part * (half // BLOCK) + i])
            copy.start()
            jobs.append((copy, to_ref, side, i))
    for copy in first:
        copy.wait()
    wh, wl = split(w_ref[...])
    both = jnp.concatenate([wh, wl], 0)
    bias = columns(b_ref[...])
    for copy, to_ref, side, i in jobs:
        copy.wait()
        xh, xl = split(to_ref[i * BLOCK : (i + 1) * BLOCK, :])
        f = dot(both, xh, (1, 1))
        f = f[:VARS] + f[VARS:] + dot(wh, xl, (1, 1))
        for j in range(CHUNKS):
            out_ref[2 * (i * CHUNKS + j) + side] = f[:, j * LANES : (j + 1) * LANES] + bias


def crps_kernel(at_ref, f_ref, t_ref, a_ref, v_ref, grad_ref, extra_ref):
    area = a_ref[pl.ds(at_ref[0], 1), :]
    scale = columns(v_ref[...]) * area
    sums = []
    loss = jnp.zeros((8, LANES), F32)
    for r in range(0, VARS, 8):
        rows = slice(r, r + 8)
        t = t_ref[rows, :]
        f = [f_ref[m, rows, :] for m in range(MEMBERS)]
        slope = [None] * MEMBERS
        near = jnp.zeros((8, LANES), F32)
        pairs = jnp.zeros((8, LANES), F32)
        total = [jnp.zeros((8, LANES), F32) for _ in range(MEMBERS)]
        for i in range(MEMBERS):
            d = f[i] - t
            q = d * d + SMOOTHING * SMOOTHING
            inv = lax.rsqrt(q)
            near = near + q * inv
            slope[i] = d * inv
            for j in range(i + 1, MEMBERS):
                d = f[i] - f[j]
                q = d * d + SMOOTHING * SMOOTHING
                inv = lax.rsqrt(q)
                pairs = pairs + q * inv
                s = d * inv
                total[i] = total[i] + s
                total[j] = total[j] - s
        norm = 1.0 / (MEMBERS * (MEMBERS - 1))
        here = scale[rows]
        loss = loss + here * (near * (1.0 / MEMBERS) - pairs * norm)
        fsum = jnp.zeros((8, LANES), F32)
        for m in range(MEMBERS):
            g = here * (slope[m] * (1.0 / MEMBERS) - total[m] * norm)
            grad_ref[m, rows, :] = g
            fsum = fsum + g
        sums.append(fsum)
    extra_ref[...] = jnp.zeros((EXTRA, LANES), F32)
    bias = jnp.sum(jnp.transpose(jnp.concatenate(sums, 0)), 0, keepdims=True)
    extra_ref[0:1, 0:VARS] = bias
    extra_ref[1:2, :] = jnp.sum(loss, 0, keepdims=True)
    extra_ref[2:3, :] = jnp.sum(a_ref[...], 0, keepdims=True)


def weight_columns(core, side, g_ref, keep_ref, got_ref, e_ref, out_ref):
    columns = pl.ds(pl.multiple_of(side * HALF, HALF), HALF)
    acc = jnp.zeros((VARS, HALF), F32)
    for x_ref, whose in ((keep_ref, core), (got_ref, 1 - core)):
        for i in range(x_ref.shape[0] // BLOCK):
            g = jnp.concatenate([g_ref[i * CHUNKS + j, whose] for j in range(CHUNKS)], 1)
            gh, gl = split(g)
            xh, xl = split(x_ref[i * BLOCK : (i + 1) * BLOCK, columns])
            both = dot(jnp.concatenate([gh, gl], 0), xh, (1, 0))
            acc = acc + (both[:VARS] + both[VARS:] + dot(gh, xl, (1, 0)))
    for i in range(HALF // LANES):
        out_ref[i * VARS : (i + 1) * VARS, :] = acc[:, i * LANES : (i + 1) * LANES]
    out_ref[ROWS:SUMS, :] = e_ref[...]


def weight_other_kernel(c_ref, g_ref, keep_ref, got_ref, e_ref, out_ref):
    core = c_ref[0]
    weight_columns(core, 1 - core, g_ref, keep_ref, got_ref, e_ref, out_ref)
    for i in range(g_ref.shape[0]):
        out_ref[SUMS + i * VARS : SUMS + (i + 1) * VARS, :] = g_ref[i, 1 - core]


def weight_own_kernel(c_ref, g_ref, keep_ref, got_ref, e_ref, out_ref):
    weight_columns(c_ref[0], c_ref[0], g_ref, keep_ref, got_ref, e_ref, out_ref)


def pair_kernel(a_ref, b_ref, *refs):
    out_ref = refs[-1]
    out_ref[...] = a_ref[...] + b_ref[:SUMS, :]


def quad_kernel(a_ref, b_ref, c_ref, d_ref, out_ref):
    out_ref[...] = (a_ref[...] + b_ref[...]) + (c_ref[...] + d_ref[...])


def latent_kernel(nodes, c_ref, g_ref, got_ref, w_ref, e_ref, out_hbm, out_ref, sems):
    core = c_ref[0]
    inv = float(nodes * MEMBERS // 2) / jnp.sum(e_ref[ROWS + 2 : ROWS + 3, :], 1, keepdims=True)
    wh, wl = split(w_ref[...])
    w = jnp.concatenate([wh, wh, wl], 0)
    half = out_ref.shape[0] // 2
    copies = []
    for part, side in enumerate((core, 1 - core)):
        for i in range(half // BLOCK):
            chips = range(i * CHUNKS, (i + 1) * CHUNKS)
            if part == 0:
                g = [g_ref[k, core] for k in chips]
            else:
                g = [got_ref[SUMS + k * VARS : SUMS + (k + 1) * VARS, :] for k in chips]
            gh, gl = split(jnp.concatenate([a * inv for a in g], 1))
            rows = pl.ds(part * half + i * BLOCK, BLOCK)
            out_ref[rows, :] = dot(jnp.concatenate([gh, gl, gh], 0), w, (0, 0))
            to = pl.ds(pl.multiple_of(side * half, BLOCK) + i * BLOCK, BLOCK)
            copies.append(pltpu.make_async_copy(out_ref.at[rows], out_hbm.at[to], sems.at[len(copies)]))
            copies[-1].start()
    for copy in copies:
        copy.wait()


def join_kernel(c_ref, a_ref, near_ref, theirs_ref, across_ref, out_ref, loss_ref, bias_ref):
    first = c_ref[0] == 0
    extra = a_ref[ROWS:, :] + near_ref[ROWS:, :]
    inv = float(MEMBERS) / jnp.sum(extra[2:3], 1, keepdims=True)
    for i in range(HALF // LANES):
        rows = slice(i * VARS, (i + 1) * VARS)
        mine = (a_ref[rows, :] + near_ref[rows, :]) * inv
        theirs = (theirs_ref[rows, :] + across_ref[rows, :]) * inv
        out_ref[:, i * LANES : (i + 1) * LANES] = jnp.where(first, mine, theirs)
        out_ref[:, HALF + i * LANES : HALF + (i + 1) * LANES] = jnp.where(first, theirs, mine)
    bias_ref[...] = extra[0:1, :VARS] * inv
    loss_ref[...] = jnp.sum(extra[1:2], 1, keepdims=True) * inv


NEAR = {0: 1, 1: 0, 2: 3, 3: 2}
FAR = {0: 3, 3: 0, 1: 2, 2: 1}
PAIRINGS = {"c": (2, {0: 1, 1: 0}), "x1": (1, NEAR), "x2": (1, FAR), "y1": (3, NEAR), "y2": (3, FAR), "z1": (4, NEAR), "z2": (4, FAR), "zl": (0, {0: 1, 1: 0})}


def trade(a, names):
    sizes = [lax.axis_size(axis) for axis in MEMBER + GRID]
    places = list(itertools.product(*[range(n) for n in sizes]))
    number = {place: i for i, place in enumerate(places)}
    pairs = []
    for place in places:
        to = list(place)
        for name in names:
            axis, pairing = PAIRINGS[name]
            to[axis] = pairing[to[axis]]
        pairs.append((number[place], number[tuple(to)]))
    return lax.ppermute(a, MEMBER + GRID, pairs)


def add_round(a, names, *after):
    if len(names) == 1:
        others = [trade(a, names)]
        kernel = pair_kernel
    else:
        others = [trade(a, names[:1]), trade(a, names[1:]), trade(a, names)]
        kernel = quad_kernel
    return pl.pallas_call(kernel, out_shape=shape(SUMS, LANES), compiler_params=params(16))(a, *others, *after)


def whole(shape):
    return pl.BlockSpec(shape, lambda *_: (0,) * len(shape))


def shape(*s):
    return jax.ShapeDtypeStruct(s, F32)


def body(latent, dec_weight, dec_bias, target, area, var_weight):
    slab = area.shape[0]
    nodes = slab * lax.axis_size("y") * lax.axis_size("zh")
    steps = slab // BLOCK
    half = slab // 2
    chips = MEMBERS // 2
    x = latent.reshape(slab, LATENT)
    wt = dec_weight.T
    core = lax.axis_index("c").astype(jnp.int32).reshape(1)
    at = core * chips + lax.axis_index(("zl", "x")).astype(jnp.int32).reshape(1)
    swap = [(0, 1), (1, 0)]

    fields, keep, send = pl.pallas_call(
        decode_kernel,
        out_shape=(shape(MEMBERS, VARS, LANES), shape(half, LATENT), shape(half, LATENT)),
        in_specs=[SMEM, SMEM, HBM, HBM, HBM],
        out_specs=(VMEM, VMEM, VMEM),
        scratch_shapes=[
            pltpu.VMEM((VARS, LATENT), F32),
            pltpu.VMEM((1, VARS), F32),
            pltpu.SemaphoreType.DMA((steps,)),
            pltpu.SemaphoreType.DMA((2,)),
        ],
        compiler_params=params(24),
    )(at, core, in_hbm(x), in_hbm(wt), in_hbm(dec_bias.reshape(1, VARS)))

    got = lax.ppermute(send, "c", swap)
    fields = lax.all_to_all(fields, MEMBER, 0, 0)

    grads, extra = pl.pallas_call(
        crps_kernel,
        out_shape=(shape(MEMBERS, VARS, LANES), shape(EXTRA, LANES)),
        grid_spec=pltpu.PrefetchScalarGridSpec(
            num_scalar_prefetch=1,
            grid=(1,),
            in_specs=[
                whole((MEMBERS, VARS, LANES)),
                pl.BlockSpec((VARS, LANES), lambda i, at: (0, at[0])),
                whole((slab // LANES, LANES)),
                whole((1, VARS)),
            ],
            out_specs=(whole((MEMBERS, VARS, LANES)), whole((EXTRA, LANES))),
        ),
        compiler_params=params(16),
    )(at, fields, target, area.reshape(slab // LANES, LANES), var_weight.reshape(1, VARS))

    grads = lax.all_to_all(grads.reshape(chips, 2, VARS, LANES), ("zl", "x"), 0, 0)

    def weight(kernel, rows):
        return pl.pallas_call(
            kernel,
            out_shape=shape(rows, LANES),
            in_specs=[SMEM, VMEM, VMEM, VMEM, VMEM],
            out_specs=VMEM,
            compiler_params=params(24),
            cost_estimate=pl.CostEstimate(flops=6 * slab * VARS * HALF, bytes_accessed=4 * slab * HALF, transcendentals=0),
        )(core, grads, keep, got, extra)

    other = weight(weight_other_kernel, SUMS + chips * VARS)
    came = lax.ppermute(other, "c", swap)
    own = weight(weight_own_kernel, SUMS)
    sums = pl.pallas_call(pair_kernel, out_shape=shape(SUMS, LANES), compiler_params=params(16))(own, came)
    sums = add_round(sums, ("x1", "y1"))
    sums = add_round(sums, ("x2", "y2"))
    sums = add_round(sums, ("z2",))
    sums = add_round(sums, ("z1",))
    across = trade(sums, ("zl", "c"))
    near = trade(sums, ("zl",))
    theirs = trade(sums, ("c",))

    grad_latent = pl.pallas_call(
        lambda *refs: latent_kernel(nodes, *refs),
        out_shape=shape(slab, LATENT),
        in_specs=[SMEM, VMEM, VMEM, VMEM, VMEM],
        out_specs=HBM,
        scratch_shapes=[pltpu.VMEM((slab, LATENT), F32), pltpu.SemaphoreType.DMA((steps,))],
        compiler_params=params(24),
        cost_estimate=pl.CostEstimate(flops=6 * slab * VARS * LATENT, bytes_accessed=4 * slab * LATENT, transcendentals=0),
    )(core, grads, came, wt, sums)

    grad_weight, loss, bias = pl.pallas_call(
        join_kernel,
        out_shape=(shape(VARS, LATENT), shape(1, 1), shape(1, VARS)),
        in_specs=[SMEM, VMEM, VMEM, VMEM, VMEM],
        out_specs=(VMEM, VMEM, VMEM),
        compiler_params=params(16),
    )(core, sums, near, theirs, across)
    return loss.reshape(()), grad_latent[None], grad_weight.T, bias.reshape(VARS)


def solution(mesh):
    shaped = Mesh(mesh.devices.reshape(2, 4, 2, 4, 4), MEMBER + GRID)
    return jax.shard_map(
        body,
        mesh=shaped,
        in_specs=(P(MEMBER, GRID, None), P(), P(), P(None, GRID), P(GRID), P()),
        out_specs=(P(), P(MEMBER, GRID, None), P(), P()),
        check_vma=False,
    )
```

time: 73.4 us -> 64.6 us (0.88)
  blocking collectives: 58.3 us -> 19.8 us
  starting transfers between devices: 4.36 us -> 26.7 us
  waiting for transfers between devices: 0.87 us -> 8.41 us
    all_to_all x3 -> x1, blocking collectives: 44.1 us -> 8.84 us  [body(): lax.all_to_all(grads.reshape(chips, 2, VARS, LANES), ('zl', 'x'), 0, 0)]
    ppermute x1 -> x12, starting transfers between devices: 3.36 us -> 24.6 us  [the longest x11 21.3 us: trade(): return lax.ppermute(a, MEMBER + GRID, pairs)]
    ppermute x1 -> x12, waiting for transfers between devices: 0.01 us -> 7.94 us  [the longest x11 7.94 us: trade(): return lax.ppermute(a, MEMBER + GRID, pairs)]
    all_to_all x1, blocking collectives: 14.1 us -> 11 us  [body(): fields = lax.all_to_all(fields, MEMBER, 0, 0)]
    ppermute x1, starting transfers between devices: 1 us -> 2.06 us  [body(): came = lax.ppermute(other, 'c', swap)]
    pallas_call x5 -> x8, Pallas kernels: 2.2 us -> 1.91 us  [the longest x2 1.14 us: weight(): pl.pallas_call(kernel, out_shape=shape(rows, LANES), in_specs=[SMEM, VMEM...]
  transfers between devices with their start and end apart: 2 -> 13, of which waited for: 1 -> 9; matrix products, arithmetic and copies ran while one was open for 0% -> 0% of each run, Pallas kernels for 3% -> 6%
where the time goes in v3:
time: 64.6 us; the launch traced here: 64.4 us
  starting transfers between devices  26.7 us (41%)
  blocking collectives  19.8 us (31%)
  Pallas kernels  8.75 us (14%)
  waiting for transfers between devices  8.41 us (13%)
  between operations  0.74 us (1%)
    ppermute x11, starting transfers between devices, trade(): return lax.ppermute(a, MEMBER + GRID, pairs)  21.3 us
    all_to_all x1, blocking collectives, body(): fields = lax.all_to_all(fields, MEMBER, 0, 0)  11 us
    all_to_all x1, blocking collectives, body(): lax.all_to_all(grads.reshape(chips, 2, VARS, LANES), ('zl', 'x'), 0, 0)  8.84 us
    ppermute x11, waiting for transfers between devices, trade(): return lax.ppermute(a, MEMBER + GRID, pairs)  7.94 us
    pallas_call x1, Pallas kernels, body(): pl.pallas_call(decode_kernel, out_shape=(shape(MEMBERS, VARS, LANES), sha...  3.56 us
    ppermute x1, starting transfers between devices, body(): got = lax.ppermute(send, 'c', swap)  3.33 us
    pallas_call x1, Pallas kernels, body(): pl.pallas_call(lambda *refs: latent_kernel(nodes, *refs), out_shape=shape...  2.46 us
    ppermute x1, starting transfers between devices, body(): came = lax.ppermute(other, 'c', swap)  2.06 us
  transfers between devices with their start and end apart: 13, of which 9 were waited for; matrix products, arithmetic and copies ran while one was open for 0% of the time, Pallas kernels for 6%

profile of v3, /device:TPU:1, one launch (start us, length us, event | category | flops | bytes accessed | tf_op | source)
XLA Modules:
  0.0 64.4 jit_solution(8601337805458241922)
XLA Ops:
  0.7 3.6 %shard_map.93 = (f32[16,32,128]{2,1,0:T(8,128)S(1)}, f32[1024,512]{1,0:T(8,128)S(1)}, f32[1024,512]{1,0:T(8,128)S(1)}) custom-call(s32[1]{0:T(128)S(6)} %add.7.me_ref.at_ref, s32[1]{0:T(128)} %bitcast.core_ref.c_ref.refs_0_, f32[2048,512]{1,0:T(8,128)} %bitcast.17, f32[32,512]{1,0:T(8,128)} %bitcast.12, f32[1,32]{1,0:T(1,128)} %bitcast.19), custom_call_target="tpu_custom_call" | custom-call | tf_op jit(solution)/shard_map/pallas_call | solution.py:248
  4.2 3.3 %collective-permute-start = (f32[1024,512]{1,0:T(8,128)S(1)}, f32[1024,512]{1,0:T(8,128)S(1)}, u32[]{:S(2)}, u32[]{:S(2)}) collective-permute-start(f32[1024,512]{1,0:T(8,128)S(1)} %get-tuple-element.15), channel_id=1, source_target_pairs={{0,16},{16,0},{1,17},{17,1},{2,18},{18,2},{3,19},{19,3},{4,20},{20... | collective-permute-start | bytes 6291464 | tf_op jit(solution)/shard_map/ppermute | solution.py:262
  7.6 11.0 %all_to_all.10.f_ref = f32[16,32,128]{2,1,0:T(8,128)S(1)} all-to-all(f32[16,32,128]{2,1,0:T(8,128)S(1)} %get-tuple-element.12), channel_id=1, replica_groups=mesh['zl'=2,'x'=4,'c'=2,'y'=4,'zh'=4] {'zl','x','c'}, dimensions={0} | all-to-all | bytes 524288 | tf_op jit(solution)/shard_map/all_to_all | solution.py:263
  18.6 0.8 %shard_map.94 = (f32[16,32,128]{2,1,0:T(8,128)S(1)}, f32[8,128]{1,0:T(8,128)S(1)}) custom-call(s32[1]{0:T(128)S(6)} %add.7.me_ref.at_ref, f32[16,32,128]{2,1,0:T(8,128)S(1)} %all_to_all.10.f_ref, f32[32,2048]{1,0:T(8,128)S(1)} %copy-done.1, f32[16,128]{1,0:T(8,128)S(1)} %bitcast.15, f32[1,32]{1,0:T(1,128)S(1)} %bitcast.16), custom_call_target="tpu_custom_call" | custom-call | tf_op jit(solution)/shard_map/pallas_call | solution.py:265
  19.4 8.8 %all_to_all.11.g_ref.refs_1_ = f32[8,2,32,128]{3,2,1,0:T(8,128)S(1)} all-to-all(f32[8,2,32,128]{3,2,1,0:T(8,128)S(1)} %bitcast.14), channel_id=1, replica_groups=mesh['zl'=2,'x'=4,'c'=2,'y'=4,'zh'=4] {'zl','x'}, dimensions={0} | all-to-all | bytes 524288 | tf_op jit(solution)/shard_map/all_to_all | solution.py:282
  28.2 0.6 shard_map.96
  28.8 0.0 copy-start
  28.8 2.1 %collective-permute-start.1 = (f32[328,128]{1,0:T(8,128)S(1)}, f32[328,128]{1,0:T(8,128)S(1)}, u32[]{:S(2)}, u32[]{:S(2)}) collective-permute-start(f32[328,128]{1,0:T(8,128)S(1)} %shard_map.96), channel_id=1, source_target_pairs={{0,16},{16,0},{1,17},{17,1},{2,18},{18,2},{3,19},{19,3},{4,20},{20... | collective-permute-start | bytes 503816 | tf_op jit(solution)/shard_map/ppermute | solution.py:295
  30.9 0.6 shard_map.95.a_ref
  31.4 0.5 collective-permute-done.1.b_ref.refs_2_
  31.9 0.9 %collective-permute-start.4 = (f32[72,128]{1,0:T(8,128)S(1)}, f32[72,128]{1,0:T(8,128)S(1)}, u32[]{:S(2)}, u32[]{:S(2)}) collective-permute-start(f32[72,128]{1,0:T(8,128)S(1)} %shard_map.97.a_ref), channel_id=1, source_target_pairs={{0,36},{1,37},{2,38},{3,39},{4,32},{5,33},{6,34},{7,35},{8,44},{9,... | collective-permute-start | bytes 110600 | tf_op jit(solution)/shard_map/ppermute | solution.py:215
  32.9 0.4 collective-permute-start.3
  33.3 1.3 %collective-permute-start.2 = (f32[72,128]{1,0:T(8,128)S(1)}, f32[72,128]{1,0:T(8,128)S(1)}, u32[]{:S(2)}, u32[]{:S(2)}) collective-permute-start(f32[72,128]{1,0:T(8,128)S(1)} %shard_map.97.a_ref), channel_id=1, source_target_pairs={{0,32},{1,33},{2,34},{3,35},{4,36},{5,37},{6,38},{7,39},{8,40},{9,... | collective-permute-start | bytes 110600 | tf_op jit(solution)/shard_map/ppermute | solution.py:215
  34.6 1.1 %collective-permute-done.4.d_ref = f32[72,128]{1,0:T(8,128)S(1)} collective-permute-done((f32[72,128]{1,0:T(8,128)S(1)}, f32[72,128]{1,0:T(8,128)S(1)}, u32[]{:S(2)}, u32[]{:S(2)}) %collective-permute-start.4) | collective-permute-done | bytes 36896 | tf_op jit(solution)/shard_map/ppermute | solution.py:215
  35.7 0.7 %collective-permute-done.3.c_ref = f32[72,128]{1,0:T(8,128)S(1)} collective-permute-done((f32[72,128]{1,0:T(8,128)S(1)}, f32[72,128]{1,0:T(8,128)S(1)}, u32[]{:S(2)}, u32[]{:S(2)}) %collective-permute-start.3) | collective-permute-done | bytes 36896 | tf_op jit(solution)/shard_map/ppermute | solution.py:215
  36.3 0.1 collective-permute-done.2.b_ref
  36.4 3.2 %collective-permute-start.7 = (f32[72,128]{1,0:T(8,128)S(1)}, f32[72,128]{1,0:T(8,128)S(1)}, u32[]{:S(2)}, u32[]{:S(2)}) collective-permute-start(f32[72,128]{1,0:T(8,128)S(1)} %shard_map.98.a_ref), channel_id=1, source_target_pairs={{0,108},{1,109},{2,110},{3,111},{4,104},{5,105},{6,106},{7,107},{8... | collective-permute-start | bytes 110600 | tf_op jit(solution)/shard_map/ppermute | solution.py:215
  39.7 0.1 collective-permute-start.6
  39.7 1.9 %collective-permute-start.5 = (f32[72,128]{1,0:T(8,128)S(1)}, f32[72,128]{1,0:T(8,128)S(1)}, u32[]{:S(2)}, u32[]{:S(2)}) collective-permute-start(f32[72,128]{1,0:T(8,128)S(1)} %shard_map.98.a_ref), channel_id=1, source_target_pairs={{0,96},{1,97},{2,98},{3,99},{4,100},{5,101},{6,102},{7,103},{8,104... | collective-permute-start | bytes 110600 | tf_op jit(solution)/shard_map/ppermute | solution.py:215
  41.7 1.0 %collective-permute-done.7.d_ref = f32[72,128]{1,0:T(8,128)S(1)} collective-permute-done((f32[72,128]{1,0:T(8,128)S(1)}, f32[72,128]{1,0:T(8,128)S(1)}, u32[]{:S(2)}, u32[]{:S(2)}) %collective-permute-start.7) | collective-permute-done | bytes 36896 | tf_op jit(solution)/shard_map/ppermute | solution.py:215
  42.7 1.3 %collective-permute-done.6.c_ref = f32[72,128]{1,0:T(8,128)S(1)} collective-permute-done((f32[72,128]{1,0:T(8,128)S(1)}, f32[72,128]{1,0:T(8,128)S(1)}, u32[]{:S(2)}, u32[]{:S(2)}) %collective-permute-start.6) | collective-permute-done | bytes 36896 | tf_op jit(solution)/shard_map/ppermute | solution.py:215
  44.0 0.1 collective-permute-done.5.b_ref
  44.1 5.2 %collective-permute-start.8 = (f32[72,128]{1,0:T(8,128)S(1)}, f32[72,128]{1,0:T(8,128)S(1)}, u32[]{:S(2)}, u32[]{:S(2)}) collective-permute-start(f32[72,128]{1,0:T(8,128)S(1)} %shard_map.99.a_ref), channel_id=1, source_target_pairs={{0,3},{1,2},{2,1},{3,0},{4,7},{5,6},{6,5},{7,4},{8,11},{9,10},{10,... | collective-permute-start | bytes 110600 | tf_op jit(solution)/shard_map/ppermute | solution.py:215
  49.3 1.3 %collective-permute-done.8.b_ref = f32[72,128]{1,0:T(8,128)S(1)} collective-permute-done((f32[72,128]{1,0:T(8,128)S(1)}, f32[72,128]{1,0:T(8,128)S(1)}, u32[]{:S(2)}, u32[]{:S(2)}) %collective-permute-start.8) | collective-permute-done | bytes 36896 | tf_op jit(solution)/shard_map/ppermute | solution.py:215
  50.6 1.8 %collective-permute-start.9 = (f32[72,128]{1,0:T(8,128)S(1)}, f32[72,128]{1,0:T(8,128)S(1)}, u32[]{:S(2)}, u32[]{:S(2)}) collective-permute-start(f32[72,128]{1,0:T(8,128)S(1)} %shard_map.100.a_ref), channel_id=1, source_target_pairs={{0,1},{1,0},{2,3},{3,2},{4,5},{5,4},{6,7},{7,6},{8,9},{9,8},{10,11... | collective-permute-start | bytes 110600 | tf_op jit(solution)/shard_map/ppermute | solution.py:215
  52.5 2.3 %collective-permute-done.9.b_ref = f32[72,128]{1,0:T(8,128)S(1)} collective-permute-done((f32[72,128]{1,0:T(8,128)S(1)}, f32[72,128]{1,0:T(8,128)S(1)}, u32[]{:S(2)}, u32[]{:S(2)}) %collective-permute-start.9) | collective-permute-done | bytes 36896 | tf_op jit(solution)/shard_map/ppermute | solution.py:215
  54.8 5.2 %collective-permute-start.12 = (f32[72,128]{1,0:T(8,128)S(1)}, f32[72,128]{1,0:T(8,128)S(1)}, u32[]{:S(2)}, u32[]{:S(2)}) collective-permute-start(f32[72,128]{1,0:T(8,128)S(1)} %shard_map.101.a_ref.refs_4_), channel_id=1, source_target_pairs={{0,144},{1,145},{2,146},{3,147},{4,148},{5,149},{6,150},{7,151},{8... | collective-permute-start | bytes 110600 | tf_op jit(solution)/shard_map/ppermute | solution.py:215
  60.0 0.0 collective-permute-start.11
  60.0 1.2 %collective-permute-start.10 = (f32[72,128]{1,0:T(8,128)S(1)}, f32[72,128]{1,0:T(8,128)S(1)}, u32[]{:S(2)}, u32[]{:S(2)}) collective-permute-start(f32[72,128]{1,0:T(8,128)S(1)} %shard_map.101.a_ref.refs_4_), channel_id=1, source_target_pairs={{0,128},{1,129},{2,130},{3,131},{4,132},{5,133},{6,134},{7,135},{8... | collective-permute-start | bytes 110600 | tf_op jit(solution)/shard_map/ppermute | solution.py:215
  61.2 2.5 %shard_map.103 = f32[2048,512]{1,0:T(8,128)} custom-call(s32[1]{0:T(128)} %bitcast.core_ref.c_ref.refs_0_, f32[8,2,32,128]{3,2,1,0:T(8,128)S(1)} %all_to_all.11.g_ref.refs_1_, f32[328,128]{1,0:T(8,128)S(1)} %collective-permute-done.1.b_ref.refs_2_, f32[32,512]{1,0:T(8,128)S(1)} %bitcast.13, f32[72,128]{1,0:T(8,128)S(1)} %shard_map.101.a_ref.refs_4_), custom_call_target="tpu_custom_call" | custom-call | flops 201326592 | bytes 4194304 | tf_op jit(solution)/shard_map/pallas_call | solution.py:306
  63.7 0.0 collective-permute-done.12.across_ref
  63.7 0.7 %shard_map.102 = (f32[32,512]{1,0:T(8,128)}, f32[1,1]{1,0:T(1,128)}, f32[1,32]{1,0:T(1,128)}) custom-call(s32[1]{0:T(128)} %bitcast.core_ref.c_ref.refs_0_, f32[72,128]{1,0:T(8,128)S(1)} %shard_map.101.a_ref.refs_4_, f32[72,128]{1,0:T(8,128)S(1)} %collective-permute-done.10.near_ref, f32[72,128]{1,0:T(8,128)S(1)} %collective-permute-done.11.theirs_ref, ...), custom_call_target="tpu_custom_call" | custom-call | tf_op jit(solution)/shard_map/pallas_call | solution.py:316
  (15 shorter events, 0.1 us)
Async XLA Ops:
  0.6 17.9 %copy-start.1 = (f32[32,2048]{1,0:T(8,128)S(1)}, f32[32,2048]{1,0:T(8,128)}, u32[]{:S(2)}) copy-start(f32[32,2048]{1,0:T(8,128)} %t_ref.1) | copy-start | bytes 786436
  0.7 17.9 %copy-start.2 = (f32[2048]{0:T(1024)S(1)}, f32[2048]{0:T(1024)}, u32[]{:S(2)}) copy-start(f32[2048]{0:T(1024)} %param.10) | copy-start | bytes 24580
  0.7 17.9 %copy-start.3 = (f32[32]{0:T(128)S(1)}, f32[32]{0:T(128)}, u32[]{:S(2)}) copy-start(f32[32]{0:T(128)} %param.11) | copy-start | bytes 388
  4.2 24.0 %collective-permute-start = (f32[1024,512]{1,0:T(8,128)S(1)}, f32[1024,512]{1,0:T(8,128)S(1)}, u32[]{:S(2)}, u32[]{:S(2)}) collective-permute-start(f32[1024,512]{1,0:T(8,128)S(1)} %get-tuple-element.15), channel_id=1, source_target_pairs={{0,16},{16,0},{1,17},{17,1},{2,18},{18,2},{3,19},{19,3},{4,20},{20... | collective-permute-start | bytes 6291464 | tf_op jit(solution)/shard_map/ppermute | solution.py:262
  28.8 32.4 %copy-start = (f32[512,32]{0,1:T(8,128)S(1)}, f32[512,32]{0,1:T(8,128)}, u32[]{:S(2)}) copy-start(f32[512,32]{0,1:T(8,128)} %param.7) | copy-start | bytes 196612
  28.8 3.1 %collective-permute-start.1 = (f32[328,128]{1,0:T(8,128)S(1)}, f32[328,128]{1,0:T(8,128)S(1)}, u32[]{:S(2)}, u32[]{:S(2)}) collective-permute-start(f32[328,128]{1,0:T(8,128)S(1)} %shard_map.96), channel_id=1, source_target_pairs={{0,16},{16,0},{1,17},{17,1},{2,18},{18,2},{3,19},{19,3},{4,20},{20... | collective-permute-start | bytes 503816 | tf_op jit(solution)/shard_map/ppermute | solution.py:295
  31.9 3.7 %collective-permute-start.4 = (f32[72,128]{1,0:T(8,128)S(1)}, f32[72,128]{1,0:T(8,128)S(1)}, u32[]{:S(2)}, u32[]{:S(2)}) collective-permute-start(f32[72,128]{1,0:T(8,128)S(1)} %shard_map.97.a_ref), channel_id=1, source_target_pairs={{0,36},{1,37},{2,38},{3,39},{4,32},{5,33},{6,34},{7,35},{8,44},{9,... | collective-permute-start | bytes 110600 | tf_op jit(solution)/shard_map/ppermute | solution.py:215
  32.9 3.5 %collective-permute-start.3 = (f32[72,128]{1,0:T(8,128)S(1)}, f32[72,128]{1,0:T(8,128)S(1)}, u32[]{:S(2)}, u32[]{:S(2)}) collective-permute-start(f32[72,128]{1,0:T(8,128)S(1)} %shard_map.97.a_ref), channel_id=1, source_target_pairs={{0,4},{1,5},{2,6},{3,7},{4,0},{5,1},{6,2},{7,3},{8,12},{9,13},{10,... | collective-permute-start | bytes 110600 | tf_op jit(solution)/shard_map/ppermute | solution.py:215
  33.3 3.1 %collective-permute-start.2 = (f32[72,128]{1,0:T(8,128)S(1)}, f32[72,128]{1,0:T(8,128)S(1)}, u32[]{:S(2)}, u32[]{:S(2)}) collective-permute-start(f32[72,128]{1,0:T(8,128)S(1)} %shard_map.97.a_ref), channel_id=1, source_target_pairs={{0,32},{1,33},{2,34},{3,35},{4,36},{5,37},{6,38},{7,39},{8,40},{9,... | collective-permute-start | bytes 110600 | tf_op jit(solution)/shard_map/ppermute | solution.py:215
  36.4 6.2 %collective-permute-start.7 = (f32[72,128]{1,0:T(8,128)S(1)}, f32[72,128]{1,0:T(8,128)S(1)}, u32[]{:S(2)}, u32[]{:S(2)}) collective-permute-start(f32[72,128]{1,0:T(8,128)S(1)} %shard_map.98.a_ref), channel_id=1, source_target_pairs={{0,108},{1,109},{2,110},{3,111},{4,104},{5,105},{6,106},{7,107},{8... | collective-permute-start | bytes 110600 | tf_op jit(solution)/shard_map/ppermute | solution.py:215
  39.7 4.3 %collective-permute-start.6 = (f32[72,128]{1,0:T(8,128)S(1)}, f32[72,128]{1,0:T(8,128)S(1)}, u32[]{:S(2)}, u32[]{:S(2)}) collective-permute-start(f32[72,128]{1,0:T(8,128)S(1)} %shard_map.98.a_ref), channel_id=1, source_target_pairs={{0,12},{1,13},{2,14},{3,15},{4,8},{5,9},{6,10},{7,11},{8,4},{9,5},... | collective-permute-start | bytes 110600 | tf_op jit(solution)/shard_map/ppermute | solution.py:215
  39.7 4.3 %collective-permute-start.5 = (f32[72,128]{1,0:T(8,128)S(1)}, f32[72,128]{1,0:T(8,128)S(1)}, u32[]{:S(2)}, u32[]{:S(2)}) collective-permute-start(f32[72,128]{1,0:T(8,128)S(1)} %shard_map.98.a_ref), channel_id=1, source_target_pairs={{0,96},{1,97},{2,98},{3,99},{4,100},{5,101},{6,102},{7,103},{8,104... | collective-permute-start | bytes 110600 | tf_op jit(solution)/shard_map/ppermute | solution.py:215
  44.1 6.6 %collective-permute-start.8 = (f32[72,128]{1,0:T(8,128)S(1)}, f32[72,128]{1,0:T(8,128)S(1)}, u32[]{:S(2)}, u32[]{:S(2)}) collective-permute-start(f32[72,128]{1,0:T(8,128)S(1)} %shard_map.99.a_ref), channel_id=1, source_target_pairs={{0,3},{1,2},{2,1},{3,0},{4,7},{5,6},{6,5},{7,4},{8,11},{9,10},{10,... | collective-permute-start | bytes 110600 | tf_op jit(solution)/shard_map/ppermute | solution.py:215
  50.6 4.2 %collective-permute-start.9 = (f32[72,128]{1,0:T(8,128)S(1)}, f32[72,128]{1,0:T(8,128)S(1)}, u32[]{:S(2)}, u32[]{:S(2)}) collective-permute-start(f32[72,128]{1,0:T(8,128)S(1)} %shard_map.100.a_ref), channel_id=1, source_target_pairs={{0,1},{1,0},{2,3},{3,2},{4,5},{5,4},{6,7},{7,6},{8,9},{9,8},{10,11... | collective-permute-start | bytes 110600 | tf_op jit(solution)/shard_map/ppermute | solution.py:215
  54.8 8.9 %collective-permute-start.12 = (f32[72,128]{1,0:T(8,128)S(1)}, f32[72,128]{1,0:T(8,128)S(1)}, u32[]{:S(2)}, u32[]{:S(2)}) collective-permute-start(f32[72,128]{1,0:T(8,128)S(1)} %shard_map.101.a_ref.refs_4_), channel_id=1, source_target_pairs={{0,144},{1,145},{2,146},{3,147},{4,148},{5,149},{6,150},{7,151},{8... | collective-permute-start | bytes 110600 | tf_op jit(solution)/shard_map/ppermute | solution.py:215
  60.0 3.7 %collective-permute-start.11 = (f32[72,128]{1,0:T(8,128)S(1)}, f32[72,128]{1,0:T(8,128)S(1)}, u32[]{:S(2)}, u32[]{:S(2)}) collective-permute-start(f32[72,128]{1,0:T(8,128)S(1)} %shard_map.101.a_ref.refs_4_), channel_id=1, source_target_pairs={{0,16},{1,17},{2,18},{3,19},{4,20},{5,21},{6,22},{7,23},{8,24},{9,... | collective-permute-start | bytes 110600 | tf_op jit(solution)/shard_map/ppermute | solution.py:215
  60.0 3.7 %collective-permute-start.10 = (f32[72,128]{1,0:T(8,128)S(1)}, f32[72,128]{1,0:T(8,128)S(1)}, u32[]{:S(2)}, u32[]{:S(2)}) collective-permute-start(f32[72,128]{1,0:T(8,128)S(1)} %shard_map.101.a_ref.refs_4_), channel_id=1, source_target_pairs={{0,128},{1,129},{2,130},{3,131},{4,132},{5,133},{6,134},{7,135},{8... | collective-permute-start | bytes 110600 | tf_op jit(solution)/shard_map/ppermute | solution.py:215

commit v4 on v3

--- a/solution.py
+++ b/solution.py
@@ -49,7 +49,7 @@
     return jnp.transpose(jnp.broadcast_to(row, (LANES, VARS)))
 
 
-def decode_kernel(me_ref, core_ref, x_hbm, w_hbm, b_hbm, out_ref, keep_ref, send_ref, w_ref, b_ref, sems, more):
+def decode_kernel(me_ref, held_ref, core_ref, x_hbm, w_hbm, b_hbm, out_ref, keep_ref, send_ref, w_ref, b_ref, sems, more):
     first = [
         pltpu.make_async_copy(w_hbm, w_ref, more.at[0]),
         pltpu.make_async_copy(b_hbm, b_ref, more.at[1]),
@@ -60,24 +60,22 @@
     half = keep_ref.shape[0]
     jobs = []
     for part, (to_ref, side) in enumerate(((send_ref, 1 - core), (keep_ref, core))):
-        for i in range(half // BLOCK):
-            rows = pl.ds(i * BLOCK, BLOCK)
-            source = pl.ds(pl.multiple_of(side * half, BLOCK) + i * BLOCK, BLOCK)
-            copy = pltpu.make_async_copy(x_hbm.at[source], to_ref.at[rows], sems.at[part * (half // BLOCK) + i])
-            copy.start()
-            jobs.append((copy, to_ref, side, i))
+        source = pl.ds(pl.multiple_of(side * half, BLOCK), half)
+        copy = pltpu.make_async_copy(x_hbm.at[source], to_ref, sems.at[part])
+        copy.start()
+        jobs.append((copy, to_ref, side))
     for copy in first:
         copy.wait()
     wh, wl = split(w_ref[...])
     both = jnp.concatenate([wh, wl], 0)
     bias = columns(b_ref[...])
-    for copy, to_ref, side, i in jobs:
+    for copy, to_ref, side in jobs:
         copy.wait()
-        xh, xl = split(to_ref[i * BLOCK : (i + 1) * BLOCK, :])
+        xh, xl = split(to_ref[...])
         f = dot(both, xh, (1, 1))
         f = f[:VARS] + f[VARS:] + dot(wh, xl, (1, 1))
-        for j in range(CHUNKS):
-            out_ref[2 * (i * CHUNKS + j) + side] = f[:, j * LANES : (j + 1) * LANES] + bias
+        for j in range(half // LANES):
+            out_ref[2 * j + side] = f[:, j * LANES : (j + 1) * LANES] + bias
 
 
 def crps_kernel(at_ref, f_ref, t_ref, a_ref, v_ref, grad_ref, extra_ref):
@@ -138,15 +136,15 @@
     out_ref[ROWS:SUMS, :] = e_ref[...]
 
 
-def weight_other_kernel(c_ref, g_ref, keep_ref, got_ref, e_ref, out_ref):
+def weight_other_kernel(c_ref, h_ref, g_ref, keep_ref, got_ref, e_ref, out_ref):
     core = c_ref[0]
-    weight_columns(core, 1 - core, g_ref, keep_ref, got_ref, e_ref, out_ref)
+    weight_columns(core, 1 - h_ref[0], g_ref, keep_ref, got_ref, e_ref, out_ref)
     for i in range(g_ref.shape[0]):
         out_ref[SUMS + i * VARS : SUMS + (i + 1) * VARS, :] = g_ref[i, 1 - core]
 
 
-def weight_own_kernel(c_ref, g_ref, keep_ref, got_ref, e_ref, out_ref):
-    weight_columns(c_ref[0], c_ref[0], g_ref, keep_ref, got_ref, e_ref, out_ref)
+def weight_own_kernel(c_ref, h_ref, g_ref, keep_ref, got_ref, e_ref, out_ref):
+    weight_columns(c_ref[0], h_ref[0], g_ref, keep_ref, got_ref, e_ref, out_ref)
 
 
 def pair_kernel(a_ref, b_ref, *refs):
@@ -160,7 +158,7 @@
 
 def latent_kernel(nodes, c_ref, g_ref, got_ref, w_ref, e_ref, out_hbm, out_ref, sems):
     core = c_ref[0]
-    inv = float(nodes * MEMBERS // 2) / jnp.sum(e_ref[ROWS + 2 : ROWS + 3, :], 1, keepdims=True)
+    inv = float(nodes * MEMBERS) / jnp.sum(e_ref[ROWS + 2 : ROWS + 3, :], 1, keepdims=True)
     wh, wl = split(w_ref[...])
     w = jnp.concatenate([wh, wh, wl], 0)
     half = out_ref.shape[0] // 2
@@ -182,14 +180,13 @@
         copy.wait()
 
 
-def join_kernel(c_ref, a_ref, near_ref, theirs_ref, across_ref, out_ref, loss_ref, bias_ref):
+def join_kernel(c_ref, mine_ref, theirs_ref, out_ref, loss_ref, bias_ref):
     first = c_ref[0] == 0
-    extra = a_ref[ROWS:, :] + near_ref[ROWS:, :]
+    extra = mine_ref[ROWS:, :]
     inv = float(MEMBERS) / jnp.sum(extra[2:3], 1, keepdims=True)
     for i in range(HALF // LANES):
         rows = slice(i * VARS, (i + 1) * VARS)
-        mine = (a_ref[rows, :] + near_ref[rows, :]) * inv
-        theirs = (theirs_ref[rows, :] + across_ref[rows, :]) * inv
+        mine, theirs = mine_ref[rows, :] * inv, theirs_ref[rows, :] * inv
         out_ref[:, i * LANES : (i + 1) * LANES] = jnp.where(first, mine, theirs)
         out_ref[:, HALF + i * LANES : HALF + (i + 1) * LANES] = jnp.where(first, theirs, mine)
     bias_ref[...] = extra[0:1, :VARS] * inv
@@ -198,7 +195,7 @@
 
 NEAR = {0: 1, 1: 0, 2: 3, 3: 2}
 FAR = {0: 3, 3: 0, 1: 2, 2: 1}
-PAIRINGS = {"c": (2, {0: 1, 1: 0}), "x1": (1, NEAR), "x2": (1, FAR), "y1": (3, NEAR), "y2": (3, FAR), "z1": (4, NEAR), "z2": (4, FAR), "zl": (0, {0: 1, 1: 0})}
+PAIRINGS = {"x1": (1, NEAR), "x2": (1, FAR), "y1": (3, NEAR), "y2": (3, FAR), "z1": (4, NEAR), "z2": (4, FAR), "zl": (0, {0: 1, 1: 0})}
 
 
 def trade(a, names):
@@ -211,6 +208,7 @@
         for name in names:
             axis, pairing = PAIRINGS[name]
             to[axis] = pairing[to[axis]]
+            to[2] = 1 - to[2]
         pairs.append((number[place], number[tuple(to)]))
     return lax.ppermute(a, MEMBER + GRID, pairs)
 
@@ -243,21 +241,22 @@
     wt = dec_weight.T
     core = lax.axis_index("c").astype(jnp.int32).reshape(1)
     at = core * chips + lax.axis_index(("zl", "x")).astype(jnp.int32).reshape(1)
+    held = (core + sum(lax.axis_index(axis) for axis in ("zl", "x", "y", "zh"))).astype(jnp.int32) & 1
     swap = [(0, 1), (1, 0)]
 
     fields, keep, send = pl.pallas_call(
         decode_kernel,
         out_shape=(shape(MEMBERS, VARS, LANES), shape(half, LATENT), shape(half, LATENT)),
-        in_specs=[SMEM, SMEM, HBM, HBM, HBM],
+        in_specs=[SMEM, SMEM, SMEM, HBM, HBM, HBM],
         out_specs=(VMEM, VMEM, VMEM),
         scratch_shapes=[
             pltpu.VMEM((VARS, LATENT), F32),
             pltpu.VMEM((1, VARS), F32),
-            pltpu.SemaphoreType.DMA((steps,)),
+            pltpu.SemaphoreType.DMA((2,)),
             pltpu.SemaphoreType.DMA((2,)),
         ],
         compiler_params=params(24),
-    )(at, core, in_hbm(x), in_hbm(wt), in_hbm(dec_bias.reshape(1, VARS)))
+    )(at, held, core, in_hbm(x), in_hbm(wt), in_hbm(dec_bias.reshape(1, VARS)))
 
     got = lax.ppermute(send, "c", swap)
     fields = lax.all_to_all(fields, MEMBER, 0, 0)
@@ -285,11 +284,11 @@
         return pl.pallas_call(
             kernel,
             out_shape=shape(rows, LANES),
-            in_specs=[SMEM, VMEM, VMEM, VMEM, VMEM],
+            in_specs=[SMEM, SMEM, VMEM, VMEM, VMEM, VMEM],
             out_specs=VMEM,
             compiler_params=params(24),
             cost_estimate=pl.CostEstimate(flops=6 * slab * VARS * HALF, bytes_accessed=4 * slab * HALF, transcendentals=0),
-        )(core, grads, keep, got, extra)
+        )(core, held, grads, keep, got, extra)
 
     other = weight(weight_other_kernel, SUMS + chips * VARS)
     came = lax.ppermute(other, "c", swap)
@@ -297,11 +296,9 @@
     sums = pl.pallas_call(pair_kernel, out_shape=shape(SUMS, LANES), compiler_params=params(16))(own, came)
     sums = add_round(sums, ("x1", "y1"))
     sums = add_round(sums, ("x2", "y2"))
+    sums = add_round(sums, ("zl", "z1"))
     sums = add_round(sums, ("z2",))
-    sums = add_round(sums, ("z1",))
-    across = trade(sums, ("zl", "c"))
-    near = trade(sums, ("zl",))
-    theirs = trade(sums, ("c",))
+    theirs = lax.ppermute(sums, "c", swap)
 
     grad_latent = pl.pallas_call(
         lambda *refs: latent_kernel(nodes, *refs),
@@ -316,10 +313,10 @@
     grad_weight, loss, bias = pl.pallas_call(
         join_kernel,
         out_shape=(shape(VARS, LATENT), shape(1, 1), shape(1, VARS)),
-        in_specs=[SMEM, VMEM, VMEM, VMEM, VMEM],
+        in_specs=[SMEM, VMEM, VMEM],
         out_specs=(VMEM, VMEM, VMEM),
         compiler_params=params(16),
-    )(core, sums, near, theirs, across)
+    )(held, sums, theirs)
     return loss.reshape(()), grad_latent[None], grad_weight.T, bias.reshape(VARS)
 
 

time: 64.6 us -> 63.3 us (0.980)
  starting transfers between devices: 26.7 us -> 21.7 us
  waiting for transfers between devices: 8.41 us -> 12.6 us
    ppermute x11 -> x10, starting transfers between devices: 21.3 us -> 15.9 us  [trade(): return lax.ppermute(a, MEMBER + GRID, pairs)]
    ppermute x11 -> x10, waiting for transfers between devices: 7.94 us -> 12.1 us  [trade(): return lax.ppermute(a, MEMBER + GRID, pairs)]
where the time goes in v4:
time: 63.3 us; the launch traced here: 63.2 us
  starting transfers between devices  21.7 us (34%)
  blocking collectives  19.8 us (31%)
  waiting for transfers between devices  12.6 us (20%)
  Pallas kernels  8.33 us (13%)
  between operations  0.74 us (1%)
    ppermute x10, starting transfers between devices, trade(): return lax.ppermute(a, MEMBER + GRID, pairs)  15.9 us
    ppermute x10, waiting for transfers between devices, trade(): return lax.ppermute(a, MEMBER + GRID, pairs)  12.1 us
    all_to_all x1, blocking collectives, body(): fields = lax.all_to_all(fields, MEMBER, 0, 0)  11 us
    all_to_all x1, blocking collectives, body(): lax.all_to_all(grads.reshape(chips, 2, VARS, LANES), ('zl', 'x'), 0, 0)  8.84 us
    ppermute x1, starting transfers between devices, body(): got = lax.ppermute(send, 'c', swap)  3.33 us
    pallas_call x1, Pallas kernels, body(): pl.pallas_call(decode_kernel, out_shape=(shape(MEMBERS, VARS, LANES), sha...  3.19 us
    pallas_call x1, Pallas kernels, body(): pl.pallas_call(lambda *refs: latent_kernel(nodes, *refs), out_shape=shape...  2.45 us
    ppermute x1, starting transfers between devices, body(): came = lax.ppermute(other, 'c', swap)  2.06 us
  transfers between devices with their start and end apart: 13, of which 9 were waited for; matrix products, arithmetic and copies ran while one was open for 0% of the time, Pallas kernels for 6%

profile of v4, /device:TPU:1, one launch (start us, length us, event | category | flops | bytes accessed | tf_op | source)
XLA Modules:
  0.0 63.2 jit_solution(14566753820711798658)
XLA Ops:
  0.7 3.2 %shard_map.93 = (f32[16,32,128]{2,1,0:T(8,128)S(1)}, f32[1024,512]{1,0:T(8,128)S(1)}, f32[1024,512]{1,0:T(8,128)S(1)}) custom-call(s32[1]{0:T(128)S(6)} %add.27.me_ref.at_ref, s32[1]{0:T(128)S(6)} %and.8.held_ref.h_ref.c_ref, s32[1]{0:T(128)} %bitcast.core_ref.c_ref.refs_0_, f32[2048,512]{1,0:T(8,128)} %bitcast.19, f32[32,512]{1,0:T(8,128)} %bitcast.13, ...), custom_call_target="tpu_custom_call" | custom-call | tf_op jit(solution)/shard_map/pallas_call | solution.py:247
  3.9 3.3 %collective-permute-start = (f32[1024,512]{1,0:T(8,128)S(1)}, f32[1024,512]{1,0:T(8,128)S(1)}, u32[]{:S(2)}, u32[]{:S(2)}) collective-permute-start(f32[1024,512]{1,0:T(8,128)S(1)} %get-tuple-element.15), channel_id=1, source_target_pairs={{0,16},{16,0},{1,17},{17,1},{2,18},{18,2},{3,19},{19,3},{4,20},{20... | collective-permute-start | bytes 6291464 | tf_op jit(solution)/shard_map/ppermute | solution.py:261
  7.2 11.0 %all_to_all.10.f_ref = f32[16,32,128]{2,1,0:T(8,128)S(1)} all-to-all(f32[16,32,128]{2,1,0:T(8,128)S(1)} %get-tuple-element.12), channel_id=1, replica_groups=mesh['zl'=2,'x'=4,'c'=2,'y'=4,'zh'=4] {'zl','x','c'}, dimensions={0} | all-to-all | bytes 524288 | tf_op jit(solution)/shard_map/all_to_all | solution.py:262
  18.2 0.8 %shard_map.94 = (f32[16,32,128]{2,1,0:T(8,128)S(1)}, f32[8,128]{1,0:T(8,128)S(1)}) custom-call(s32[1]{0:T(128)S(6)} %add.27.me_ref.at_ref, f32[16,32,128]{2,1,0:T(8,128)S(1)} %all_to_all.10.f_ref, f32[32,2048]{1,0:T(8,128)S(1)} %copy-done.1, f32[16,128]{1,0:T(8,128)S(1)} %bitcast.16, f32[1,32]{1,0:T(1,128)S(1)} %bitcast.17), custom_call_target="tpu_custom_call" | custom-call | tf_op jit(solution)/shard_map/pallas_call | solution.py:264
  19.0 8.8 %all_to_all.11.g_ref.refs_1_ = f32[8,2,32,128]{3,2,1,0:T(8,128)S(1)} all-to-all(f32[8,2,32,128]{3,2,1,0:T(8,128)S(1)} %bitcast.15), channel_id=1, replica_groups=mesh['zl'=2,'x'=4,'c'=2,'y'=4,'zh'=4] {'zl','x'}, dimensions={0} | all-to-all | bytes 524288 | tf_op jit(solution)/shard_map/all_to_all | solution.py:281
  27.9 0.6 shard_map.96
  28.4 0.0 copy-start
  28.4 2.1 %collective-permute-start.1 = (f32[328,128]{1,0:T(8,128)S(1)}, f32[328,128]{1,0:T(8,128)S(1)}, u32[]{:S(2)}, u32[]{:S(2)}) collective-permute-start(f32[328,128]{1,0:T(8,128)S(1)} %shard_map.96), channel_id=1, source_target_pairs={{0,16},{16,0},{1,17},{17,1},{2,18},{18,2},{3,19},{19,3},{4,20},{20... | collective-permute-start | bytes 503816 | tf_op jit(solution)/shard_map/ppermute | solution.py:294
  30.5 0.5 shard_map.95.a_ref
  31.0 0.5 collective-permute-done.1.b_ref.refs_2_
  31.5 0.9 %collective-permute-start.4 = (f32[72,128]{1,0:T(8,128)S(1)}, f32[72,128]{1,0:T(8,128)S(1)}, u32[]{:S(2)}, u32[]{:S(2)}) collective-permute-start(f32[72,128]{1,0:T(8,128)S(1)} %shard_map.97.a_ref), channel_id=1, source_target_pairs={{0,36},{1,37},{2,38},{3,39},{4,32},{5,33},{6,34},{7,35},{8,44},{9,... | collective-permute-start | bytes 110600 | tf_op jit(solution)/shard_map/ppermute | solution.py:213
  32.5 0.7 %collective-permute-start.3 = (f32[72,128]{1,0:T(8,128)S(1)}, f32[72,128]{1,0:T(8,128)S(1)}, u32[]{:S(2)}, u32[]{:S(2)}) collective-permute-start(f32[72,128]{1,0:T(8,128)S(1)} %shard_map.97.a_ref), channel_id=1, source_target_pairs={{0,20},{1,21},{2,22},{3,23},{4,16},{5,17},{6,18},{7,19},{8,28},{9,... | collective-permute-start | bytes 110600 | tf_op jit(solution)/shard_map/ppermute | solution.py:213
  33.2 1.4 %collective-permute-start.2 = (f32[72,128]{1,0:T(8,128)S(1)}, f32[72,128]{1,0:T(8,128)S(1)}, u32[]{:S(2)}, u32[]{:S(2)}) collective-permute-start(f32[72,128]{1,0:T(8,128)S(1)} %shard_map.97.a_ref), channel_id=1, source_target_pairs={{0,48},{1,49},{2,50},{3,51},{4,52},{5,53},{6,54},{7,55},{8,56},{9,... | collective-permute-start | bytes 110600 | tf_op jit(solution)/shard_map/ppermute | solution.py:213
  34.5 0.7 %collective-permute-done.4.d_ref = f32[72,128]{1,0:T(8,128)S(1)} collective-permute-done((f32[72,128]{1,0:T(8,128)S(1)}, f32[72,128]{1,0:T(8,128)S(1)}, u32[]{:S(2)}, u32[]{:S(2)}) %collective-permute-start.4) | collective-permute-done | bytes 36896 | tf_op jit(solution)/shard_map/ppermute | solution.py:213
  35.2 1.6 %collective-permute-done.3.c_ref = f32[72,128]{1,0:T(8,128)S(1)} collective-permute-done((f32[72,128]{1,0:T(8,128)S(1)}, f32[72,128]{1,0:T(8,128)S(1)}, u32[]{:S(2)}, u32[]{:S(2)}) %collective-permute-start.3) | collective-permute-done | bytes 36896 | tf_op jit(solution)/shard_map/ppermute | solution.py:213
  36.9 3.2 %collective-permute-start.7 = (f32[72,128]{1,0:T(8,128)S(1)}, f32[72,128]{1,0:T(8,128)S(1)}, u32[]{:S(2)}, u32[]{:S(2)}) collective-permute-start(f32[72,128]{1,0:T(8,128)S(1)} %shard_map.98.a_ref), channel_id=1, source_target_pairs={{0,108},{1,109},{2,110},{3,111},{4,104},{5,105},{6,106},{7,107},{8... | collective-permute-start | bytes 110600 | tf_op jit(solution)/shard_map/ppermute | solution.py:213
  40.1 0.6 collective-permute-start.6
  40.7 1.6 %collective-permute-start.5 = (f32[72,128]{1,0:T(8,128)S(1)}, f32[72,128]{1,0:T(8,128)S(1)}, u32[]{:S(2)}, u32[]{:S(2)}) collective-permute-start(f32[72,128]{1,0:T(8,128)S(1)} %shard_map.98.a_ref), channel_id=1, source_target_pairs={{0,112},{1,113},{2,114},{3,115},{4,116},{5,117},{6,118},{7,119},{8... | collective-permute-start | bytes 110600 | tf_op jit(solution)/shard_map/ppermute | solution.py:213
  42.4 0.7 %collective-permute-done.7.d_ref = f32[72,128]{1,0:T(8,128)S(1)} collective-permute-done((f32[72,128]{1,0:T(8,128)S(1)}, f32[72,128]{1,0:T(8,128)S(1)}, u32[]{:S(2)}, u32[]{:S(2)}) %collective-permute-start.7) | collective-permute-done | bytes 36896 | tf_op jit(solution)/shard_map/ppermute | solution.py:213
  43.1 1.7 %collective-permute-done.6.c_ref = f32[72,128]{1,0:T(8,128)S(1)} collective-permute-done((f32[72,128]{1,0:T(8,128)S(1)}, f32[72,128]{1,0:T(8,128)S(1)}, u32[]{:S(2)}, u32[]{:S(2)}) %collective-permute-start.6) | collective-permute-done | bytes 36896 | tf_op jit(solution)/shard_map/ppermute | solution.py:213
  44.8 0.6 collective-permute-done.5.b_ref
  45.4 3.5 %collective-permute-start.10 = (f32[72,128]{1,0:T(8,128)S(1)}, f32[72,128]{1,0:T(8,128)S(1)}, u32[]{:S(2)}, u32[]{:S(2)}) collective-permute-start(f32[72,128]{1,0:T(8,128)S(1)} %shard_map.99.a_ref), channel_id=1, source_target_pairs={{0,129},{1,128},{2,131},{3,130},{4,133},{5,132},{6,135},{7,134},{8... | collective-permute-start | bytes 110600 | tf_op jit(solution)/shard_map/ppermute | solution.py:213
  48.8 0.0 collective-permute-start.9
  48.8 0.7 %collective-permute-start.8 = (f32[72,128]{1,0:T(8,128)S(1)}, f32[72,128]{1,0:T(8,128)S(1)}, u32[]{:S(2)}, u32[]{:S(2)}) collective-permute-start(f32[72,128]{1,0:T(8,128)S(1)} %shard_map.99.a_ref), channel_id=1, source_target_pairs={{0,144},{1,145},{2,146},{3,147},{4,148},{5,149},{6,150},{7,151},{8... | collective-permute-start | bytes 110600 | tf_op jit(solution)/shard_map/ppermute | solution.py:213
  49.5 0.8 %collective-permute-done.10.d_ref = f32[72,128]{1,0:T(8,128)S(1)} collective-permute-done((f32[72,128]{1,0:T(8,128)S(1)}, f32[72,128]{1,0:T(8,128)S(1)}, u32[]{:S(2)}, u32[]{:S(2)}) %collective-permute-start.10) | collective-permute-done | bytes 36896 | tf_op jit(solution)/shard_map/ppermute | solution.py:213
  50.3 3.5 %collective-permute-done.9.c_ref = f32[72,128]{1,0:T(8,128)S(1)} collective-permute-done((f32[72,128]{1,0:T(8,128)S(1)}, f32[72,128]{1,0:T(8,128)S(1)}, u32[]{:S(2)}, u32[]{:S(2)}) %collective-permute-start.9) | collective-permute-done | bytes 36896 | tf_op jit(solution)/shard_map/ppermute | solution.py:213
  53.8 3.3 %collective-permute-start.11 = (f32[72,128]{1,0:T(8,128)S(1)}, f32[72,128]{1,0:T(8,128)S(1)}, u32[]{:S(2)}, u32[]{:S(2)}) collective-permute-start(f32[72,128]{1,0:T(8,128)S(1)} %shard_map.100.a_ref), channel_id=1, source_target_pairs={{0,19},{1,18},{2,17},{3,16},{4,23},{5,22},{6,21},{7,20},{8,27},{9,... | collective-permute-start | bytes 110600 | tf_op jit(solution)/shard_map/ppermute | solution.py:213
  57.1 2.5 %collective-permute-done.11.b_ref = f32[72,128]{1,0:T(8,128)S(1)} collective-permute-done((f32[72,128]{1,0:T(8,128)S(1)}, f32[72,128]{1,0:T(8,128)S(1)}, u32[]{:S(2)}, u32[]{:S(2)}) %collective-permute-start.11) | collective-permute-done | bytes 36896 | tf_op jit(solution)/shard_map/ppermute | solution.py:213
  59.6 0.4 collective-permute-start.12
  60.0 2.5 %shard_map.103 = f32[2048,512]{1,0:T(8,128)} custom-call(s32[1]{0:T(128)} %bitcast.core_ref.c_ref.refs_0_, f32[8,2,32,128]{3,2,1,0:T(8,128)S(1)} %all_to_all.11.g_ref.refs_1_, f32[328,128]{1,0:T(8,128)S(1)} %collective-permute-done.1.b_ref.refs_2_, f32[32,512]{1,0:T(8,128)S(1)} %bitcast.14, f32[72,128]{1,0:T(8,128)S(1)} %shard_map.101.mine_ref.refs_4_), custom_call_target="tpu_custom_call" | custom-call | flops 201326592 | bytes 4194304 | tf_op jit(solution)/shard_map/pallas_call | solution.py:303
  62.4 0.0 collective-permute-done.12.theirs_ref
  62.4 0.7 %shard_map.102 = (f32[32,512]{1,0:T(8,128)}, f32[1,1]{1,0:T(1,128)}, f32[1,32]{1,0:T(1,128)}) custom-call(s32[1]{0:T(128)S(6)} %and.8.held_ref.h_ref.c_ref, f32[72,128]{1,0:T(8,128)S(1)} %shard_map.101.mine_ref.refs_4_, f32[72,128]{1,0:T(8,128)S(1)} %collective-permute-done.12.theirs_ref), custom_call_target="tpu_custom_call" | custom-call | tf_op jit(solution)/shard_map/pallas_call | solution.py:313
  (15 shorter events, 0.1 us)
Async XLA Ops:
  0.6 17.6 %copy-start.1 = (f32[32,2048]{1,0:T(8,128)S(1)}, f32[32,2048]{1,0:T(8,128)}, u32[]{:S(2)}) copy-start(f32[32,2048]{1,0:T(8,128)} %t_ref.1) | copy-start | bytes 786436
  0.7 17.5 %copy-start.2 = (f32[2048]{0:T(1024)S(1)}, f32[2048]{0:T(1024)}, u32[]{:S(2)}) copy-start(f32[2048]{0:T(1024)} %param.10) | copy-start | bytes 24580
  0.7 17.5 %copy-start.3 = (f32[32]{0:T(128)S(1)}, f32[32]{0:T(128)}, u32[]{:S(2)}) copy-start(f32[32]{0:T(128)} %param.11) | copy-start | bytes 388
  3.9 24.0 %collective-permute-start = (f32[1024,512]{1,0:T(8,128)S(1)}, f32[1024,512]{1,0:T(8,128)S(1)}, u32[]{:S(2)}, u32[]{:S(2)}) collective-permute-start(f32[1024,512]{1,0:T(8,128)S(1)} %get-tuple-element.15), channel_id=1, source_target_pairs={{0,16},{16,0},{1,17},{17,1},{2,18},{18,2},{3,19},{19,3},{4,20},{20... | collective-permute-start | bytes 6291464 | tf_op jit(solution)/shard_map/ppermute | solution.py:261
  28.4 31.5 %copy-start = (f32[512,32]{0,1:T(8,128)S(1)}, f32[512,32]{0,1:T(8,128)}, u32[]{:S(2)}) copy-start(f32[512,32]{0,1:T(8,128)} %param.7) | copy-start | bytes 196612
  28.4 3.1 %collective-permute-start.1 = (f32[328,128]{1,0:T(8,128)S(1)}, f32[328,128]{1,0:T(8,128)S(1)}, u32[]{:S(2)}, u32[]{:S(2)}) collective-permute-start(f32[328,128]{1,0:T(8,128)S(1)} %shard_map.96), channel_id=1, source_target_pairs={{0,16},{16,0},{1,17},{17,1},{2,18},{18,2},{3,19},{19,3},{4,20},{20... | collective-permute-start | bytes 503816 | tf_op jit(solution)/shard_map/ppermute | solution.py:294
  31.5 3.7 %collective-permute-start.4 = (f32[72,128]{1,0:T(8,128)S(1)}, f32[72,128]{1,0:T(8,128)S(1)}, u32[]{:S(2)}, u32[]{:S(2)}) collective-permute-start(f32[72,128]{1,0:T(8,128)S(1)} %shard_map.97.a_ref), channel_id=1, source_target_pairs={{0,36},{1,37},{2,38},{3,39},{4,32},{5,33},{6,34},{7,35},{8,44},{9,... | collective-permute-start | bytes 110600 | tf_op jit(solution)/shard_map/ppermute | solution.py:213
  32.5 4.4 %collective-permute-start.3 = (f32[72,128]{1,0:T(8,128)S(1)}, f32[72,128]{1,0:T(8,128)S(1)}, u32[]{:S(2)}, u32[]{:S(2)}) collective-permute-start(f32[72,128]{1,0:T(8,128)S(1)} %shard_map.97.a_ref), channel_id=1, source_target_pairs={{0,20},{1,21},{2,22},{3,23},{4,16},{5,17},{6,18},{7,19},{8,28},{9,... | collective-permute-start | bytes 110600 | tf_op jit(solution)/shard_map/ppermute | solution.py:213
  33.2 3.7 %collective-permute-start.2 = (f32[72,128]{1,0:T(8,128)S(1)}, f32[72,128]{1,0:T(8,128)S(1)}, u32[]{:S(2)}, u32[]{:S(2)}) collective-permute-start(f32[72,128]{1,0:T(8,128)S(1)} %shard_map.97.a_ref), channel_id=1, source_target_pairs={{0,48},{1,49},{2,50},{3,51},{4,52},{5,53},{6,54},{7,55},{8,56},{9,... | collective-permute-start | bytes 110600 | tf_op jit(solution)/shard_map/ppermute | solution.py:213
  36.9 6.2 %collective-permute-start.7 = (f32[72,128]{1,0:T(8,128)S(1)}, f32[72,128]{1,0:T(8,128)S(1)}, u32[]{:S(2)}, u32[]{:S(2)}) collective-permute-start(f32[72,128]{1,0:T(8,128)S(1)} %shard_map.98.a_ref), channel_id=1, source_target_pairs={{0,108},{1,109},{2,110},{3,111},{4,104},{5,105},{6,106},{7,107},{8... | collective-permute-start | bytes 110600 | tf_op jit(solution)/shard_map/ppermute | solution.py:213
  40.1 4.7 %collective-permute-start.6 = (f32[72,128]{1,0:T(8,128)S(1)}, f32[72,128]{1,0:T(8,128)S(1)}, u32[]{:S(2)}, u32[]{:S(2)}) collective-permute-start(f32[72,128]{1,0:T(8,128)S(1)} %shard_map.98.a_ref), channel_id=1, source_target_pairs={{0,28},{1,29},{2,30},{3,31},{4,24},{5,25},{6,26},{7,27},{8,20},{9,... | collective-permute-start | bytes 110600 | tf_op jit(solution)/shard_map/ppermute | solution.py:213
  40.7 4.6 %collective-permute-start.5 = (f32[72,128]{1,0:T(8,128)S(1)}, f32[72,128]{1,0:T(8,128)S(1)}, u32[]{:S(2)}, u32[]{:S(2)}) collective-permute-start(f32[72,128]{1,0:T(8,128)S(1)} %shard_map.98.a_ref), channel_id=1, source_target_pairs={{0,112},{1,113},{2,114},{3,115},{4,116},{5,117},{6,118},{7,119},{8... | collective-permute-start | bytes 110600 | tf_op jit(solution)/shard_map/ppermute | solution.py:213
  45.4 4.9 %collective-permute-start.10 = (f32[72,128]{1,0:T(8,128)S(1)}, f32[72,128]{1,0:T(8,128)S(1)}, u32[]{:S(2)}, u32[]{:S(2)}) collective-permute-start(f32[72,128]{1,0:T(8,128)S(1)} %shard_map.99.a_ref), channel_id=1, source_target_pairs={{0,129},{1,128},{2,131},{3,130},{4,133},{5,132},{6,135},{7,134},{8... | collective-permute-start | bytes 110600 | tf_op jit(solution)/shard_map/ppermute | solution.py:213
  48.8 5.0 %collective-permute-start.9 = (f32[72,128]{1,0:T(8,128)S(1)}, f32[72,128]{1,0:T(8,128)S(1)}, u32[]{:S(2)}, u32[]{:S(2)}) collective-permute-start(f32[72,128]{1,0:T(8,128)S(1)} %shard_map.99.a_ref), channel_id=1, source_target_pairs={{0,17},{1,16},{2,19},{3,18},{4,21},{5,20},{6,23},{7,22},{8,25},{9,... | collective-permute-start | bytes 110600 | tf_op jit(solution)/shard_map/ppermute | solution.py:213
  48.8 5.0 %collective-permute-start.8 = (f32[72,128]{1,0:T(8,128)S(1)}, f32[72,128]{1,0:T(8,128)S(1)}, u32[]{:S(2)}, u32[]{:S(2)}) collective-permute-start(f32[72,128]{1,0:T(8,128)S(1)} %shard_map.99.a_ref), channel_id=1, source_target_pairs={{0,144},{1,145},{2,146},{3,147},{4,148},{5,149},{6,150},{7,151},{8... | collective-permute-start | bytes 110600 | tf_op jit(solution)/shard_map/ppermute | solution.py:213
  53.8 5.7 %collective-permute-start.11 = (f32[72,128]{1,0:T(8,128)S(1)}, f32[72,128]{1,0:T(8,128)S(1)}, u32[]{:S(2)}, u32[]{:S(2)}) collective-permute-start(f32[72,128]{1,0:T(8,128)S(1)} %shard_map.100.a_ref), channel_id=1, source_target_pairs={{0,19},{1,18},{2,17},{3,16},{4,23},{5,22},{6,21},{7,20},{8,27},{9,... | collective-permute-start | bytes 110600 | tf_op jit(solution)/shard_map/ppermute | solution.py:213
  59.6 2.8 %collective-permute-start.12 = (f32[72,128]{1,0:T(8,128)S(1)}, f32[72,128]{1,0:T(8,128)S(1)}, u32[]{:S(2)}, u32[]{:S(2)}) collective-permute-start(f32[72,128]{1,0:T(8,128)S(1)} %shard_map.101.mine_ref.refs_4_), channel_id=1, source_target_pairs={{0,16},{16,0},{1,17},{17,1},{2,18},{18,2},{3,19},{19,3},{4,20},{20... | collective-permute-start | bytes 110600 | tf_op jit(solution)/shard_map/ppermute | solution.py:301

commit v5 on v4

--- a/solution.py
+++ b/solution.py
@@ -137,19 +137,19 @@
 
 
 def weight_other_kernel(c_ref, h_ref, g_ref, keep_ref, got_ref, e_ref, out_ref):
+    weight_columns(c_ref[0], 1 - h_ref[0], g_ref, keep_ref, got_ref, e_ref, out_ref)
+
+
+def weight_own_kernel(c_ref, h_ref, g_ref, keep_ref, got_ref, e_ref, out_ref, send_ref):
     core = c_ref[0]
-    weight_columns(core, 1 - h_ref[0], g_ref, keep_ref, got_ref, e_ref, out_ref)
+    weight_columns(core, h_ref[0], g_ref, keep_ref, got_ref, e_ref, out_ref)
     for i in range(g_ref.shape[0]):
-        out_ref[SUMS + i * VARS : SUMS + (i + 1) * VARS, :] = g_ref[i, 1 - core]
-
-
-def weight_own_kernel(c_ref, h_ref, g_ref, keep_ref, got_ref, e_ref, out_ref):
-    weight_columns(c_ref[0], h_ref[0], g_ref, keep_ref, got_ref, e_ref, out_ref)
+        send_ref[i] = g_ref[i, 1 - core]
 
 
 def pair_kernel(a_ref, b_ref, *refs):
     out_ref = refs[-1]
-    out_ref[...] = a_ref[...] + b_ref[:SUMS, :]
+    out_ref[...] = a_ref[...] + b_ref[...]
 
 
 def quad_kernel(a_ref, b_ref, c_ref, d_ref, out_ref):
@@ -169,7 +169,7 @@
             if part == 0:
                 g = [g_ref[k, core] for k in chips]
             else:
-                g = [got_ref[SUMS + k * VARS : SUMS + (k + 1) * VARS, :] for k in chips]
+                g = [got_ref[k] for k in chips]
             gh, gl = split(jnp.concatenate([a * inv for a in g], 1))
             rows = pl.ds(part * half + i * BLOCK, BLOCK)
             out_ref[rows, :] = dot(jnp.concatenate([gh, gl, gh], 0), w, (0, 0))
@@ -280,23 +280,24 @@
 
     grads = lax.all_to_all(grads.reshape(chips, 2, VARS, LANES), ("zl", "x"), 0, 0)
 
-    def weight(kernel, rows):
+    def weight(kernel, *outs):
         return pl.pallas_call(
             kernel,
-            out_shape=shape(rows, LANES),
+            out_shape=outs,
             in_specs=[SMEM, SMEM, VMEM, VMEM, VMEM, VMEM],
-            out_specs=VMEM,
+            out_specs=(VMEM,) * len(outs),
             compiler_params=params(24),
             cost_estimate=pl.CostEstimate(flops=6 * slab * VARS * HALF, bytes_accessed=4 * slab * HALF, transcendentals=0),
         )(core, held, grads, keep, got, extra)
 
-    other = weight(weight_other_kernel, SUMS + chips * VARS)
+    (other,) = weight(weight_other_kernel, shape(SUMS, LANES))
     came = lax.ppermute(other, "c", swap)
-    own = weight(weight_own_kernel, SUMS)
+    own, send = weight(weight_own_kernel, shape(SUMS, LANES), shape(chips, VARS, LANES))
+    rest = lax.ppermute(send, "c", swap)
     sums = pl.pallas_call(pair_kernel, out_shape=shape(SUMS, LANES), compiler_params=params(16))(own, came)
-    sums = add_round(sums, ("x1", "y1"))
+    sums = add_round(sums, ("x1", "zl"))
     sums = add_round(sums, ("x2", "y2"))
-    sums = add_round(sums, ("zl", "z1"))
+    sums = add_round(sums, ("y1", "z1"))
     sums = add_round(sums, ("z2",))
     theirs = lax.ppermute(sums, "c", swap)
 
@@ -308,7 +309,7 @@
         scratch_shapes=[pltpu.VMEM((slab, LATENT), F32), pltpu.SemaphoreType.DMA((steps,))],
         compiler_params=params(24),
         cost_estimate=pl.CostEstimate(flops=6 * slab * VARS * LATENT, bytes_accessed=4 * slab * LATENT, transcendentals=0),
-    )(core, grads, came, wt, sums)
+    )(core, grads, rest, wt, sums)
 
     grad_weight, loss, bias = pl.pallas_call(
         join_kernel,

time: 63.3 us -> 62.3 us (0.984)
  waiting for transfers between devices: 12.6 us -> 9.37 us
  starting transfers between devices: 21.7 us -> 23.7 us
    ppermute x10, waiting for transfers between devices: 12.1 us -> 9.05 us  [trade(): return lax.ppermute(a, MEMBER + GRID, pairs)]
    ppermute x10, starting transfers between devices: 15.9 us -> 17.5 us  [trade(): return lax.ppermute(a, MEMBER + GRID, pairs)]
  transfers between devices with their start and end apart: 13 -> 14, of which waited for: 9 -> 8; matrix products, arithmetic and copies ran while one was open for 0% -> 0% of each run, Pallas kernels for 6% -> 6%
where the time goes in v5:
time: 62.3 us; the launch traced here: 62 us
  starting transfers between devices  23.7 us (38%)
  blocking collectives  19.8 us (32%)
  waiting for transfers between devices  9.37 us (15%)
  Pallas kernels  8.34 us (13%)
  between operations  0.74 us (1%)
    ppermute x10, starting transfers between devices, trade(): return lax.ppermute(a, MEMBER + GRID, pairs)  17.5 us
    all_to_all x1, blocking collectives, body(): fields = lax.all_to_all(fields, MEMBER, 0, 0)  11 us
    ppermute x10, waiting for transfers between devices, trade(): return lax.ppermute(a, MEMBER + GRID, pairs)  9.05 us
    all_to_all x1, blocking collectives, body(): lax.all_to_all(grads.reshape(chips, 2, VARS, LANES), ('zl', 'x'), 0, 0)  8.84 us
    ppermute x1, starting transfers between devices, body(): got = lax.ppermute(send, 'c', swap)  3.33 us
    pallas_call x1, Pallas kernels, body(): pl.pallas_call(decode_kernel, out_shape=(shape(MEMBERS, VARS, LANES), sha...  3.19 us
    pallas_call x1, Pallas kernels, body(): pl.pallas_call(lambda *refs: latent_kernel(nodes, *refs), out_shape=shape...  2.46 us
    ppermute x1, starting transfers between devices, body(): came = lax.ppermute(other, 'c', swap)  2.05 us
  transfers between devices with their start and end apart: 14, of which 8 were waited for; matrix products, arithmetic and copies ran while one was open for 0% of the time, Pallas kernels for 6%

profile of v5, /device:TPU:1, one launch (start us, length us, event | category | flops | bytes accessed | tf_op | source)
XLA Modules:
  0.0 62.0 jit_solution(954974095447626152)
XLA Ops:
  0.7 3.2 %shard_map.93 = (f32[16,32,128]{2,1,0:T(8,128)S(1)}, f32[1024,512]{1,0:T(8,128)S(1)}, f32[1024,512]{1,0:T(8,128)S(1)}) custom-call(s32[1]{0:T(128)S(6)} %add.27.me_ref.at_ref, s32[1]{0:T(128)S(6)} %and.8.held_ref.h_ref.c_ref, s32[1]{0:T(128)} %bitcast.core_ref.c_ref.refs_0_, f32[2048,512]{1,0:T(8,128)} %bitcast.18, f32[32,512]{1,0:T(8,128)} %bitcast.13, ...), custom_call_target="tpu_custom_call" | custom-call | tf_op jit(solution)/shard_map/pallas_call | solution.py:247
  3.9 3.3 %collective-permute-start = (f32[1024,512]{1,0:T(8,128)S(1)}, f32[1024,512]{1,0:T(8,128)S(1)}, u32[]{:S(2)}, u32[]{:S(2)}) collective-permute-start(f32[1024,512]{1,0:T(8,128)S(1)} %get-tuple-element.17), channel_id=1, source_target_pairs={{0,16},{16,0},{1,17},{17,1},{2,18},{18,2},{3,19},{19,3},{4,20},{20... | collective-permute-start | bytes 6291464 | tf_op jit(solution)/shard_map/ppermute | solution.py:261
  7.2 11.0 %all_to_all.10.f_ref = f32[16,32,128]{2,1,0:T(8,128)S(1)} all-to-all(f32[16,32,128]{2,1,0:T(8,128)S(1)} %get-tuple-element.14), channel_id=1, replica_groups=mesh['zl'=2,'x'=4,'c'=2,'y'=4,'zh'=4] {'zl','x','c'}, dimensions={0} | all-to-all | bytes 524288 | tf_op jit(solution)/shard_map/all_to_all | solution.py:262
  18.2 0.8 %shard_map.94 = (f32[16,32,128]{2,1,0:T(8,128)S(1)}, f32[8,128]{1,0:T(8,128)S(1)}) custom-call(s32[1]{0:T(128)S(6)} %add.27.me_ref.at_ref, f32[16,32,128]{2,1,0:T(8,128)S(1)} %all_to_all.10.f_ref, f32[32,2048]{1,0:T(8,128)S(1)} %copy-done.1, f32[16,128]{1,0:T(8,128)S(1)} %bitcast.16, f32[1,32]{1,0:T(1,128)S(1)} %bitcast.17), custom_call_target="tpu_custom_call" | custom-call | tf_op jit(solution)/shard_map/pallas_call | solution.py:264
  19.0 8.8 %all_to_all.11.g_ref.refs_1_ = f32[8,2,32,128]{3,2,1,0:T(8,128)S(1)} all-to-all(f32[8,2,32,128]{3,2,1,0:T(8,128)S(1)} %bitcast.15), channel_id=1, replica_groups=mesh['zl'=2,'x'=4,'c'=2,'y'=4,'zh'=4] {'zl','x'}, dimensions={0} | all-to-all | bytes 524288 | tf_op jit(solution)/shard_map/all_to_all | solution.py:281
  27.9 0.6 shard_map.96
  28.4 0.0 copy-start
  28.4 2.1 %collective-permute-start.1 = (f32[72,128]{1,0:T(8,128)S(1)}, f32[72,128]{1,0:T(8,128)S(1)}, u32[]{:S(2)}, u32[]{:S(2)}) collective-permute-start(f32[72,128]{1,0:T(8,128)S(1)} %shard_map.96), channel_id=1, source_target_pairs={{0,16},{16,0},{1,17},{17,1},{2,18},{18,2},{3,19},{19,3},{4,20},{20... | collective-permute-start | bytes 110600 | tf_op jit(solution)/shard_map/ppermute | solution.py:294
  30.5 0.6 shard_map.95
  31.0 0.3 collective-permute-done.1.b_ref
  31.4 0.6 %collective-permute-start.4 = (f32[72,128]{1,0:T(8,128)S(1)}, f32[72,128]{1,0:T(8,128)S(1)}, u32[]{:S(2)}, u32[]{:S(2)}) collective-permute-start(f32[72,128]{1,0:T(8,128)S(1)} %shard_map.97.a_ref), channel_id=1, source_target_pairs={{0,160},{1,161},{2,162},{3,163},{4,164},{5,165},{6,166},{7,167},{8... | collective-permute-start | bytes 110600 | tf_op jit(solution)/shard_map/ppermute | solution.py:213
  32.0 1.0 %collective-permute-start.3 = (f32[72,128]{1,0:T(8,128)S(1)}, f32[72,128]{1,0:T(8,128)S(1)}, u32[]{:S(2)}, u32[]{:S(2)}) collective-permute-start(f32[72,128]{1,0:T(8,128)S(1)} %shard_map.97.a_ref), channel_id=1, source_target_pairs={{0,144},{1,145},{2,146},{3,147},{4,148},{5,149},{6,150},{7,151},{8... | collective-permute-start | bytes 110600 | tf_op jit(solution)/shard_map/ppermute | solution.py:213
  33.0 1.3 %collective-permute-start.2 = (f32[72,128]{1,0:T(8,128)S(1)}, f32[72,128]{1,0:T(8,128)S(1)}, u32[]{:S(2)}, u32[]{:S(2)}) collective-permute-start(f32[72,128]{1,0:T(8,128)S(1)} %shard_map.97.a_ref), channel_id=1, source_target_pairs={{0,48},{1,49},{2,50},{3,51},{4,52},{5,53},{6,54},{7,55},{8,56},{9,... | collective-permute-start | bytes 110600 | tf_op jit(solution)/shard_map/ppermute | solution.py:213
  34.3 0.6 %collective-permute-start.13 = (f32[8,32,128]{2,1,0:T(8,128)S(1)}, f32[8,32,128]{2,1,0:T(8,128)S(1)}, u32[]{:S(2)}, u32[]{:S(2)}) collective-permute-start(f32[8,32,128]{2,1,0:T(8,128)S(1)} %get-tuple-element.21), channel_id=1, source_target_pairs={{0,16},{16,0},{1,17},{17,1},{2,18},{18,2},{3,19},{19,3},{4,20},{20... | collective-permute-start | bytes 393224 | tf_op jit(solution)/shard_map/ppermute | solution.py:296
  34.9 0.1 collective-permute-done.4.d_ref
  35.1 0.9 %collective-permute-done.3.c_ref = f32[72,128]{1,0:T(8,128)S(1)} collective-permute-done((f32[72,128]{1,0:T(8,128)S(1)}, f32[72,128]{1,0:T(8,128)S(1)}, u32[]{:S(2)}, u32[]{:S(2)}) %collective-permute-start.3) | collective-permute-done | bytes 36896 | tf_op jit(solution)/shard_map/ppermute | solution.py:213
  36.0 0.7 %collective-permute-done.2.b_ref = f32[72,128]{1,0:T(8,128)S(1)} collective-permute-done((f32[72,128]{1,0:T(8,128)S(1)}, f32[72,128]{1,0:T(8,128)S(1)}, u32[]{:S(2)}, u32[]{:S(2)}) %collective-permute-start.2) | collective-permute-done | bytes 36896 | tf_op jit(solution)/shard_map/ppermute | solution.py:213
  36.7 3.2 %collective-permute-start.7 = (f32[72,128]{1,0:T(8,128)S(1)}, f32[72,128]{1,0:T(8,128)S(1)}, u32[]{:S(2)}, u32[]{:S(2)}) collective-permute-start(f32[72,128]{1,0:T(8,128)S(1)} %shard_map.98.a_ref), channel_id=1, source_target_pairs={{0,108},{1,109},{2,110},{3,111},{4,104},{5,105},{6,106},{7,107},{8... | collective-permute-start | bytes 110600 | tf_op jit(solution)/shard_map/ppermute | solution.py:213
  39.9 0.3 collective-permute-start.6
  40.2 2.3 %collective-permute-start.5 = (f32[72,128]{1,0:T(8,128)S(1)}, f32[72,128]{1,0:T(8,128)S(1)}, u32[]{:S(2)}, u32[]{:S(2)}) collective-permute-start(f32[72,128]{1,0:T(8,128)S(1)} %shard_map.98.a_ref), channel_id=1, source_target_pairs={{0,112},{1,113},{2,114},{3,115},{4,116},{5,117},{6,118},{7,119},{8... | collective-permute-start | bytes 110600 | tf_op jit(solution)/shard_map/ppermute | solution.py:213
  42.5 0.4 collective-permute-done.7.d_ref
  43.0 2.0 %collective-permute-done.6.c_ref = f32[72,128]{1,0:T(8,128)S(1)} collective-permute-done((f32[72,128]{1,0:T(8,128)S(1)}, f32[72,128]{1,0:T(8,128)S(1)}, u32[]{:S(2)}, u32[]{:S(2)}) %collective-permute-start.6) | collective-permute-done | bytes 36896 | tf_op jit(solution)/shard_map/ppermute | solution.py:213
  45.0 2.7 %collective-permute-start.10 = (f32[72,128]{1,0:T(8,128)S(1)}, f32[72,128]{1,0:T(8,128)S(1)}, u32[]{:S(2)}, u32[]{:S(2)}) collective-permute-start(f32[72,128]{1,0:T(8,128)S(1)} %shard_map.99.a_ref), channel_id=1, source_target_pairs={{0,5},{1,4},{2,7},{3,6},{4,1},{5,0},{6,3},{7,2},{8,13},{9,12},{10,... | collective-permute-start | bytes 110600 | tf_op jit(solution)/shard_map/ppermute | solution.py:213
  47.7 0.7 %collective-permute-start.9 = (f32[72,128]{1,0:T(8,128)S(1)}, f32[72,128]{1,0:T(8,128)S(1)}, u32[]{:S(2)}, u32[]{:S(2)}) collective-permute-start(f32[72,128]{1,0:T(8,128)S(1)} %shard_map.99.a_ref), channel_id=1, source_target_pairs={{0,17},{1,16},{2,19},{3,18},{4,21},{5,20},{6,23},{7,22},{8,25},{9,... | collective-permute-start | bytes 110600 | tf_op jit(solution)/shard_map/ppermute | solution.py:213
  48.4 1.4 %collective-permute-start.8 = (f32[72,128]{1,0:T(8,128)S(1)}, f32[72,128]{1,0:T(8,128)S(1)}, u32[]{:S(2)}, u32[]{:S(2)}) collective-permute-start(f32[72,128]{1,0:T(8,128)S(1)} %shard_map.99.a_ref), channel_id=1, source_target_pairs={{0,20},{1,21},{2,22},{3,23},{4,16},{5,17},{6,18},{7,19},{8,28},{9,... | collective-permute-start | bytes 110600 | tf_op jit(solution)/shard_map/ppermute | solution.py:213
  49.8 3.2 %collective-permute-done.9.c_ref = f32[72,128]{1,0:T(8,128)S(1)} collective-permute-done((f32[72,128]{1,0:T(8,128)S(1)}, f32[72,128]{1,0:T(8,128)S(1)}, u32[]{:S(2)}, u32[]{:S(2)}) %collective-permute-start.9) | collective-permute-done | bytes 36896 | tf_op jit(solution)/shard_map/ppermute | solution.py:213
  53.0 0.0 collective-permute-done.8.b_ref
  53.0 4.0 %collective-permute-start.11 = (f32[72,128]{1,0:T(8,128)S(1)}, f32[72,128]{1,0:T(8,128)S(1)}, u32[]{:S(2)}, u32[]{:S(2)}) collective-permute-start(f32[72,128]{1,0:T(8,128)S(1)} %shard_map.100.a_ref), channel_id=1, source_target_pairs={{0,19},{1,18},{2,17},{3,16},{4,23},{5,22},{6,21},{7,20},{8,27},{9,... | collective-permute-start | bytes 110600 | tf_op jit(solution)/shard_map/ppermute | solution.py:213
  57.0 1.6 %collective-permute-done.11.b_ref = f32[72,128]{1,0:T(8,128)S(1)} collective-permute-done((f32[72,128]{1,0:T(8,128)S(1)}, f32[72,128]{1,0:T(8,128)S(1)}, u32[]{:S(2)}, u32[]{:S(2)}) %collective-permute-start.11) | collective-permute-done | bytes 36896 | tf_op jit(solution)/shard_map/ppermute | solution.py:213
  58.6 0.1 collective-permute-start.12
  58.8 2.5 %shard_map.103 = f32[2048,512]{1,0:T(8,128)} custom-call(s32[1]{0:T(128)} %bitcast.core_ref.c_ref.refs_0_, f32[8,2,32,128]{3,2,1,0:T(8,128)S(1)} %all_to_all.11.g_ref.refs_1_, f32[8,32,128]{2,1,0:T(8,128)S(1)} %collective-permute-done.13.refs_2_, f32[32,512]{1,0:T(8,128)S(1)} %bitcast.14, f32[72,128]{1,0:T(8,128)S(1)} %shard_map.101.mine_ref.refs_4_), custom_call_target="tpu_custom_call" | custom-call | flops 201326592 | bytes 4194304 | tf_op jit(solution)/shard_map/pallas_call | solution.py:304
  61.3 0.7 %shard_map.102 = (f32[32,512]{1,0:T(8,128)}, f32[1,1]{1,0:T(1,128)}, f32[1,32]{1,0:T(1,128)}) custom-call(s32[1]{0:T(128)S(6)} %and.8.held_ref.h_ref.c_ref, f32[72,128]{1,0:T(8,128)S(1)} %shard_map.101.mine_ref.refs_4_, f32[72,128]{1,0:T(8,128)S(1)} %collective-permute-done.12.theirs_ref), custom_call_target="tpu_custom_call" | custom-call | tf_op jit(solution)/shard_map/pallas_call | solution.py:314
  (17 shorter events, 0.1 us)
Async XLA Ops:
  0.6 17.6 %copy-start.1 = (f32[32,2048]{1,0:T(8,128)S(1)}, f32[32,2048]{1,0:T(8,128)}, u32[]{:S(2)}) copy-start(f32[32,2048]{1,0:T(8,128)} %t_ref.1) | copy-start | bytes 786436
  0.7 17.5 %copy-start.2 = (f32[2048]{0:T(1024)S(1)}, f32[2048]{0:T(1024)}, u32[]{:S(2)}) copy-start(f32[2048]{0:T(1024)} %param.10) | copy-start | bytes 24580
  0.7 17.5 %copy-start.3 = (f32[32]{0:T(128)S(1)}, f32[32]{0:T(128)}, u32[]{:S(2)}) copy-start(f32[32]{0:T(128)} %param.11) | copy-start | bytes 388
  3.9 24.0 %collective-permute-start = (f32[1024,512]{1,0:T(8,128)S(1)}, f32[1024,512]{1,0:T(8,128)S(1)}, u32[]{:S(2)}, u32[]{:S(2)}) collective-permute-start(f32[1024,512]{1,0:T(8,128)S(1)} %get-tuple-element.17), channel_id=1, source_target_pairs={{0,16},{16,0},{1,17},{17,1},{2,18},{18,2},{3,19},{19,3},{4,20},{20... | collective-permute-start | bytes 6291464 | tf_op jit(solution)/shard_map/ppermute | solution.py:261
  28.4 30.4 %copy-start = (f32[512,32]{0,1:T(8,128)S(1)}, f32[512,32]{0,1:T(8,128)}, u32[]{:S(2)}) copy-start(f32[512,32]{0,1:T(8,128)} %param.7) | copy-start | bytes 196612
  28.4 2.9 %collective-permute-start.1 = (f32[72,128]{1,0:T(8,128)S(1)}, f32[72,128]{1,0:T(8,128)S(1)}, u32[]{:S(2)}, u32[]{:S(2)}) collective-permute-start(f32[72,128]{1,0:T(8,128)S(1)} %shard_map.96), channel_id=1, source_target_pairs={{0,16},{16,0},{1,17},{17,1},{2,18},{18,2},{3,19},{19,3},{4,20},{20... | collective-permute-start | bytes 110600 | tf_op jit(solution)/shard_map/ppermute | solution.py:294
  31.4 3.7 %collective-permute-start.4 = (f32[72,128]{1,0:T(8,128)S(1)}, f32[72,128]{1,0:T(8,128)S(1)}, u32[]{:S(2)}, u32[]{:S(2)}) collective-permute-start(f32[72,128]{1,0:T(8,128)S(1)} %shard_map.97.a_ref), channel_id=1, source_target_pairs={{0,160},{1,161},{2,162},{3,163},{4,164},{5,165},{6,166},{7,167},{8... | collective-permute-start | bytes 110600 | tf_op jit(solution)/shard_map/ppermute | solution.py:213
  32.0 4.0 %collective-permute-start.3 = (f32[72,128]{1,0:T(8,128)S(1)}, f32[72,128]{1,0:T(8,128)S(1)}, u32[]{:S(2)}, u32[]{:S(2)}) collective-permute-start(f32[72,128]{1,0:T(8,128)S(1)} %shard_map.97.a_ref), channel_id=1, source_target_pairs={{0,144},{1,145},{2,146},{3,147},{4,148},{5,149},{6,150},{7,151},{8... | collective-permute-start | bytes 110600 | tf_op jit(solution)/shard_map/ppermute | solution.py:213
  33.0 3.7 %collective-permute-start.2 = (f32[72,128]{1,0:T(8,128)S(1)}, f32[72,128]{1,0:T(8,128)S(1)}, u32[]{:S(2)}, u32[]{:S(2)}) collective-permute-start(f32[72,128]{1,0:T(8,128)S(1)} %shard_map.97.a_ref), channel_id=1, source_target_pairs={{0,48},{1,49},{2,50},{3,51},{4,52},{5,53},{6,54},{7,55},{8,56},{9,... | collective-permute-start | bytes 110600 | tf_op jit(solution)/shard_map/ppermute | solution.py:213
  34.3 24.5 %collective-permute-start.13 = (f32[8,32,128]{2,1,0:T(8,128)S(1)}, f32[8,32,128]{2,1,0:T(8,128)S(1)}, u32[]{:S(2)}, u32[]{:S(2)}) collective-permute-start(f32[8,32,128]{2,1,0:T(8,128)S(1)} %get-tuple-element.21), channel_id=1, source_target_pairs={{0,16},{16,0},{1,17},{17,1},{2,18},{18,2},{3,19},{19,3},{4,20},{20... | collective-permute-start | bytes 393224 | tf_op jit(solution)/shard_map/ppermute | solution.py:296
  36.7 6.2 %collective-permute-start.7 = (f32[72,128]{1,0:T(8,128)S(1)}, f32[72,128]{1,0:T(8,128)S(1)}, u32[]{:S(2)}, u32[]{:S(2)}) collective-permute-start(f32[72,128]{1,0:T(8,128)S(1)} %shard_map.98.a_ref), channel_id=1, source_target_pairs={{0,108},{1,109},{2,110},{3,111},{4,104},{5,105},{6,106},{7,107},{8... | collective-permute-start | bytes 110600 | tf_op jit(solution)/shard_map/ppermute | solution.py:213
  39.9 5.0 %collective-permute-start.6 = (f32[72,128]{1,0:T(8,128)S(1)}, f32[72,128]{1,0:T(8,128)S(1)}, u32[]{:S(2)}, u32[]{:S(2)}) collective-permute-start(f32[72,128]{1,0:T(8,128)S(1)} %shard_map.98.a_ref), channel_id=1, source_target_pairs={{0,28},{1,29},{2,30},{3,31},{4,24},{5,25},{6,26},{7,27},{8,20},{9,... | collective-permute-start | bytes 110600 | tf_op jit(solution)/shard_map/ppermute | solution.py:213
  40.2 4.8 %collective-permute-start.5 = (f32[72,128]{1,0:T(8,128)S(1)}, f32[72,128]{1,0:T(8,128)S(1)}, u32[]{:S(2)}, u32[]{:S(2)}) collective-permute-start(f32[72,128]{1,0:T(8,128)S(1)} %shard_map.98.a_ref), channel_id=1, source_target_pairs={{0,112},{1,113},{2,114},{3,115},{4,116},{5,117},{6,118},{7,119},{8... | collective-permute-start | bytes 110600 | tf_op jit(solution)/shard_map/ppermute | solution.py:213
  45.0 4.8 %collective-permute-start.10 = (f32[72,128]{1,0:T(8,128)S(1)}, f32[72,128]{1,0:T(8,128)S(1)}, u32[]{:S(2)}, u32[]{:S(2)}) collective-permute-start(f32[72,128]{1,0:T(8,128)S(1)} %shard_map.99.a_ref), channel_id=1, source_target_pairs={{0,5},{1,4},{2,7},{3,6},{4,1},{5,0},{6,3},{7,2},{8,13},{9,12},{10,... | collective-permute-start | bytes 110600 | tf_op jit(solution)/shard_map/ppermute | solution.py:213
  47.7 5.3 %collective-permute-start.9 = (f32[72,128]{1,0:T(8,128)S(1)}, f32[72,128]{1,0:T(8,128)S(1)}, u32[]{:S(2)}, u32[]{:S(2)}) collective-permute-start(f32[72,128]{1,0:T(8,128)S(1)} %shard_map.99.a_ref), channel_id=1, source_target_pairs={{0,17},{1,16},{2,19},{3,18},{4,21},{5,20},{6,23},{7,22},{8,25},{9,... | collective-permute-start | bytes 110600 | tf_op jit(solution)/shard_map/ppermute | solution.py:213
  48.4 4.5 %collective-permute-start.8 = (f32[72,128]{1,0:T(8,128)S(1)}, f32[72,128]{1,0:T(8,128)S(1)}, u32[]{:S(2)}, u32[]{:S(2)}) collective-permute-start(f32[72,128]{1,0:T(8,128)S(1)} %shard_map.99.a_ref), channel_id=1, source_target_pairs={{0,20},{1,21},{2,22},{3,23},{4,16},{5,17},{6,18},{7,19},{8,28},{9,... | collective-permute-start | bytes 110600 | tf_op jit(solution)/shard_map/ppermute | solution.py:213
  53.0 5.6 %collective-permute-start.11 = (f32[72,128]{1,0:T(8,128)S(1)}, f32[72,128]{1,0:T(8,128)S(1)}, u32[]{:S(2)}, u32[]{:S(2)}) collective-permute-start(f32[72,128]{1,0:T(8,128)S(1)} %shard_map.100.a_ref), channel_id=1, source_target_pairs={{0,19},{1,18},{2,17},{3,16},{4,23},{5,22},{6,21},{7,20},{8,27},{9,... | collective-permute-start | bytes 110600 | tf_op jit(solution)/shard_map/ppermute | solution.py:213
  58.6 2.6 %collective-permute-start.12 = (f32[72,128]{1,0:T(8,128)S(1)}, f32[72,128]{1,0:T(8,128)S(1)}, u32[]{:S(2)}, u32[]{:S(2)}) collective-permute-start(f32[72,128]{1,0:T(8,128)S(1)} %shard_map.101.mine_ref.refs_4_), channel_id=1, source_target_pairs={{0,16},{16,0},{1,17},{17,1},{2,18},{18,2},{3,19},{19,3},{4,20},{20... | collective-permute-start | bytes 110600 | tf_op jit(solution)/shard_map/ppermute | solution.py:302

commit v6 on v5

--- a/solution.py
+++ b/solution.py
@@ -164,16 +164,13 @@
     half = out_ref.shape[0] // 2
     copies = []
     for part, side in enumerate((core, 1 - core)):
-        for i in range(half // BLOCK):
-            chips = range(i * CHUNKS, (i + 1) * CHUNKS)
-            if part == 0:
-                g = [g_ref[k, core] for k in chips]
-            else:
-                g = [got_ref[k] for k in chips]
+        for start, size in ((0, LANES), (LANES, half // 2 - LANES), (half // 2, half // 2)) if part == 0 else ((0, half // 2), (half // 2, half // 2)):
+            chips = range(start // LANES, (start + size) // LANES)
+            g = [g_ref[k, core] if part == 0 else got_ref[k] for k in chips]
             gh, gl = split(jnp.concatenate([a * inv for a in g], 1))
-            rows = pl.ds(part * half + i * BLOCK, BLOCK)
+            rows = pl.ds(part * half + start, size)
             out_ref[rows, :] = dot(jnp.concatenate([gh, gl, gh], 0), w, (0, 0))
-            to = pl.ds(pl.multiple_of(side * half, BLOCK) + i * BLOCK, BLOCK)
+            to = pl.ds(pl.multiple_of(side * half, BLOCK) + start, size)
             copies.append(pltpu.make_async_copy(out_ref.at[rows], out_hbm.at[to], sems.at[len(copies)]))
             copies[-1].start()
     for copy in copies:
@@ -306,7 +303,7 @@
         out_shape=shape(slab, LATENT),
         in_specs=[SMEM, VMEM, VMEM, VMEM, VMEM],
         out_specs=HBM,
-        scratch_shapes=[pltpu.VMEM((slab, LATENT), F32), pltpu.SemaphoreType.DMA((steps,))],
+        scratch_shapes=[pltpu.VMEM((slab, LATENT), F32), pltpu.SemaphoreType.DMA((steps + 1,))],
         compiler_params=params(24),
         cost_estimate=pl.CostEstimate(flops=6 * slab * VARS * LATENT, bytes_accessed=4 * slab * LATENT, transcendentals=0),
     )(core, grads, rest, wt, sums)

time: 62.3 us -> 62.2 us (level)
  no operation moved by 1% of the time
where the time goes in v6:
time: 62.2 us; the launch traced here: 61.9 us
  starting transfers between devices  23.7 us (38%)
  blocking collectives  19.8 us (32%)
  waiting for transfers between devices  9.37 us (15%)
  Pallas kernels  8.27 us (13%)
  between operations  0.74 us (1%)
    ppermute x10, starting transfers between devices, trade(): return lax.ppermute(a, MEMBER + GRID, pairs)  17.5 us
    all_to_all x1, blocking collectives, body(): fields = lax.all_to_all(fields, MEMBER, 0, 0)  11 us
    ppermute x10, waiting for transfers between devices, trade(): return lax.ppermute(a, MEMBER + GRID, pairs)  9.05 us
    all_to_all x1, blocking collectives, body(): lax.all_to_all(grads.reshape(chips, 2, VARS, LANES), ('zl', 'x'), 0, 0)  8.84 us
    ppermute x1, starting transfers between devices, body(): got = lax.ppermute(send, 'c', swap)  3.33 us
    pallas_call x1, Pallas kernels, body(): pl.pallas_call(decode_kernel, out_shape=(shape(MEMBERS, VARS, LANES), sha...  3.19 us
    pallas_call x1, Pallas kernels, body(): pl.pallas_call(lambda *refs: latent_kernel(nodes, *refs), out_shape=shape...  2.38 us
    ppermute x1, starting transfers between devices, body(): came = lax.ppermute(other, 'c', swap)  2.05 us
  transfers between devices with their start and end apart: 14, of which 8 were waited for; matrix products, arithmetic and copies ran while one was open for 0% of the time, Pallas kernels for 6%

profile of v6, /device:TPU:1, one launch (start us, length us, event | category | flops | bytes accessed | tf_op | source)
XLA Modules:
  0.0 61.9 jit_solution(943713313944705364)
XLA Ops:
  0.7 3.2 %shard_map.93 = (f32[16,32,128]{2,1,0:T(8,128)S(1)}, f32[1024,512]{1,0:T(8,128)S(1)}, f32[1024,512]{1,0:T(8,128)S(1)}) custom-call(s32[1]{0:T(128)S(6)} %add.27.me_ref.at_ref, s32[1]{0:T(128)S(6)} %and.8.held_ref.h_ref.c_ref, s32[1]{0:T(128)} %bitcast.core_ref.c_ref.refs_0_, f32[2048,512]{1,0:T(8,128)} %bitcast.18, f32[32,512]{1,0:T(8,128)} %bitcast.13, ...), custom_call_target="tpu_custom_call" | custom-call | tf_op jit(solution)/shard_map/pallas_call | solution.py:244
  3.9 3.3 %collective-permute-start = (f32[1024,512]{1,0:T(8,128)S(1)}, f32[1024,512]{1,0:T(8,128)S(1)}, u32[]{:S(2)}, u32[]{:S(2)}) collective-permute-start(f32[1024,512]{1,0:T(8,128)S(1)} %get-tuple-element.17), channel_id=1, source_target_pairs={{0,16},{16,0},{1,17},{17,1},{2,18},{18,2},{3,19},{19,3},{4,20},{20... | collective-permute-start | bytes 6291464 | tf_op jit(solution)/shard_map/ppermute | solution.py:258
  7.2 11.0 %all_to_all.10.f_ref = f32[16,32,128]{2,1,0:T(8,128)S(1)} all-to-all(f32[16,32,128]{2,1,0:T(8,128)S(1)} %get-tuple-element.14), channel_id=1, replica_groups=mesh['zl'=2,'x'=4,'c'=2,'y'=4,'zh'=4] {'zl','x','c'}, dimensions={0} | all-to-all | bytes 524288 | tf_op jit(solution)/shard_map/all_to_all | solution.py:259
  18.2 0.8 %shard_map.94 = (f32[16,32,128]{2,1,0:T(8,128)S(1)}, f32[8,128]{1,0:T(8,128)S(1)}) custom-call(s32[1]{0:T(128)S(6)} %add.27.me_ref.at_ref, f32[16,32,128]{2,1,0:T(8,128)S(1)} %all_to_all.10.f_ref, f32[32,2048]{1,0:T(8,128)S(1)} %copy-done.1, f32[16,128]{1,0:T(8,128)S(1)} %bitcast.16, f32[1,32]{1,0:T(1,128)S(1)} %bitcast.17), custom_call_target="tpu_custom_call" | custom-call | tf_op jit(solution)/shard_map/pallas_call | solution.py:261
  19.0 8.8 %all_to_all.11.g_ref.refs_1_ = f32[8,2,32,128]{3,2,1,0:T(8,128)S(1)} all-to-all(f32[8,2,32,128]{3,2,1,0:T(8,128)S(1)} %bitcast.15), channel_id=1, replica_groups=mesh['zl'=2,'x'=4,'c'=2,'y'=4,'zh'=4] {'zl','x'}, dimensions={0} | all-to-all | bytes 524288 | tf_op jit(solution)/shard_map/all_to_all | solution.py:278
  27.9 0.0 collective-permute-done.got_ref
  27.9 0.6 shard_map.96
  28.4 0.0 copy-start
  28.4 2.1 %collective-permute-start.1 = (f32[72,128]{1,0:T(8,128)S(1)}, f32[72,128]{1,0:T(8,128)S(1)}, u32[]{:S(2)}, u32[]{:S(2)}) collective-permute-start(f32[72,128]{1,0:T(8,128)S(1)} %shard_map.96), channel_id=1, source_target_pairs={{0,16},{16,0},{1,17},{17,1},{2,18},{18,2},{3,19},{19,3},{4,20},{20... | collective-permute-start | bytes 110600 | tf_op jit(solution)/shard_map/ppermute | solution.py:291
  30.5 0.6 shard_map.95
  31.0 0.3 collective-permute-done.1.b_ref
  31.4 0.6 %collective-permute-start.4 = (f32[72,128]{1,0:T(8,128)S(1)}, f32[72,128]{1,0:T(8,128)S(1)}, u32[]{:S(2)}, u32[]{:S(2)}) collective-permute-start(f32[72,128]{1,0:T(8,128)S(1)} %shard_map.97.a_ref), channel_id=1, source_target_pairs={{0,160},{1,161},{2,162},{3,163},{4,164},{5,165},{6,166},{7,167},{8... | collective-permute-start | bytes 110600 | tf_op jit(solution)/shard_map/ppermute | solution.py:210
  32.0 1.0 %collective-permute-start.3 = (f32[72,128]{1,0:T(8,128)S(1)}, f32[72,128]{1,0:T(8,128)S(1)}, u32[]{:S(2)}, u32[]{:S(2)}) collective-permute-start(f32[72,128]{1,0:T(8,128)S(1)} %shard_map.97.a_ref), channel_id=1, source_target_pairs={{0,144},{1,145},{2,146},{3,147},{4,148},{5,149},{6,150},{7,151},{8... | collective-permute-start | bytes 110600 | tf_op jit(solution)/shard_map/ppermute | solution.py:210
  33.0 1.3 %collective-permute-start.2 = (f32[72,128]{1,0:T(8,128)S(1)}, f32[72,128]{1,0:T(8,128)S(1)}, u32[]{:S(2)}, u32[]{:S(2)}) collective-permute-start(f32[72,128]{1,0:T(8,128)S(1)} %shard_map.97.a_ref), channel_id=1, source_target_pairs={{0,48},{1,49},{2,50},{3,51},{4,52},{5,53},{6,54},{7,55},{8,56},{9,... | collective-permute-start | bytes 110600 | tf_op jit(solution)/shard_map/ppermute | solution.py:210
  34.3 0.6 %collective-permute-start.13 = (f32[8,32,128]{2,1,0:T(8,128)S(1)}, f32[8,32,128]{2,1,0:T(8,128)S(1)}, u32[]{:S(2)}, u32[]{:S(2)}) collective-permute-start(f32[8,32,128]{2,1,0:T(8,128)S(1)} %get-tuple-element.21), channel_id=1, source_target_pairs={{0,16},{16,0},{1,17},{17,1},{2,18},{18,2},{3,19},{19,3},{4,20},{20... | collective-permute-start | bytes 393224 | tf_op jit(solution)/shard_map/ppermute | solution.py:293
  34.9 0.1 collective-permute-done.4.d_ref
  35.1 0.9 %collective-permute-done.3.c_ref = f32[72,128]{1,0:T(8,128)S(1)} collective-permute-done((f32[72,128]{1,0:T(8,128)S(1)}, f32[72,128]{1,0:T(8,128)S(1)}, u32[]{:S(2)}, u32[]{:S(2)}) %collective-permute-start.3) | collective-permute-done | bytes 36896 | tf_op jit(solution)/shard_map/ppermute | solution.py:210
  36.0 0.7 %collective-permute-done.2.b_ref = f32[72,128]{1,0:T(8,128)S(1)} collective-permute-done((f32[72,128]{1,0:T(8,128)S(1)}, f32[72,128]{1,0:T(8,128)S(1)}, u32[]{:S(2)}, u32[]{:S(2)}) %collective-permute-start.2) | collective-permute-done | bytes 36896 | tf_op jit(solution)/shard_map/ppermute | solution.py:210
  36.7 3.2 %collective-permute-start.7 = (f32[72,128]{1,0:T(8,128)S(1)}, f32[72,128]{1,0:T(8,128)S(1)}, u32[]{:S(2)}, u32[]{:S(2)}) collective-permute-start(f32[72,128]{1,0:T(8,128)S(1)} %shard_map.98.a_ref), channel_id=1, source_target_pairs={{0,108},{1,109},{2,110},{3,111},{4,104},{5,105},{6,106},{7,107},{8... | collective-permute-start | bytes 110600 | tf_op jit(solution)/shard_map/ppermute | solution.py:210
  39.9 0.3 collective-permute-start.6
  40.2 2.3 %collective-permute-start.5 = (f32[72,128]{1,0:T(8,128)S(1)}, f32[72,128]{1,0:T(8,128)S(1)}, u32[]{:S(2)}, u32[]{:S(2)}) collective-permute-start(f32[72,128]{1,0:T(8,128)S(1)} %shard_map.98.a_ref), channel_id=1, source_target_pairs={{0,112},{1,113},{2,114},{3,115},{4,116},{5,117},{6,118},{7,119},{8... | collective-permute-start | bytes 110600 | tf_op jit(solution)/shard_map/ppermute | solution.py:210
  42.5 0.4 collective-permute-done.7.d_ref
  43.0 2.0 %collective-permute-done.6.c_ref = f32[72,128]{1,0:T(8,128)S(1)} collective-permute-done((f32[72,128]{1,0:T(8,128)S(1)}, f32[72,128]{1,0:T(8,128)S(1)}, u32[]{:S(2)}, u32[]{:S(2)}) %collective-permute-start.6) | collective-permute-done | bytes 36896 | tf_op jit(solution)/shard_map/ppermute | solution.py:210
  45.0 2.7 %collective-permute-start.10 = (f32[72,128]{1,0:T(8,128)S(1)}, f32[72,128]{1,0:T(8,128)S(1)}, u32[]{:S(2)}, u32[]{:S(2)}) collective-permute-start(f32[72,128]{1,0:T(8,128)S(1)} %shard_map.99.a_ref), channel_id=1, source_target_pairs={{0,5},{1,4},{2,7},{3,6},{4,1},{5,0},{6,3},{7,2},{8,13},{9,12},{10,... | collective-permute-start | bytes 110600 | tf_op jit(solution)/shard_map/ppermute | solution.py:210
  47.7 0.7 %collective-permute-start.9 = (f32[72,128]{1,0:T(8,128)S(1)}, f32[72,128]{1,0:T(8,128)S(1)}, u32[]{:S(2)}, u32[]{:S(2)}) collective-permute-start(f32[72,128]{1,0:T(8,128)S(1)} %shard_map.99.a_ref), channel_id=1, source_target_pairs={{0,17},{1,16},{2,19},{3,18},{4,21},{5,20},{6,23},{7,22},{8,25},{9,... | collective-permute-start | bytes 110600 | tf_op jit(solution)/shard_map/ppermute | solution.py:210
  48.4 1.4 %collective-permute-start.8 = (f32[72,128]{1,0:T(8,128)S(1)}, f32[72,128]{1,0:T(8,128)S(1)}, u32[]{:S(2)}, u32[]{:S(2)}) collective-permute-start(f32[72,128]{1,0:T(8,128)S(1)} %shard_map.99.a_ref), channel_id=1, source_target_pairs={{0,20},{1,21},{2,22},{3,23},{4,16},{5,17},{6,18},{7,19},{8,28},{9,... | collective-permute-start | bytes 110600 | tf_op jit(solution)/shard_map/ppermute | solution.py:210
  49.8 3.2 %collective-permute-done.9.c_ref = f32[72,128]{1,0:T(8,128)S(1)} collective-permute-done((f32[72,128]{1,0:T(8,128)S(1)}, f32[72,128]{1,0:T(8,128)S(1)}, u32[]{:S(2)}, u32[]{:S(2)}) %collective-permute-start.9) | collective-permute-done | bytes 36896 | tf_op jit(solution)/shard_map/ppermute | solution.py:210
  53.0 4.0 %collective-permute-start.11 = (f32[72,128]{1,0:T(8,128)S(1)}, f32[72,128]{1,0:T(8,128)S(1)}, u32[]{:S(2)}, u32[]{:S(2)}) collective-permute-start(f32[72,128]{1,0:T(8,128)S(1)} %shard_map.100.a_ref), channel_id=1, source_target_pairs={{0,19},{1,18},{2,17},{3,16},{4,23},{5,22},{6,21},{7,20},{8,27},{9,... | collective-permute-start | bytes 110600 | tf_op jit(solution)/shard_map/ppermute | solution.py:210
  57.0 1.6 %collective-permute-done.11.b_ref = f32[72,128]{1,0:T(8,128)S(1)} collective-permute-done((f32[72,128]{1,0:T(8,128)S(1)}, f32[72,128]{1,0:T(8,128)S(1)}, u32[]{:S(2)}, u32[]{:S(2)}) %collective-permute-start.11) | collective-permute-done | bytes 36896 | tf_op jit(solution)/shard_map/ppermute | solution.py:210
  58.6 0.1 collective-permute-start.12
  58.8 2.4 %shard_map.103 = f32[2048,512]{1,0:T(8,128)} custom-call(s32[1]{0:T(128)} %bitcast.core_ref.c_ref.refs_0_, f32[8,2,32,128]{3,2,1,0:T(8,128)S(1)} %all_to_all.11.g_ref.refs_1_, f32[8,32,128]{2,1,0:T(8,128)S(1)} %collective-permute-done.13.refs_2_, f32[32,512]{1,0:T(8,128)S(1)} %bitcast.14, f32[72,128]{1,0:T(8,128)S(1)} %shard_map.101.mine_ref.refs_4_), custom_call_target="tpu_custom_call" | custom-call | flops 201326592 | bytes 4194304 | tf_op jit(solution)/shard_map/pallas_call | solution.py:301
  61.2 0.7 %shard_map.102 = (f32[32,512]{1,0:T(8,128)}, f32[1,1]{1,0:T(1,128)}, f32[1,32]{1,0:T(1,128)}) custom-call(s32[1]{0:T(128)S(6)} %and.8.held_ref.h_ref.c_ref, f32[72,128]{1,0:T(8,128)S(1)} %shard_map.101.mine_ref.refs_4_, f32[72,128]{1,0:T(8,128)S(1)} %collective-permute-done.12.theirs_ref), custom_call_target="tpu_custom_call" | custom-call | tf_op jit(solution)/shard_map/pallas_call | solution.py:311
  (17 shorter events, 0.1 us)
Async XLA Ops:
  0.6 17.6 %copy-start.1 = (f32[32,2048]{1,0:T(8,128)S(1)}, f32[32,2048]{1,0:T(8,128)}, u32[]{:S(2)}) copy-start(f32[32,2048]{1,0:T(8,128)} %t_ref.1) | copy-start | bytes 786436
  0.7 17.5 %copy-start.2 = (f32[2048]{0:T(1024)S(1)}, f32[2048]{0:T(1024)}, u32[]{:S(2)}) copy-start(f32[2048]{0:T(1024)} %param.10) | copy-start | bytes 24580
  0.7 17.5 %copy-start.3 = (f32[32]{0:T(128)S(1)}, f32[32]{0:T(128)}, u32[]{:S(2)}) copy-start(f32[32]{0:T(128)} %param.11) | copy-start | bytes 388
  3.9 24.0 %collective-permute-start = (f32[1024,512]{1,0:T(8,128)S(1)}, f32[1024,512]{1,0:T(8,128)S(1)}, u32[]{:S(2)}, u32[]{:S(2)}) collective-permute-start(f32[1024,512]{1,0:T(8,128)S(1)} %get-tuple-element.17), channel_id=1, source_target_pairs={{0,16},{16,0},{1,17},{17,1},{2,18},{18,2},{3,19},{19,3},{4,20},{20... | collective-permute-start | bytes 6291464 | tf_op jit(solution)/shard_map/ppermute | solution.py:258
  28.4 30.4 %copy-start = (f32[512,32]{0,1:T(8,128)S(1)}, f32[512,32]{0,1:T(8,128)}, u32[]{:S(2)}) copy-start(f32[512,32]{0,1:T(8,128)} %param.7) | copy-start | bytes 196612
  28.4 2.9 %collective-permute-start.1 = (f32[72,128]{1,0:T(8,128)S(1)}, f32[72,128]{1,0:T(8,128)S(1)}, u32[]{:S(2)}, u32[]{:S(2)}) collective-permute-start(f32[72,128]{1,0:T(8,128)S(1)} %shard_map.96), channel_id=1, source_target_pairs={{0,16},{16,0},{1,17},{17,1},{2,18},{18,2},{3,19},{19,3},{4,20},{20... | collective-permute-start | bytes 110600 | tf_op jit(solution)/shard_map/ppermute | solution.py:291
  31.4 3.7 %collective-permute-start.4 = (f32[72,128]{1,0:T(8,128)S(1)}, f32[72,128]{1,0:T(8,128)S(1)}, u32[]{:S(2)}, u32[]{:S(2)}) collective-permute-start(f32[72,128]{1,0:T(8,128)S(1)} %shard_map.97.a_ref), channel_id=1, source_target_pairs={{0,160},{1,161},{2,162},{3,163},{4,164},{5,165},{6,166},{7,167},{8... | collective-permute-start | bytes 110600 | tf_op jit(solution)/shard_map/ppermute | solution.py:210
  32.0 4.0 %collective-permute-start.3 = (f32[72,128]{1,0:T(8,128)S(1)}, f32[72,128]{1,0:T(8,128)S(1)}, u32[]{:S(2)}, u32[]{:S(2)}) collective-permute-start(f32[72,128]{1,0:T(8,128)S(1)} %shard_map.97.a_ref), channel_id=1, source_target_pairs={{0,144},{1,145},{2,146},{3,147},{4,148},{5,149},{6,150},{7,151},{8... | collective-permute-start | bytes 110600 | tf_op jit(solution)/shard_map/ppermute | solution.py:210
  33.0 3.7 %collective-permute-start.2 = (f32[72,128]{1,0:T(8,128)S(1)}, f32[72,128]{1,0:T(8,128)S(1)}, u32[]{:S(2)}, u32[]{:S(2)}) collective-permute-start(f32[72,128]{1,0:T(8,128)S(1)} %shard_map.97.a_ref), channel_id=1, source_target_pairs={{0,48},{1,49},{2,50},{3,51},{4,52},{5,53},{6,54},{7,55},{8,56},{9,... | collective-permute-start | bytes 110600 | tf_op jit(solution)/shard_map/ppermute | solution.py:210
  34.3 24.5 %collective-permute-start.13 = (f32[8,32,128]{2,1,0:T(8,128)S(1)}, f32[8,32,128]{2,1,0:T(8,128)S(1)}, u32[]{:S(2)}, u32[]{:S(2)}) collective-permute-start(f32[8,32,128]{2,1,0:T(8,128)S(1)} %get-tuple-element.21), channel_id=1, source_target_pairs={{0,16},{16,0},{1,17},{17,1},{2,18},{18,2},{3,19},{19,3},{4,20},{20... | collective-permute-start | bytes 393224 | tf_op jit(solution)/shard_map/ppermute | solution.py:293
  36.7 6.2 %collective-permute-start.7 = (f32[72,128]{1,0:T(8,128)S(1)}, f32[72,128]{1,0:T(8,128)S(1)}, u32[]{:S(2)}, u32[]{:S(2)}) collective-permute-start(f32[72,128]{1,0:T(8,128)S(1)} %shard_map.98.a_ref), channel_id=1, source_target_pairs={{0,108},{1,109},{2,110},{3,111},{4,104},{5,105},{6,106},{7,107},{8... | collective-permute-start | bytes 110600 | tf_op jit(solution)/shard_map/ppermute | solution.py:210
  39.9 5.0 %collective-permute-start.6 = (f32[72,128]{1,0:T(8,128)S(1)}, f32[72,128]{1,0:T(8,128)S(1)}, u32[]{:S(2)}, u32[]{:S(2)}) collective-permute-start(f32[72,128]{1,0:T(8,128)S(1)} %shard_map.98.a_ref), channel_id=1, source_target_pairs={{0,28},{1,29},{2,30},{3,31},{4,24},{5,25},{6,26},{7,27},{8,20},{9,... | collective-permute-start | bytes 110600 | tf_op jit(solution)/shard_map/ppermute | solution.py:210
  40.2 4.8 %collective-permute-start.5 = (f32[72,128]{1,0:T(8,128)S(1)}, f32[72,128]{1,0:T(8,128)S(1)}, u32[]{:S(2)}, u32[]{:S(2)}) collective-permute-start(f32[72,128]{1,0:T(8,128)S(1)} %shard_map.98.a_ref), channel_id=1, source_target_pairs={{0,112},{1,113},{2,114},{3,115},{4,116},{5,117},{6,118},{7,119},{8... | collective-permute-start | bytes 110600 | tf_op jit(solution)/shard_map/ppermute | solution.py:210
  45.0 4.8 %collective-permute-start.10 = (f32[72,128]{1,0:T(8,128)S(1)}, f32[72,128]{1,0:T(8,128)S(1)}, u32[]{:S(2)}, u32[]{:S(2)}) collective-permute-start(f32[72,128]{1,0:T(8,128)S(1)} %shard_map.99.a_ref), channel_id=1, source_target_pairs={{0,5},{1,4},{2,7},{3,6},{4,1},{5,0},{6,3},{7,2},{8,13},{9,12},{10,... | collective-permute-start | bytes 110600 | tf_op jit(solution)/shard_map/ppermute | solution.py:210
  47.7 5.3 %collective-permute-start.9 = (f32[72,128]{1,0:T(8,128)S(1)}, f32[72,128]{1,0:T(8,128)S(1)}, u32[]{:S(2)}, u32[]{:S(2)}) collective-permute-start(f32[72,128]{1,0:T(8,128)S(1)} %shard_map.99.a_ref), channel_id=1, source_target_pairs={{0,17},{1,16},{2,19},{3,18},{4,21},{5,20},{6,23},{7,22},{8,25},{9,... | collective-permute-start | bytes 110600 | tf_op jit(solution)/shard_map/ppermute | solution.py:210
  48.4 4.5 %collective-permute-start.8 = (f32[72,128]{1,0:T(8,128)S(1)}, f32[72,128]{1,0:T(8,128)S(1)}, u32[]{:S(2)}, u32[]{:S(2)}) collective-permute-start(f32[72,128]{1,0:T(8,128)S(1)} %shard_map.99.a_ref), channel_id=1, source_target_pairs={{0,20},{1,21},{2,22},{3,23},{4,16},{5,17},{6,18},{7,19},{8,28},{9,... | collective-permute-start | bytes 110600 | tf_op jit(solution)/shard_map/ppermute | solution.py:210
  53.0 5.6 %collective-permute-start.11 = (f32[72,128]{1,0:T(8,128)S(1)}, f32[72,128]{1,0:T(8,128)S(1)}, u32[]{:S(2)}, u32[]{:S(2)}) collective-permute-start(f32[72,128]{1,0:T(8,128)S(1)} %shard_map.100.a_ref), channel_id=1, source_target_pairs={{0,19},{1,18},{2,17},{3,16},{4,23},{5,22},{6,21},{7,20},{8,27},{9,... | collective-permute-start | bytes 110600 | tf_op jit(solution)/shard_map/ppermute | solution.py:210
  58.6 2.5 %collective-permute-start.12 = (f32[72,128]{1,0:T(8,128)S(1)}, f32[72,128]{1,0:T(8,128)S(1)}, u32[]{:S(2)}, u32[]{:S(2)}) collective-permute-start(f32[72,128]{1,0:T(8,128)S(1)} %shard_map.101.mine_ref.refs_4_), channel_id=1, source_target_pairs={{0,16},{16,0},{1,17},{17,1},{2,18},{18,2},{3,19},{19,3},{4,20},{20... | collective-permute-start | bytes 110600 | tf_op jit(solution)/shard_map/ppermute | solution.py:299

commit v7 on v6

--- a/solution.py
+++ b/solution.py
@@ -125,12 +125,10 @@
     columns = pl.ds(pl.multiple_of(side * HALF, HALF), HALF)
     acc = jnp.zeros((VARS, HALF), F32)
     for x_ref, whose in ((keep_ref, core), (got_ref, 1 - core)):
-        for i in range(x_ref.shape[0] // BLOCK):
-            g = jnp.concatenate([g_ref[i * CHUNKS + j, whose] for j in range(CHUNKS)], 1)
-            gh, gl = split(g)
-            xh, xl = split(x_ref[i * BLOCK : (i + 1) * BLOCK, columns])
-            both = dot(jnp.concatenate([gh, gl], 0), xh, (1, 0))
-            acc = acc + (both[:VARS] + both[VARS:] + dot(gh, xl, (1, 0)))
+        gh, gl = split(jnp.concatenate([g_ref[i, whose] for i in range(g_ref.shape[0])], 1))
+        xh, xl = split(x_ref[:, columns])
+        both = dot(jnp.concatenate([gh, gl], 0), xh, (1, 0))
+        acc = acc + (both[:VARS] + both[VARS:] + dot(gh, xl, (1, 0)))
     for i in range(HALF // LANES):
         out_ref[i * VARS : (i + 1) * VARS, :] = acc[:, i * LANES : (i + 1) * LANES]
     out_ref[ROWS:SUMS, :] = e_ref[...]

time: 62.2 us -> 62.2 us (level)
  no operation moved by 1% of the time
where the time goes in v7:
time: 62.2 us; the launch traced here: 61.9 us
  starting transfers between devices  23.7 us (38%)
  blocking collectives  19.8 us (32%)
  waiting for transfers between devices  9.34 us (15%)
  Pallas kernels  8.31 us (13%)
  between operations  0.74 us (1%)
    ppermute x10, starting transfers between devices, trade(): return lax.ppermute(a, MEMBER + GRID, pairs)  17.5 us
    all_to_all x1, blocking collectives, body(): fields = lax.all_to_all(fields, MEMBER, 0, 0)  11 us
    ppermute x10, waiting for transfers between devices, trade(): return lax.ppermute(a, MEMBER + GRID, pairs)  9.05 us
    all_to_all x1, blocking collectives, body(): lax.all_to_all(grads.reshape(chips, 2, VARS, LANES), ('zl', 'x'), 0, 0)  8.84 us
    ppermute x1, starting transfers between devices, body(): got = lax.ppermute(send, 'c', swap)  3.33 us
    pallas_call x1, Pallas kernels, body(): pl.pallas_call(decode_kernel, out_shape=(shape(MEMBERS, VARS, LANES), sha...  3.19 us
    pallas_call x1, Pallas kernels, body(): pl.pallas_call(lambda *refs: latent_kernel(nodes, *refs), out_shape=shape...  2.39 us
    ppermute x1, starting transfers between devices, body(): came = lax.ppermute(other, 'c', swap)  2.06 us
  transfers between devices with their start and end apart: 14, of which 8 were waited for; matrix products, arithmetic and copies ran while one was open for 0% of the time, Pallas kernels for 6%

profile of v7, /device:TPU:1, one launch (start us, length us, event | category | flops | bytes accessed | tf_op | source)
XLA Modules:
  0.0 61.9 jit_solution(279261070618195153)
XLA Ops:
  0.7 3.2 %shard_map.93 = (f32[16,32,128]{2,1,0:T(8,128)S(1)}, f32[1024,512]{1,0:T(8,128)S(1)}, f32[1024,512]{1,0:T(8,128)S(1)}) custom-call(s32[1]{0:T(128)S(6)} %add.27.me_ref.at_ref, s32[1]{0:T(128)S(6)} %and.8.held_ref.h_ref.c_ref, s32[1]{0:T(128)} %bitcast.core_ref.c_ref.refs_0_, f32[2048,512]{1,0:T(8,128)} %bitcast.18, f32[32,512]{1,0:T(8,128)} %bitcast.13, ...), custom_call_target="tpu_custom_call" | custom-call | tf_op jit(solution)/shard_map/pallas_call | solution.py:242
  3.9 3.3 %collective-permute-start = (f32[1024,512]{1,0:T(8,128)S(1)}, f32[1024,512]{1,0:T(8,128)S(1)}, u32[]{:S(2)}, u32[]{:S(2)}) collective-permute-start(f32[1024,512]{1,0:T(8,128)S(1)} %get-tuple-element.17), channel_id=1, source_target_pairs={{0,16},{16,0},{1,17},{17,1},{2,18},{18,2},{3,19},{19,3},{4,20},{20... | collective-permute-start | bytes 6291464 | tf_op jit(solution)/shard_map/ppermute | solution.py:256
  7.2 11.0 %all_to_all.10.f_ref = f32[16,32,128]{2,1,0:T(8,128)S(1)} all-to-all(f32[16,32,128]{2,1,0:T(8,128)S(1)} %get-tuple-element.14), channel_id=1, replica_groups=mesh['zl'=2,'x'=4,'c'=2,'y'=4,'zh'=4] {'zl','x','c'}, dimensions={0} | all-to-all | bytes 524288 | tf_op jit(solution)/shard_map/all_to_all | solution.py:257
  18.2 0.8 %shard_map.94 = (f32[16,32,128]{2,1,0:T(8,128)S(1)}, f32[8,128]{1,0:T(8,128)S(1)}) custom-call(s32[1]{0:T(128)S(6)} %add.27.me_ref.at_ref, f32[16,32,128]{2,1,0:T(8,128)S(1)} %all_to_all.10.f_ref, f32[32,2048]{1,0:T(8,128)S(1)} %copy-done.1, f32[16,128]{1,0:T(8,128)S(1)} %bitcast.16, f32[1,32]{1,0:T(1,128)S(1)} %bitcast.17), custom_call_target="tpu_custom_call" | custom-call | tf_op jit(solution)/shard_map/pallas_call | solution.py:259
  19.0 8.8 %all_to_all.11.g_ref.refs_1_ = f32[8,2,32,128]{3,2,1,0:T(8,128)S(1)} all-to-all(f32[8,2,32,128]{3,2,1,0:T(8,128)S(1)} %bitcast.15), channel_id=1, replica_groups=mesh['zl'=2,'x'=4,'c'=2,'y'=4,'zh'=4] {'zl','x'}, dimensions={0} | all-to-all | bytes 524288 | tf_op jit(solution)/shard_map/all_to_all | solution.py:276
  27.9 0.0 collective-permute-done.got_ref
  27.9 0.6 shard_map.96
  28.4 0.0 copy-start
  28.4 2.1 %collective-permute-start.1 = (f32[72,128]{1,0:T(8,128)S(1)}, f32[72,128]{1,0:T(8,128)S(1)}, u32[]{:S(2)}, u32[]{:S(2)}) collective-permute-start(f32[72,128]{1,0:T(8,128)S(1)} %shard_map.96), channel_id=1, source_target_pairs={{0,16},{16,0},{1,17},{17,1},{2,18},{18,2},{3,19},{19,3},{4,20},{20... | collective-permute-start | bytes 110600 | tf_op jit(solution)/shard_map/ppermute | solution.py:289
  30.5 0.6 shard_map.95
  31.1 0.3 collective-permute-done.1.b_ref
  31.4 0.6 %collective-permute-start.4 = (f32[72,128]{1,0:T(8,128)S(1)}, f32[72,128]{1,0:T(8,128)S(1)}, u32[]{:S(2)}, u32[]{:S(2)}) collective-permute-start(f32[72,128]{1,0:T(8,128)S(1)} %shard_map.97.a_ref), channel_id=1, source_target_pairs={{0,160},{1,161},{2,162},{3,163},{4,164},{5,165},{6,166},{7,167},{8... | collective-permute-start | bytes 110600 | tf_op jit(solution)/shard_map/ppermute | solution.py:208
  32.0 1.0 %collective-permute-start.3 = (f32[72,128]{1,0:T(8,128)S(1)}, f32[72,128]{1,0:T(8,128)S(1)}, u32[]{:S(2)}, u32[]{:S(2)}) collective-permute-start(f32[72,128]{1,0:T(8,128)S(1)} %shard_map.97.a_ref), channel_id=1, source_target_pairs={{0,144},{1,145},{2,146},{3,147},{4,148},{5,149},{6,150},{7,151},{8... | collective-permute-start | bytes 110600 | tf_op jit(solution)/shard_map/ppermute | solution.py:208
  33.0 1.3 %collective-permute-start.2 = (f32[72,128]{1,0:T(8,128)S(1)}, f32[72,128]{1,0:T(8,128)S(1)}, u32[]{:S(2)}, u32[]{:S(2)}) collective-permute-start(f32[72,128]{1,0:T(8,128)S(1)} %shard_map.97.a_ref), channel_id=1, source_target_pairs={{0,48},{1,49},{2,50},{3,51},{4,52},{5,53},{6,54},{7,55},{8,56},{9,... | collective-permute-start | bytes 110600 | tf_op jit(solution)/shard_map/ppermute | solution.py:208
  34.3 0.6 %collective-permute-start.13 = (f32[8,32,128]{2,1,0:T(8,128)S(1)}, f32[8,32,128]{2,1,0:T(8,128)S(1)}, u32[]{:S(2)}, u32[]{:S(2)}) collective-permute-start(f32[8,32,128]{2,1,0:T(8,128)S(1)} %get-tuple-element.21), channel_id=1, source_target_pairs={{0,16},{16,0},{1,17},{17,1},{2,18},{18,2},{3,19},{19,3},{4,20},{20... | collective-permute-start | bytes 393224 | tf_op jit(solution)/shard_map/ppermute | solution.py:291
  34.9 0.1 collective-permute-done.4.d_ref
  35.1 0.9 %collective-permute-done.3.c_ref = f32[72,128]{1,0:T(8,128)S(1)} collective-permute-done((f32[72,128]{1,0:T(8,128)S(1)}, f32[72,128]{1,0:T(8,128)S(1)}, u32[]{:S(2)}, u32[]{:S(2)}) %collective-permute-start.3) | collective-permute-done | bytes 36896 | tf_op jit(solution)/shard_map/ppermute | solution.py:208
  36.0 0.7 %collective-permute-done.2.b_ref = f32[72,128]{1,0:T(8,128)S(1)} collective-permute-done((f32[72,128]{1,0:T(8,128)S(1)}, f32[72,128]{1,0:T(8,128)S(1)}, u32[]{:S(2)}, u32[]{:S(2)}) %collective-permute-start.2) | collective-permute-done | bytes 36896 | tf_op jit(solution)/shard_map/ppermute | solution.py:208
  36.8 3.2 %collective-permute-start.7 = (f32[72,128]{1,0:T(8,128)S(1)}, f32[72,128]{1,0:T(8,128)S(1)}, u32[]{:S(2)}, u32[]{:S(2)}) collective-permute-start(f32[72,128]{1,0:T(8,128)S(1)} %shard_map.98.a_ref), channel_id=1, source_target_pairs={{0,108},{1,109},{2,110},{3,111},{4,104},{5,105},{6,106},{7,107},{8... | collective-permute-start | bytes 110600 | tf_op jit(solution)/shard_map/ppermute | solution.py:208
  39.9 0.3 collective-permute-start.6
  40.2 2.3 %collective-permute-start.5 = (f32[72,128]{1,0:T(8,128)S(1)}, f32[72,128]{1,0:T(8,128)S(1)}, u32[]{:S(2)}, u32[]{:S(2)}) collective-permute-start(f32[72,128]{1,0:T(8,128)S(1)} %shard_map.98.a_ref), channel_id=1, source_target_pairs={{0,112},{1,113},{2,114},{3,115},{4,116},{5,117},{6,118},{7,119},{8... | collective-permute-start | bytes 110600 | tf_op jit(solution)/shard_map/ppermute | solution.py:208
  42.5 0.4 collective-permute-done.7.d_ref
  43.0 2.0 %collective-permute-done.6.c_ref = f32[72,128]{1,0:T(8,128)S(1)} collective-permute-done((f32[72,128]{1,0:T(8,128)S(1)}, f32[72,128]{1,0:T(8,128)S(1)}, u32[]{:S(2)}, u32[]{:S(2)}) %collective-permute-start.6) | collective-permute-done | bytes 36896 | tf_op jit(solution)/shard_map/ppermute | solution.py:208
  45.0 2.7 %collective-permute-start.10 = (f32[72,128]{1,0:T(8,128)S(1)}, f32[72,128]{1,0:T(8,128)S(1)}, u32[]{:S(2)}, u32[]{:S(2)}) collective-permute-start(f32[72,128]{1,0:T(8,128)S(1)} %shard_map.99.a_ref), channel_id=1, source_target_pairs={{0,5},{1,4},{2,7},{3,6},{4,1},{5,0},{6,3},{7,2},{8,13},{9,12},{10,... | collective-permute-start | bytes 110600 | tf_op jit(solution)/shard_map/ppermute | solution.py:208
  47.7 0.7 %collective-permute-start.9 = (f32[72,128]{1,0:T(8,128)S(1)}, f32[72,128]{1,0:T(8,128)S(1)}, u32[]{:S(2)}, u32[]{:S(2)}) collective-permute-start(f32[72,128]{1,0:T(8,128)S(1)} %shard_map.99.a_ref), channel_id=1, source_target_pairs={{0,17},{1,16},{2,19},{3,18},{4,21},{5,20},{6,23},{7,22},{8,25},{9,... | collective-permute-start | bytes 110600 | tf_op jit(solution)/shard_map/ppermute | solution.py:208
  48.4 1.4 %collective-permute-start.8 = (f32[72,128]{1,0:T(8,128)S(1)}, f32[72,128]{1,0:T(8,128)S(1)}, u32[]{:S(2)}, u32[]{:S(2)}) collective-permute-start(f32[72,128]{1,0:T(8,128)S(1)} %shard_map.99.a_ref), channel_id=1, source_target_pairs={{0,20},{1,21},{2,22},{3,23},{4,16},{5,17},{6,18},{7,19},{8,28},{9,... | collective-permute-start | bytes 110600 | tf_op jit(solution)/shard_map/ppermute | solution.py:208
  49.8 3.2 %collective-permute-done.9.c_ref = f32[72,128]{1,0:T(8,128)S(1)} collective-permute-done((f32[72,128]{1,0:T(8,128)S(1)}, f32[72,128]{1,0:T(8,128)S(1)}, u32[]{:S(2)}, u32[]{:S(2)}) %collective-permute-start.9) | collective-permute-done | bytes 36896 | tf_op jit(solution)/shard_map/ppermute | solution.py:208
  53.0 4.0 %collective-permute-start.11 = (f32[72,128]{1,0:T(8,128)S(1)}, f32[72,128]{1,0:T(8,128)S(1)}, u32[]{:S(2)}, u32[]{:S(2)}) collective-permute-start(f32[72,128]{1,0:T(8,128)S(1)} %shard_map.100.a_ref), channel_id=1, source_target_pairs={{0,19},{1,18},{2,17},{3,16},{4,23},{5,22},{6,21},{7,20},{8,27},{9,... | collective-permute-start | bytes 110600 | tf_op jit(solution)/shard_map/ppermute | solution.py:208
  57.0 1.6 %collective-permute-done.11.b_ref = f32[72,128]{1,0:T(8,128)S(1)} collective-permute-done((f32[72,128]{1,0:T(8,128)S(1)}, f32[72,128]{1,0:T(8,128)S(1)}, u32[]{:S(2)}, u32[]{:S(2)}) %collective-permute-start.11) | collective-permute-done | bytes 36896 | tf_op jit(solution)/shard_map/ppermute | solution.py:208
  58.6 0.1 collective-permute-start.12
  58.8 2.4 %shard_map.103 = f32[2048,512]{1,0:T(8,128)} custom-call(s32[1]{0:T(128)} %bitcast.core_ref.c_ref.refs_0_, f32[8,2,32,128]{3,2,1,0:T(8,128)S(1)} %all_to_all.11.g_ref.refs_1_, f32[8,32,128]{2,1,0:T(8,128)S(1)} %collective-permute-done.13.refs_2_, f32[32,512]{1,0:T(8,128)S(1)} %bitcast.14, f32[72,128]{1,0:T(8,128)S(1)} %shard_map.101.mine_ref.refs_4_), custom_call_target="tpu_custom_call" | custom-call | flops 201326592 | bytes 4194304 | tf_op jit(solution)/shard_map/pallas_call | solution.py:299
  61.2 0.7 %shard_map.102 = (f32[32,512]{1,0:T(8,128)}, f32[1,1]{1,0:T(1,128)}, f32[1,32]{1,0:T(1,128)}) custom-call(s32[1]{0:T(128)S(6)} %and.8.held_ref.h_ref.c_ref, f32[72,128]{1,0:T(8,128)S(1)} %shard_map.101.mine_ref.refs_4_, f32[72,128]{1,0:T(8,128)S(1)} %collective-permute-done.12.theirs_ref), custom_call_target="tpu_custom_call" | custom-call | tf_op jit(solution)/shard_map/pallas_call | solution.py:309
  (17 shorter events, 0.1 us)
Async XLA Ops:
  0.6 17.6 %copy-start.1 = (f32[32,2048]{1,0:T(8,128)S(1)}, f32[32,2048]{1,0:T(8,128)}, u32[]{:S(2)}) copy-start(f32[32,2048]{1,0:T(8,128)} %t_ref.1) | copy-start | bytes 786436
  0.7 17.5 %copy-start.2 = (f32[2048]{0:T(1024)S(1)}, f32[2048]{0:T(1024)}, u32[]{:S(2)}) copy-start(f32[2048]{0:T(1024)} %param.10) | copy-start | bytes 24580
  0.7 17.5 %copy-start.3 = (f32[32]{0:T(128)S(1)}, f32[32]{0:T(128)}, u32[]{:S(2)}) copy-start(f32[32]{0:T(128)} %param.11) | copy-start | bytes 388
  3.9 24.0 %collective-permute-start = (f32[1024,512]{1,0:T(8,128)S(1)}, f32[1024,512]{1,0:T(8,128)S(1)}, u32[]{:S(2)}, u32[]{:S(2)}) collective-permute-start(f32[1024,512]{1,0:T(8,128)S(1)} %get-tuple-element.17), channel_id=1, source_target_pairs={{0,16},{16,0},{1,17},{17,1},{2,18},{18,2},{3,19},{19,3},{4,20},{20... | collective-permute-start | bytes 6291464 | tf_op jit(solution)/shard_map/ppermute | solution.py:256
  28.4 30.4 %copy-start = (f32[512,32]{0,1:T(8,128)S(1)}, f32[512,32]{0,1:T(8,128)}, u32[]{:S(2)}) copy-start(f32[512,32]{0,1:T(8,128)} %param.7) | copy-start | bytes 196612
  28.4 2.9 %collective-permute-start.1 = (f32[72,128]{1,0:T(8,128)S(1)}, f32[72,128]{1,0:T(8,128)S(1)}, u32[]{:S(2)}, u32[]{:S(2)}) collective-permute-start(f32[72,128]{1,0:T(8,128)S(1)} %shard_map.96), channel_id=1, source_target_pairs={{0,16},{16,0},{1,17},{17,1},{2,18},{18,2},{3,19},{19,3},{4,20},{20... | collective-permute-start | bytes 110600 | tf_op jit(solution)/shard_map/ppermute | solution.py:289
  31.4 3.7 %collective-permute-start.4 = (f32[72,128]{1,0:T(8,128)S(1)}, f32[72,128]{1,0:T(8,128)S(1)}, u32[]{:S(2)}, u32[]{:S(2)}) collective-permute-start(f32[72,128]{1,0:T(8,128)S(1)} %shard_map.97.a_ref), channel_id=1, source_target_pairs={{0,160},{1,161},{2,162},{3,163},{4,164},{5,165},{6,166},{7,167},{8... | collective-permute-start | bytes 110600 | tf_op jit(solution)/shard_map/ppermute | solution.py:208
  32.0 4.0 %collective-permute-start.3 = (f32[72,128]{1,0:T(8,128)S(1)}, f32[72,128]{1,0:T(8,128)S(1)}, u32[]{:S(2)}, u32[]{:S(2)}) collective-permute-start(f32[72,128]{1,0:T(8,128)S(1)} %shard_map.97.a_ref), channel_id=1, source_target_pairs={{0,144},{1,145},{2,146},{3,147},{4,148},{5,149},{6,150},{7,151},{8... | collective-permute-start | bytes 110600 | tf_op jit(solution)/shard_map/ppermute | solution.py:208
  33.0 3.7 %collective-permute-start.2 = (f32[72,128]{1,0:T(8,128)S(1)}, f32[72,128]{1,0:T(8,128)S(1)}, u32[]{:S(2)}, u32[]{:S(2)}) collective-permute-start(f32[72,128]{1,0:T(8,128)S(1)} %shard_map.97.a_ref), channel_id=1, source_target_pairs={{0,48},{1,49},{2,50},{3,51},{4,52},{5,53},{6,54},{7,55},{8,56},{9,... | collective-permute-start | bytes 110600 | tf_op jit(solution)/shard_map/ppermute | solution.py:208
  34.3 24.5 %collective-permute-start.13 = (f32[8,32,128]{2,1,0:T(8,128)S(1)}, f32[8,32,128]{2,1,0:T(8,128)S(1)}, u32[]{:S(2)}, u32[]{:S(2)}) collective-permute-start(f32[8,32,128]{2,1,0:T(8,128)S(1)} %get-tuple-element.21), channel_id=1, source_target_pairs={{0,16},{16,0},{1,17},{17,1},{2,18},{18,2},{3,19},{19,3},{4,20},{20... | collective-permute-start | bytes 393224 | tf_op jit(solution)/shard_map/ppermute | solution.py:291
  36.8 6.2 %collective-permute-start.7 = (f32[72,128]{1,0:T(8,128)S(1)}, f32[72,128]{1,0:T(8,128)S(1)}, u32[]{:S(2)}, u32[]{:S(2)}) collective-permute-start(f32[72,128]{1,0:T(8,128)S(1)} %shard_map.98.a_ref), channel_id=1, source_target_pairs={{0,108},{1,109},{2,110},{3,111},{4,104},{5,105},{6,106},{7,107},{8... | collective-permute-start | bytes 110600 | tf_op jit(solution)/shard_map/ppermute | solution.py:208
  39.9 5.0 %collective-permute-start.6 = (f32[72,128]{1,0:T(8,128)S(1)}, f32[72,128]{1,0:T(8,128)S(1)}, u32[]{:S(2)}, u32[]{:S(2)}) collective-permute-start(f32[72,128]{1,0:T(8,128)S(1)} %shard_map.98.a_ref), channel_id=1, source_target_pairs={{0,28},{1,29},{2,30},{3,31},{4,24},{5,25},{6,26},{7,27},{8,20},{9,... | collective-permute-start | bytes 110600 | tf_op jit(solution)/shard_map/ppermute | solution.py:208
  40.2 4.8 %collective-permute-start.5 = (f32[72,128]{1,0:T(8,128)S(1)}, f32[72,128]{1,0:T(8,128)S(1)}, u32[]{:S(2)}, u32[]{:S(2)}) collective-permute-start(f32[72,128]{1,0:T(8,128)S(1)} %shard_map.98.a_ref), channel_id=1, source_target_pairs={{0,112},{1,113},{2,114},{3,115},{4,116},{5,117},{6,118},{7,119},{8... | collective-permute-start | bytes 110600 | tf_op jit(solution)/shard_map/ppermute | solution.py:208
  45.0 4.8 %collective-permute-start.10 = (f32[72,128]{1,0:T(8,128)S(1)}, f32[72,128]{1,0:T(8,128)S(1)}, u32[]{:S(2)}, u32[]{:S(2)}) collective-permute-start(f32[72,128]{1,0:T(8,128)S(1)} %shard_map.99.a_ref), channel_id=1, source_target_pairs={{0,5},{1,4},{2,7},{3,6},{4,1},{5,0},{6,3},{7,2},{8,13},{9,12},{10,... | collective-permute-start | bytes 110600 | tf_op jit(solution)/shard_map/ppermute | solution.py:208
  47.7 5.3 %collective-permute-start.9 = (f32[72,128]{1,0:T(8,128)S(1)}, f32[72,128]{1,0:T(8,128)S(1)}, u32[]{:S(2)}, u32[]{:S(2)}) collective-permute-start(f32[72,128]{1,0:T(8,128)S(1)} %shard_map.99.a_ref), channel_id=1, source_target_pairs={{0,17},{1,16},{2,19},{3,18},{4,21},{5,20},{6,23},{7,22},{8,25},{9,... | collective-permute-start | bytes 110600 | tf_op jit(solution)/shard_map/ppermute | solution.py:208
  48.4 4.5 %collective-permute-start.8 = (f32[72,128]{1,0:T(8,128)S(1)}, f32[72,128]{1,0:T(8,128)S(1)}, u32[]{:S(2)}, u32[]{:S(2)}) collective-permute-start(f32[72,128]{1,0:T(8,128)S(1)} %shard_map.99.a_ref), channel_id=1, source_target_pairs={{0,20},{1,21},{2,22},{3,23},{4,16},{5,17},{6,18},{7,19},{8,28},{9,... | collective-permute-start | bytes 110600 | tf_op jit(solution)/shard_map/ppermute | solution.py:208
  53.0 5.6 %collective-permute-start.11 = (f32[72,128]{1,0:T(8,128)S(1)}, f32[72,128]{1,0:T(8,128)S(1)}, u32[]{:S(2)}, u32[]{:S(2)}) collective-permute-start(f32[72,128]{1,0:T(8,128)S(1)} %shard_map.100.a_ref), channel_id=1, source_target_pairs={{0,19},{1,18},{2,17},{3,16},{4,23},{5,22},{6,21},{7,20},{8,27},{9,... | collective-permute-start | bytes 110600 | tf_op jit(solution)/shard_map/ppermute | solution.py:208
  58.6 2.5 %collective-permute-start.12 = (f32[72,128]{1,0:T(8,128)S(1)}, f32[72,128]{1,0:T(8,128)S(1)}, u32[]{:S(2)}, u32[]{:S(2)}) collective-permute-start(f32[72,128]{1,0:T(8,128)S(1)} %shard_map.101.mine_ref.refs_4_), channel_id=1, source_target_pairs={{0,16},{16,0},{1,17},{17,1},{2,18},{18,2},{3,19},{19,3},{4,20},{20... | collective-permute-start | bytes 110600 | tf_op jit(solution)/shard_map/ppermute | solution.py:297
